TPU v7x, 32 devices: a whole 2x2x4 slice. The times are simulated.
32 devices in a mesh: band: 8 (over y, x, core), lev: 4 (over z).
Axes of the slice: x: 2, y: 2, z: 4, core: 2. Of those that a mesh axis runs over, the one named last changes fastest.
Arguments:
- concentration: float32 [64, 4, 64, 1024], P(None, None, 'band', 'lev'), may hold values from 0.2 to 3
- observed: bfloat16 [64, 4, 64, 1024], P(None, None, 'band', 'lev'), may hold values from 0 to 2
- wind_zonal: float32 [64, 1024], P('band'), may hold values from 0.05 to 0.25
- wind_meridional: float32 [64, 1024], P('band'), may hold values from 0.05 to 0.25
- eddy_diffusion: float32 [64, 64, 1024], P(None, 'band', 'lev'), may hold values from 0.1 to 2000, as said below
- land_mask: int32 [64, 1024], P('band', 'lev'), may hold values 0 or 1
- surface_class: int32 [64, 1024], P('band', 'lev'), may hold values from 0 to 15
- class_embed: float32 [16, 128], replicated, may hold values from -6 to 6
- weight_first: bfloat16 [384, 256], replicated, may hold values from -0.3125 to 0.3125
- bias_first: float32 [256], replicated, may hold values from -3 to 3
- weight_second: bfloat16 [256, 256], replicated, may hold values from -0.375 to 0.375
- bias_second: float32 [256], replicated, may hold values from -3 to 3
- weight_third: bfloat16 [256, 64], replicated, may hold values from -0.375 to 0.375
- bias_third: float32 [64], replicated, may hold values from -3 to 3
Outputs:
- final_field: float32 [64, 4, 64, 1024], P(None, None, 'band', 'lev')
- weight_first_gradient: float32 [384, 256], replicated
- bias_first_gradient: float32 [256], replicated
- weight_second_gradient: float32 [256, 256], replicated
- bias_second_gradient: float32 [256], replicated
- weight_third_gradient: float32 [256, 64], replicated
- bias_third_gradient: float32 [64], replicated
Inputs may be any that keep to these rules, and one draw needn't show every extreme that they name: `eddy_diffusion`: positive mixing coefficients.
All inputs are finite; a program needn't handle non-finite values. No bound on the sum of `land_mask` on one device may be relied on, other than what follows from the above.
Results may differ from a plain program's by a relative error of at most 0.00048.
Values sent between devices are 32-bit elements; how exact they have to be, the bound alone decides.
No kernel may reach another device: no remote copies, remote signals or barrier semaphores. Data moves between devices by JAX's collectives and lax.ppermute only.
A program may use at most 128 MiB of HBM per device.

v0:
```python
import functools

import jax
import jax.numpy as jnp
from jax import lax
from jax.experimental import pallas as pl
from jax.experimental.pallas import tpu as pltpu
from jax.sharding import PartitionSpec as P

STEPS = 6
DIFFUSIVITY = 0.1
LATITUDE_EDGE = 1.25
LAND_SHARE = 0.7
SETTLING_SPEEDS = (0.5, 1.0, 1.5, 2.0)

F32 = jnp.float32
BF16 = jnp.bfloat16
LANES = 128
SLOT = 8
SLOTS = LANES // SLOT
VMEM_LIMIT = 56 * 1024 * 1024


def params():
    return pltpu.CompilerParams(vmem_limit_bytes=VMEM_LIMIT)


def specs(count):
    return [pl.BlockSpec(memory_space=pltpu.VMEM)] * count


def dot(a, b, dims):
    return lax.dot_general(a, b, (dims, ((), ())), preferred_element_type=F32)


def sigmoid(x):
    return 1.0 / (1.0 + jnp.exp(-x))


def bias_column(bias_ref):
    row = bias_ref[...]
    return jnp.broadcast_to(row, (LANES, row.shape[1])).T


def add_column(values, column):
    width = values.shape[1] // LANES
    return values + jnp.concatenate([column] * width, axis=1)


def lane_ids():
    return lax.broadcasted_iota(jnp.int32, (8, LANES), 1)


def spread(ref, start, count):
    return jnp.concatenate(
        [ref[t, pl.ds(start, count, stride=8), :] for t in range(ref.shape[0])], axis=1
    )


def put_spread(ref, start, values):
    for t in range(ref.shape[0]):
        ref[t, pl.ds(start, values.shape[0], stride=8), :] = values[:, t * LANES : (t + 1) * LANES]


def fetch_tiles(source, dest, sem):
    copies = [
        pltpu.make_async_copy(source.at[:, pl.ds(t * LANES, LANES)], dest.at[t], sem.at[t])
        for t in range(dest.shape[0])
    ]
    for copy in copies:
        copy.start()
    for copy in copies:
        copy.wait()


def tiles_at(ref, at):
    return [ref[t, at, :] for t in range(ref.shape[0])]


def split_tiles(values):
    return [values[:, t * LANES : (t + 1) * LANES] for t in range(values.shape[1] // LANES)]


def closure_row(r, conc, cls, embed_t, w1, c1, w2, c2, w3, c3):
    planes = conc.shape[1] // 8
    features = spread(conc, r, planes).astype(BF16)
    classes = cls[pl.ds(r, 1), :]
    n_class = embed_t.shape[1]
    ids = lax.broadcasted_iota(jnp.int32, (n_class, classes.shape[1]), 0)
    onehot = (ids == classes).astype(F32).astype(BF16)
    surface = dot(embed_t, onehot, ((1,), (0,))).astype(BF16)
    inputs = jnp.concatenate([features, surface], axis=0)
    pre1 = add_column(dot(w1[...], inputs, ((0,), (0,))), c1)
    sig1 = sigmoid(pre1)
    act1 = (pre1 * sig1).astype(BF16)
    pre2 = add_column(dot(w2[...], act1, ((0,), (0,))), c2)
    sig2 = sigmoid(pre2)
    act2 = (pre2 * sig2).astype(BF16)
    raw = add_column(dot(w3[...], act2, ((0,), (0,))), c3)
    return inputs, pre1, sig1, act1, pre2, sig2, act2, raw


def factor_level(z, carry, conc, eddy, removal, levels):
    rests, halves, lower = carry
    level = pl.ds(pl.multiple_of(z * 8, 8), 8)
    upper = split_tiles(jnp.where(z < levels - 1, eddy[level, :], 0.0))
    rem = tiles_at(removal, level)
    bins = len(SETTLING_SPEEDS)
    tiles = len(upper)
    new_rests, new_halves, invs, ratios = [], [], [], []
    for b in range(bins):
        at = pl.ds(pl.multiple_of((z * bins + b) * 8, 8), 8)
        for t in range(tiles):
            n = b * tiles + t
            excess = 1.0 + SETTLING_SPEEDS[b] * rem[t] + rests[n]
            inv = 1.0 / (excess + upper[t])
            ratio = upper[t] * inv
            half = (conc[t, at, :] + lower[t] * halves[n]) * inv
            new_rests.append(ratio * excess)
            new_halves.append(half)
            invs.append(inv)
            ratios.append(ratio)
    return (tuple(new_rests), tuple(new_halves), tuple(upper)), invs, ratios, new_halves


def zero_tiles(count):
    return tuple(jnp.zeros((8, LANES), F32) for _ in range(count))


def store_bins(ref, z, bins, values):
    tiles = ref.shape[0]
    for b in range(bins):
        at = pl.ds(pl.multiple_of((z * bins + b) * 8, 8), 8)
        for t in range(tiles):
            ref[t, at, :] = values[b * tiles + t]


def load_bins(ref, z, bins):
    out = []
    for b in range(bins):
        out += tiles_at(ref, pl.ds(pl.multiple_of((z * bins + b) * 8, 8), 8))
    return out


def pack_sides(row_of, r, east, west):
    lane = lane_ids()
    groups = row_of.shape[0] // 8
    width = row_of.shape[1]
    for j in range(groups // SLOTS):
        e = jnp.zeros((8, LANES), F32)
        w = jnp.zeros((8, LANES), F32)
        for k in range(SLOTS):
            g = j * SLOTS + k
            here = (lane // SLOT) == k
            first = row_of[g * 8 : g * 8 + 8, :LANES]
            last = row_of[g * 8 : g * 8 + 8, width - LANES :]
            e = jnp.where(here, pltpu.roll(first, SLOT * k, 1), e)
            w = jnp.where(here, pltpu.roll(last, (SLOT * k + SLOT) % LANES, 1), w)
        east[r, j] = e
        west[r, j] = w


def forward_kernel(
    conc_hbm, eddy, land, cls, embed, w1, b1, w2, b2, w3, b3, wind_u, wind_v,
    settled, north, south, first, last, wind_own,
    conc, removal, ratio_s, sem,
):
    fetch_tiles(conc_hbm, conc, sem)
    levels = eddy.shape[0] // 8
    bins = conc_hbm.shape[0] // eddy.shape[0]
    planes = levels * bins
    width = conc_hbm.shape[1]
    tiles = width // LANES
    lon_total = wind_u.shape[1]
    c1, c2, c3 = bias_column(b1), bias_column(b2), bias_column(b3)
    embed_t = embed[...].T.astype(BF16)

    for r in range(8):
        raw = closure_row(r, conc, cls, embed_t, w1, c1, w2, c2, w3, c3)[-1]
        landing = 1.0 - LAND_SHARE * land[r : r + 1, :].astype(F32)
        soft = jnp.maximum(raw, 0.0) + jnp.log1p(jnp.exp(-jnp.abs(raw)))
        put_spread(removal, r, soft * landing)

    def down(z, carry):
        carry, _, ratios, halves = factor_level(z, carry, conc, eddy, removal, levels)
        store_bins(ratio_s, z, bins, ratios)
        store_bins(settled, z, bins, halves)
        return carry

    many = bins * tiles
    start = (zero_tiles(many), zero_tiles(many), zero_tiles(tiles))
    lax.fori_loop(0, levels, down, start, unroll=2)

    def up(i, following):
        z = levels - 1 - i
        halves, ratios = load_bins(settled, z, bins), load_bins(ratio_s, z, bins)
        new = tuple(h + r * q for h, r, q in zip(halves, ratios, following))
        store_bins(settled, z, bins, new)
        return new

    lax.fori_loop(0, levels, up, zero_tiles(many), unroll=4)

    lon0 = lax.axis_index("lev") * width
    own = pl.ds(pl.multiple_of(lon0, LANES), width)
    east_at = pl.ds(pl.multiple_of(lax.rem(lon0 + width, lon_total), LANES), LANES)
    west_at = pl.ds(pl.multiple_of(lax.rem(lon0 + lon_total - LANES, lon_total), LANES), LANES)
    lane = lane_ids()
    for n, wind in enumerate((wind_u, wind_v)):
        wind_own[n, :, :width] = wind[:, own]
        wind_own[n, :, width:] = jnp.where(lane < LANES // 2, wind[:, east_at], wind[:, west_at])

    pad = jnp.zeros((8 - 4, width), F32)
    for r in range(8):
        row = spread(settled, r, planes)
        pack_sides(row, r, first, last)
        winds = []
        for n in range(2):
            line = wind_own[n, r : r + 1, :]
            winds.append(line[:, :width])
            winds.append(jnp.concatenate([line[:, width:]] * (width // LANES), axis=1))
        extra = jnp.concatenate(winds + [pad], axis=0)
        if r >= 8 - STEPS:
            north[r - (8 - STEPS), :planes, :] = row
            north[r - (8 - STEPS), planes:, :] = extra
        if r < STEPS:
            south[r, :planes, :] = row
            south[r, planes:, :] = extra


def unpack_sides(e, w, k):
    lane = lane_ids()
    back = lax.rem(LANES - SLOT * k, LANES)
    return jnp.where(
        lane < LANES // 2,
        pltpu.roll(e, back, 1),
        pltpu.roll(w, LANES - SLOT - SLOT * k, 1),
    )


def edge_flags():
    band = lax.axis_index("band")
    last = lax.axis_size("band") - 1
    south = jnp.where(band > 0, 1.0, 0.0).astype(F32)
    north = jnp.where(band < last, 1.0, 0.0).astype(F32)
    return south, north


def fill_coefficients(wind, coef, transposed):
    rows = wind.shape[1]
    halo = STEPS
    south, north = edge_flags()
    shape = (8, wind.shape[2])
    for i in range(rows):
        flag = south if i < halo else (north if i >= rows - halo else 1.0)
        u = jnp.broadcast_to(wind[0, i : i + 1, :], shape)
        v = jnp.broadcast_to(wind[1, i : i + 1, :], shape)
        centre = 1.0 - 4.0 * DIFFUSIVITY - u - v
        if transposed:
            along, across = u, v
        else:
            along = pltpu.roll(u, 1, 1)
            below = max(i - 1, 0)
            across = jnp.broadcast_to(wind[1, below : below + 1, :], shape)
        coef[0, i] = centre * flag
        coef[1, i] = (DIFFUSIVITY + along) * flag
        coef[2, i] = (DIFFUSIVITY + across) * flag
        coef[3, i] = jnp.full(shape, DIFFUSIVITY, F32) * flag


def run_steps(state, coef, transposed):
    rows = len(state)
    width = state[0].shape[1]
    for step in range(1, STEPS + 1):
        new = list(state)
        for i in range(step, rows - step):
            c = state[i]
            east = pltpu.roll(c, width - 1, 1)
            west = pltpu.roll(c, 1, 1)
            if transposed:
                plain, along, across = west + state[i - 1], east, state[i + 1]
            else:
                plain, along, across = east + state[i + 1], west, state[i - 1]
            new[i] = (
                coef[0, i] * c
                + coef[1, i] * along
                + (coef[2, i] * across + coef[3, i] * plain)
            )
        state = new
    return state[STEPS : rows - STEPS]


def load_state(g, j, k, own_rows, south, north, first, last, s_edge, n_edge):
    at = pl.ds(pl.multiple_of(g * 8, 8), 8)
    state = []
    for i in range(STEPS):
        side = unpack_sides(s_edge[0, i, j], s_edge[1, i, j], k)
        state.append(jnp.concatenate([south[i, at, :], side], axis=1))
    for r in range(8):
        side = unpack_sides(first[r, j], last[r, j], k)
        state.append(jnp.concatenate([own_rows(r), side], axis=1))
    for i in range(STEPS):
        side = unpack_sides(n_edge[0, i, j], n_edge[1, i, j], k)
        state.append(jnp.concatenate([north[i, at, :], side], axis=1))
    return state


def transport_kernel(
    settled, south, north, first, last, s_edge, n_edge, wind_own, observed, area,
    final_hbm, misfit, m_north, m_south, m_first, m_last, wind,
    coef, final, sem,
):
    width = north.shape[2]
    planes = settled.shape[1] // 8
    for n in range(2):
        for i in range(STEPS):
            for halo, to in ((south, i), (north, i + STEPS + 8)):
                wind[n, to : to + 1, :width] = halo[i, planes + 2 * n : planes + 2 * n + 1, :]
                wind[n, to : to + 1, width:] = halo[
                    i, planes + 2 * n + 1 : planes + 2 * n + 2, :LANES
                ]
        wind[n, STEPS : STEPS + 8, :] = wind_own[n]
    fill_coefficients(wind, coef, False)
    lane = lane_ids()

    def group(g, carry):
        j, k = g // SLOTS, lax.rem(g, SLOTS)
        base = g * 64
        at = pl.ds(pl.multiple_of(g * 8, 8), 8)
        own_rows = lambda r: spread(settled, base + r, 8)
        state = load_state(g, j, k, own_rows, south, north, first, last, s_edge, n_edge)
        state = run_steps(state, coef, False)
        here = (lane // SLOT) == k
        for r in range(8):
            out = state[r][:, :width]
            put_spread(final, base + r, out)
            m = area[r : r + 1, :] * (out - spread(observed, base + r, 8))
            misfit[r, at, :] = m
            if r >= 8 - STEPS:
                m_north[r - (8 - STEPS), at, :] = m
            if r < STEPS:
                m_south[r, at, :] = m
            m_first[r, j] = jnp.where(here, pltpu.roll(m[:, :LANES], SLOT * k, 1), m_first[r, j])
            m_last[r, j] = jnp.where(
                here,
                pltpu.roll(m[:, width - LANES :], lax.rem(SLOT * k + SLOT, LANES), 1),
                m_last[r, j],
            )
        return carry

    m_first[...] = jnp.zeros_like(m_first)
    m_last[...] = jnp.zeros_like(m_last)
    parts = sem.shape[0]
    each = planes // 8 // parts
    copies = []
    for part in range(parts):
        lax.fori_loop(part * each, (part + 1) * each, group, 0)
        at = pl.ds(part * each * 64, each * 64)
        for t in range(final.shape[0]):
            copies.append(
                pltpu.make_async_copy(
                    final.at[t, at, :],
                    final_hbm.at[at, pl.ds(t * LANES, LANES)],
                    sem.at[part, t],
                )
            )
            copies[-1].start()
    for copy in copies:
        copy.wait()


def adjoint_kernel(misfit, south, north, first, last, s_edge, n_edge, wind, adjoint, coef):
    planes = misfit.shape[1]
    width = misfit.shape[2]
    fill_coefficients(wind, coef, True)

    def group(g, carry):
        j, k = g // SLOTS, lax.rem(g, SLOTS)
        at = pl.ds(pl.multiple_of(g * 8, 8), 8)
        own_rows = lambda r: misfit[r, at, :]
        state = load_state(g, j, k, own_rows, south, north, first, last, s_edge, n_edge)
        state = run_steps(state, coef, True)
        for r in range(8):
            put_spread(adjoint, g * 64 + r, state[r][:, :width])
        return carry

    lax.fori_loop(0, planes // 8, group, 0)


def recompute_kernel(
    conc_hbm, eddy, land, cls, embed, w1, b1, w2, b2, w3, b3,
    inverse, ratio, inputs_o, act1_o, slope1_o, act2_o, slope2_o, rate_o,
    conc, removal, sem,
):
    fetch_tiles(conc_hbm, conc, sem)
    levels = eddy.shape[0] // 8
    bins = conc_hbm.shape[0] // eddy.shape[0]
    tiles = conc.shape[0]
    c1, c2, c3 = bias_column(b1), bias_column(b2), bias_column(b3)
    embed_t = embed[...].T.astype(BF16)

    for r in range(8):
        inputs, pre1, sig1, act1, pre2, sig2, act2, raw = closure_row(
            r, conc, cls, embed_t, w1, c1, w2, c2, w3, c3
        )
        inputs_o[r] = inputs
        act1_o[r] = act1
        act2_o[r] = act2
        slope1_o[r] = sig1 * (1.0 + pre1 * (1.0 - sig1))
        slope2_o[r] = sig2 * (1.0 + pre2 * (1.0 - sig2))
        landing = 1.0 - LAND_SHARE * land[r : r + 1, :].astype(F32)
        soft = jnp.maximum(raw, 0.0) + jnp.log1p(jnp.exp(-jnp.abs(raw)))
        put_spread(removal, r, soft * landing)
        put_spread(rate_o, r, sigmoid(raw) * landing)

    def down(z, carry):
        carry, invs, ratios, _ = factor_level(z, carry, conc, eddy, removal, levels)
        store_bins(ratio, z, bins, ratios)
        store_bins(inverse, z, bins, invs)
        return carry

    many = bins * tiles
    start = (zero_tiles(many), zero_tiles(many), zero_tiles(tiles))
    lax.fori_loop(0, levels, down, start, unroll=2)


def gradient_kernel(
    adjoint, settled, inverse, ratio, eddy, rate, inputs, act1, slope1, act2, slope2, w2, w3,
    out, half, raw_grad,
):
    levels = eddy.shape[0] // 8
    bins = adjoint.shape[1] // eddy.shape[0]
    width = eddy.shape[1]
    tiles = width // LANES
    many = bins * tiles

    def down(z, carry):
        before, lower = carry
        upper = tuple(split_tiles(eddy[pl.ds(pl.multiple_of(z * 8, 8), 8), :]))
        rights, invs = load_bins(adjoint, z, bins), load_bins(inverse, z, bins)
        new = tuple(
            (rights[n] + lower[n % tiles] * before[n]) * invs[n] for n in range(many)
        )
        store_bins(half, z, bins, new)
        return new, upper

    lax.fori_loop(0, levels, down, (zero_tiles(many), zero_tiles(tiles)), unroll=4)

    def up(i, following):
        z = levels - 1 - i
        halves, ratios = load_bins(half, z, bins), load_bins(ratio, z, bins)
        own = load_bins(settled, z, bins)
        new = tuple(h + r * q for h, r, q in zip(halves, ratios, following))
        at = pl.ds(pl.multiple_of(z * 8, 8), 8)
        for t in range(tiles):
            total = sum(
                SETTLING_SPEEDS[b] * (new[b * tiles + t] * own[b * tiles + t])
                for b in range(bins)
            )
            raw_grad[t, at, :] = -total * rate[t, at, :]
        return new

    lax.fori_loop(0, levels, up, zero_tiles(many), unroll=4)

    fin, hid = inputs.shape[1], act1.shape[1]
    g1 = jnp.zeros((fin, hid), F32)
    g2 = jnp.zeros((hid, hid), F32)
    g3 = jnp.zeros((levels, hid), F32)
    s1 = jnp.zeros((hid, width), F32)
    s2 = jnp.zeros((hid, width), F32)
    s3 = jnp.zeros((levels, width), F32)
    for r in range(8):
        grad3 = spread(raw_grad, r, levels)
        half3 = grad3.astype(BF16)
        s3 = s3 + grad3
        g3 = g3 + dot(half3, act2[r], ((1,), (1,)))
        grad2 = dot(w3[...], half3, ((1,), (0,))) * slope2[r]
        half2 = grad2.astype(BF16)
        s2 = s2 + grad2
        g2 = g2 + dot(act1[r], half2, ((1,), (1,)))
        grad1 = dot(w2[...], half2, ((1,), (0,))) * slope1[r]
        half1 = grad1.astype(BF16)
        s1 = s1 + grad1
        g1 = g1 + dot(inputs[r], half1, ((1,), (1,)))
    out[:fin, :] = g1
    out[fin : fin + hid, :] = g2
    at = fin + hid
    out[at : at + levels, :] = g3
    at += levels
    rows1 = jnp.sum(s1.T, axis=0, keepdims=True)
    rows2 = jnp.sum(s2.T, axis=0, keepdims=True)
    rows3 = jnp.sum(s3.T, axis=0, keepdims=True)
    rows3 = jnp.concatenate([rows3, jnp.zeros((1, hid - levels), F32)], axis=1)
    out[at:, :] = jnp.zeros((out.shape[0] - at, hid), F32)
    out[at : at + 1, :] = rows1
    out[at + 1 : at + 2, :] = rows2
    out[at + 2 : at + 3, :] = rows3


def sum_over_devices(x):
    size = lax.axis_size("band")
    index = lax.axis_index("band")
    bits = []
    step = 1
    while step < size:
        perm = [(i, i ^ step) for i in range(size)]
        bit = (index // step) % 2
        half = x.shape[0] // 2
        parts = x.reshape(2, half, x.shape[1])
        mine = lax.dynamic_index_in_dim(parts, bit, 0, False)
        theirs = lax.dynamic_index_in_dim(parts, 1 - bit, 0, False)
        x = mine + lax.ppermute(theirs, "band", perm)
        bits.append((step, bit, perm))
        step *= 2
    lev = lax.axis_size("lev")
    step = 1
    while step < lev:
        x = x + lax.ppermute(x, "lev", [(i, i ^ step) for i in range(lev)])
        step *= 2
    for step, bit, perm in reversed(bits):
        other = lax.ppermute(x, "band", perm)
        low = jnp.where(bit == 0, x, other)
        high = jnp.where(bit == 0, other, x)
        x = jnp.concatenate([low, high], 0)
    return x


def exchange(north, south, first, last):
    bands, levs = lax.axis_size("band"), lax.axis_size("lev")
    up = [(i, i + 1) for i in range(bands - 1)]
    down = [(j, i) for i, j in up]
    from_east = [((i + 1) % levs, i) for i in range(levs)]
    from_west = [(i, (i + 1) % levs) for i in range(levs)]
    e = lax.ppermute(first, "lev", from_east)
    w = lax.ppermute(last, "lev", from_west)
    s = lax.ppermute(north, "band", up)
    n = lax.ppermute(south, "band", down)
    s_edge = lax.ppermute(jnp.stack([e[8 - STEPS :], w[8 - STEPS :]]), "band", up)
    n_edge = lax.ppermute(jnp.stack([e[:STEPS], w[:STEPS]]), "band", down)
    return s, n, e, w, s_edge, n_edge


def per_device(
    concentration,
    observed,
    wind_zonal,
    wind_meridional,
    eddy_diffusion,
    land_mask,
    surface_class,
    class_embed,
    weight_first,
    bias_first,
    weight_second,
    bias_second,
    weight_third,
    bias_third,
):
    levels, bins, rows, width = concentration.shape
    lon_total = wind_zonal.shape[1]
    planes = levels * bins
    groups = planes // 8
    fin, hid = weight_first.shape
    shape = jax.ShapeDtypeStruct
    conc = concentration.reshape(planes * rows, width)
    eddy = eddy_diffusion.reshape(levels * rows, width)
    closure = (
        land_mask, surface_class, class_embed, weight_first, bias_first.reshape(1, -1),
        weight_second, bias_second.reshape(1, -1), weight_third, bias_third.reshape(1, -1),
    )
    tiles = width // LANES
    flat = shape((tiles, planes * rows, LANES), F32)
    level_flat = shape((tiles, levels * rows, LANES), F32)
    any_space = pl.BlockSpec(memory_space=pl.ANY)
    tiled = pltpu.VMEM((tiles, planes * rows, LANES), F32)
    tiled_levels = pltpu.VMEM((tiles, levels * rows, LANES), F32)
    halo = shape((STEPS, planes + 8, width), F32)
    m_halo = shape((STEPS, planes, width), F32)
    side = shape((rows, groups // SLOTS, 8, LANES), F32)
    ext = width + LANES
    n_rows = rows + 2 * STEPS

    settled, north, south, first, last, wind_own = pl.pallas_call(
        forward_kernel,
        out_shape=(flat, halo, halo, side, side, shape((2, rows, ext), F32)),
        in_specs=[any_space] + specs(12),
        out_specs=tuple(specs(6)),
        scratch_shapes=[tiled, tiled_levels, tiled, pltpu.SemaphoreType.DMA((tiles,))],
        compiler_params=params(),
        name="forward",
    )(conc, eddy, *closure, wind_zonal, wind_meridional)

    s, n, e, w, s_edge, n_edge = exchange(north, south, first, last)

    conc_b, eddy_b, observed_b, *closure_b = lax.optimization_barrier(
        (conc, eddy, observed, *closure, north)
    )[:-1]
    kept = pl.pallas_call(
        recompute_kernel,
        out_shape=(
            flat, flat,
            shape((rows, fin, width), BF16),
            shape((rows, hid, width), BF16),
            shape((rows, hid, width), F32),
            shape((rows, hid, width), BF16),
            shape((rows, hid, width), F32),
            level_flat,
        ),
        in_specs=[any_space] + specs(10),
        out_specs=tuple(specs(8)),
        scratch_shapes=[tiled, tiled_levels, pltpu.SemaphoreType.DMA((tiles,))],
        compiler_params=params(),
        cost_estimate=pl.CostEstimate(
            flops=2 * 2048 * (384 + 256 + 64) * 256, bytes_accessed=20 << 20, transcendentals=1 << 21
        ),
        name="recompute",
    )(conc_b, eddy_b, *closure_b)
    inverse, ratio, inputs, act1, slope1, act2, slope2, rate = kept
    observed_flat = observed_b.astype(F32).reshape(planes * rows, tiles, LANES)
    observed_flat = observed_flat.transpose(1, 0, 2)
    total_rows = rows * lax.axis_size("band")
    row_ids = lax.axis_index("band") * rows + jnp.arange(rows, dtype=jnp.int32)
    latitude = LATITUDE_EDGE * (row_ids.astype(F32) + 0.5) / total_rows
    area = jnp.cos(latitude) / (bins * total_rows * lon_total)
    area = jnp.broadcast_to(area[:, None], (rows, width))

    final, misfit, m_north, m_south, m_first, m_last, wind = pl.pallas_call(
        transport_kernel,
        out_shape=(
            shape((planes * rows, width), F32), shape((rows, planes, width), F32), m_halo, m_halo, side, side,
            shape((2, n_rows, ext), F32),
        ),
        in_specs=specs(10),
        out_specs=tuple([any_space] + specs(6)),
        scratch_shapes=[
            pltpu.VMEM((4, n_rows, 8, ext), F32), tiled, pltpu.SemaphoreType.DMA((4, tiles)),
        ],
        compiler_params=params(),
        name="transport",
    )(settled, s, n, e, w, s_edge, n_edge, wind_own, observed_flat, area)

    s, n, e, w, s_edge, n_edge = exchange(m_north, m_south, m_first, m_last)

    adjoint = pl.pallas_call(
        adjoint_kernel,
        out_shape=flat,
        in_specs=specs(8),
        out_specs=specs(1)[0],
        scratch_shapes=[pltpu.VMEM((4, n_rows, 8, ext), F32)],
        compiler_params=params(),
        name="adjoint",
    )(misfit, s, n, e, w, s_edge, n_edge, wind)

    bands = lax.axis_size("band")
    used = fin + hid + levels + 3
    padded = -(-used // (8 * bands)) * (8 * bands)
    grads = pl.pallas_call(
        gradient_kernel,
        out_shape=shape((padded, hid), F32),
        in_specs=specs(13),
        out_specs=specs(1)[0],
        scratch_shapes=[tiled, tiled_levels],
        compiler_params=params(),
        name="gradient",
    )(
        adjoint, settled, inverse, ratio, eddy, rate, inputs, act1, slope1, act2, slope2,
        weight_second, weight_third,
    )
    grads = sum_over_devices(grads)
    at = fin + hid + levels
    return (
        final.reshape(levels, bins, rows, width),
        grads[:fin],
        grads[at],
        grads[fin : fin + hid],
        grads[at + 1],
        grads[fin + hid : at].T,
        grads[at + 2, :levels],
    )


def solution(mesh):
    return jax.shard_map(
        per_device,
        mesh=mesh,
        in_specs=(
            P(None, None, "band", "lev"),
            P(None, None, "band", "lev"),
            P("band", None),
            P("band", None),
            P(None, "band", "lev"),
            P("band", "lev"),
            P("band", "lev"),
            P(),
            P(),
            P(),
            P(),
            P(),
            P(),
            P(),
        ),
        out_specs=(P(None, None, "band", "lev"), P(), P(), P(), P(), P(), P()),
        check_vma=False,
    )
```

profile of v0, /device:TPU:0, one launch (start us, length us, event | category | flops | bytes accessed | tf_op | source)
XLA Modules:
  0.0 209.2 jit_solution(4354552493638572178)
XLA Ops:
  0.6 1.6 copy.24.w3
  2.2 12.1 %forward.1 = (f32[2,2048,128]{2,1,0:T(8,128)}, f32[6,264,256]{2,1,0:T(8,128)}, f32[6,264,256]{2,1,0:T(8,128)}, f32[8,2,8,128]{3,2,1,0:T(8,128)}, f32[8,2,8,128]{3,2,1,0:T(8,128)}, /*index=5*/f32[2,8,384]{2,1,0:T(8,128)}) custom-call(f32[2048,256]{1,0:T(8,128)} %bitcast.51, f32[512,256]{1,0:T(8,128)} %bitcast.53, s32[8,256]{1,0:T(8,128)} %land.2, ...), custom_call_target="tpu_custom_call" | custom-call | tf_op jit(solution)/shard_map/forward/pallas_call | solution.py:582
  14.3 3.6 %collective-permute-start = (f32[6,264,256]{2,1,0:T(8,128)}, f32[6,264,256]{2,1,0:T(8,128)}, u32[]{:S(2)}, u32[]{:S(2)}) collective-permute-start(f32[6,264,256]{2,1,0:T(8,128)} %get-tuple-element.41), channel_id=1, source_target_pairs={{0,4},{4,8},{8,12},{12,16},{16,20},{20,24},{24,28},{1,5},{5,9},{9,... | collective-permute-start | bytes 4866056 | tf_op jit(solution)/shard_map/ppermute | solution.py:535
  17.9 1.3 collective-permute-start.1
  19.2 2.5 %collective-permute-start.3 = (f32[8,2,8,128]{3,2,1,0:T(8,128)}, f32[8,2,8,128]{3,2,1,0:T(8,128)S(1)}, u32[]{:S(2)}, u32[]{:S(2)}) collective-permute-start(f32[8,2,8,128]{3,2,1,0:T(8,128)} %get-tuple-element.44), channel_id=1, source_target_pairs={{0,1},{1,2},{2,3},{3,0},{4,5},{5,6},{6,7},{7,4},{8,9},{9,10},{10,1... | collective-permute-start | bytes 196616 | tf_op jit(solution)/shard_map/ppermute | solution.py:534
  21.6 2.1 %collective-permute-start.2 = (f32[8,2,8,128]{3,2,1,0:T(8,128)}, f32[8,2,8,128]{3,2,1,0:T(8,128)S(1)}, u32[]{:S(2)}, u32[]{:S(2)}) collective-permute-start(f32[8,2,8,128]{3,2,1,0:T(8,128)} %get-tuple-element.43), channel_id=1, source_target_pairs={{1,0},{2,1},{3,2},{0,3},{5,4},{6,5},{7,6},{4,7},{9,8},{10,9},{11,1... | collective-permute-start | bytes 196616 | tf_op jit(solution)/shard_map/ppermute | solution.py:533
  23.7 1.0 reshape.64
  24.8 1.5 copy.29
  26.4 1.7 collective-permute-done.2.first
  28.2 2.0 collective-permute-start.4
  30.2 1.3 collective-permute-start.5
  31.6 2.8 %collective-permute-done.5.n_edge = f32[2,6,2,8,128]{4,3,2,1,0:T(8,128)S(1)} collective-permute-done((f32[2,6,2,8,128]{4,3,2,1,0:T(8,128)S(1)}, f32[2,6,2,8,128]{4,3,2,1,0:T(8,128)S(1)}, u32[]{:S(2)}, u32[]{:S(2)}) %collective-permute-start.5) | collective-permute-done | bytes 98336 | tf_op jit(solution)/shard_map/ppermute | solution.py:538
  34.5 0.7 broadcast_in_dim.2.area
  35.1 31.0 %transport.1 = (f32[2048,256]{1,0:T(8,128)}, f32[8,256,256]{2,1,0:T(8,128)}, f32[6,256,256]{2,1,0:T(8,128)}, f32[6,256,256]{2,1,0:T(8,128)}, f32[8,2,8,128]{3,2,...) custom-call(f32[2,2048,128]{2,1,0:T(8,128)} %get-tuple-element.40.settled, ...), custom_call_target="tpu_custom_call" | custom-call | tf_op jit(solution)/shard_map/transport/pallas_call | solution.py:626
  66.2 26.1 %collective-permute-start.6 = (f32[6,256,256]{2,1,0:T(8,128)}, f32[6,256,256]{2,1,0:T(8,128)S(1)}, u32[]{:S(2)}, u32[]{:S(2)}) collective-permute-start(f32[6,256,256]{2,1,0:T(8,128)} %get-tuple-element.49), channel_id=1, source_target_pairs={{0,4},{4,8},{8,12},{12,16},{16,20},{20,24},{24,28},{1,5},{5,9},{9,... | collective-permute-start | bytes 4718600 | tf_op jit(solution)/shard_map/ppermute | solution.py:535
  92.2 1.3 collective-permute-start.7
  93.5 1.6 collective-permute-start.9
  95.2 2.3 %collective-permute-start.8 = (f32[8,2,8,128]{3,2,1,0:T(8,128)}, f32[8,2,8,128]{3,2,1,0:T(8,128)S(1)}, u32[]{:S(2)}, u32[]{:S(2)}) collective-permute-start(f32[8,2,8,128]{3,2,1,0:T(8,128)} %get-tuple-element.51), channel_id=1, source_target_pairs={{1,0},{2,1},{3,2},{0,3},{5,4},{6,5},{7,6},{4,7},{9,8},{10,9},{11,1... | collective-permute-start | bytes 196616 | tf_op jit(solution)/shard_map/ppermute | solution.py:533
  97.4 3.1 %collective-permute-done.9.last = f32[8,2,8,128]{3,2,1,0:T(8,128)S(1)} collective-permute-done((f32[8,2,8,128]{3,2,1,0:T(8,128)}, f32[8,2,8,128]{3,2,1,0:T(8,128)S(1)}, u32[]{:S(2)}, u32[]{:S(2)}) %collective-permute-start.9) | collective-permute-done | bytes 65568 | tf_op jit(solution)/shard_map/ppermute | solution.py:534
  100.5 1.1 collective-permute-done.8.first
  101.6 0.6 pad_maximum_fusion.4
  102.3 1.9 collective-permute-start.10
  104.2 0.6 pad_maximum_fusion.5
  104.8 1.5 collective-permute-start.11
  106.3 0.7 copy.26.w3
  107.1 13.8 %recompute.1 = (f32[2,2048,128]{2,1,0:T(8,128)}, f32[2,2048,128]{2,1,0:T(8,128)}, bf16[8,384,256]{2,1,0:T(8,128)(2,1)}, bf16[8,256,256]{2,1,0:T(8,128)(2,1)}, f3...) custom-call(f32[2048,256]{1,0:T(8,128)} %bitcast.52, ...), custom_call_target="tpu_custom_call" | custom-call | flops 738197504 | bytes 20971520 | tf_op jit(solution)/shard_map/recompute/pallas_call | solution.py:597
  120.9 0.6 copy-done.8
  121.5 0.6 copy-done
  122.6 25.2 %adjoint.1 = f32[2,2048,128]{2,1,0:T(8,128)} custom-call(f32[8,256,256]{2,1,0:T(8,128)} %get-tuple-element.48.misfit, f32[6,256,256]{2,1,0:T(8,128)} %copy-done, f32[6,256,256]{2,1,0:T(8,128)} %copy-done.1, f32[8,2,8,128]{3,2,1,0:T(8,128)} %copy-done.4, f32[8,2,8,128]{3,2,1,0:T(8,128)} %copy-done.3, f32[2,6,2,8,128]{4,3,2,1,0:T(8,128)} %copy-done.8, ...), custom_call_target="tpu_custom_call" | custom-call | tf_op jit(solution)/shard_map/adjoint/pallas_call | solution.py:643
  147.8 10.6 %gradient.1 = f32[768,256]{1,0:T(8,128)} custom-call(f32[2,2048,128]{2,1,0:T(8,128)} %adjoint.1, f32[2,2048,128]{2,1,0:T(8,128)} %get-tuple-element.40.settled, f32[2,2048,128]{2,1,0:T(8,128)} %get-tuple-element.65.inverse, f32[2,2048,128]{2,1,0:T(8,128)} %get-tuple-element.66.ratio, f32[512,256]{1,0:T(8,128)} %bitcast.55, ...), custom_call_target="tpu_custom_call" | custom-call | tf_op jit(solution)/shard_map/gradient/pallas_call | solution.py:656
  158.4 1.0 dynamic-slice_bitcast_fusion
  159.5 9.5 %collective-permute-start.12 = (f32[384,256]{1,0:T(8,128)S(1)}, f32[384,256]{1,0:T(8,128)S(1)}, u32[]{:S(2)}, u32[]{:S(2)}) collective-permute-start(f32[384,256]{1,0:T(8,128)S(1)} %dynamic-slice_bitcast_fusion), channel_id=1, source_target_pairs={{0,4},{4,0},{8,12},{12,8},{16,20},{20,16},{24,28},{28,24},{1,5},{5... | collective-permute-start | bytes 1179656 | tf_op jit(solution)/shard_map/ppermute | solution.py:511
  169.0 1.3 collective-permute-done.12
  170.3 1.0 bitcast_add_fusion
  171.6 7.0 %collective-permute-done.13 = f32[192,256]{1,0:T(8,128)S(1)} collective-permute-done((f32[192,256]{1,0:T(8,128)S(1)}, f32[192,256]{1,0:T(8,128)S(1)}, u32[]{:S(2)}, u32[]{:S(2)}) %collective-permute-start.13) | collective-permute-done | bytes 196640 | tf_op jit(solution)/shard_map/ppermute | solution.py:511
  178.8 4.6 %collective-permute-done.14 = f32[96,256]{1,0:T(8,128)S(1)} collective-permute-done((f32[96,256]{1,0:T(8,128)S(1)}, f32[96,256]{1,0:T(8,128)S(1)}, u32[]{:S(2)}, u32[]{:S(2)}) %collective-permute-start.14) | collective-permute-done | bytes 98336 | tf_op jit(solution)/shard_map/ppermute | solution.py:511
  183.4 1.6 collective-permute-start.15
  185.0 3.0 %collective-permute-done.15 = f32[96,256]{1,0:T(8,128)S(1)} collective-permute-done((f32[96,256]{1,0:T(8,128)S(1)}, f32[96,256]{1,0:T(8,128)S(1)}, u32[]{:S(2)}, u32[]{:S(2)}) %collective-permute-start.15) | collective-permute-done | bytes 98336 | tf_op jit(solution)/shard_map/ppermute | solution.py:517
  188.1 2.8 %collective-permute-start.16 = (f32[96,256]{1,0:T(8,128)S(1)}, f32[96,256]{1,0:T(8,128)S(1)}, u32[]{:S(2)}, u32[]{:S(2)}) collective-permute-start(f32[96,256]{1,0:T(8,128)S(1)} %add.84), channel_id=1, source_target_pairs={{0,2},{1,3},{2,0},{3,1},{4,6},{5,7},{6,4},{7,5},{8,10},{9,11},{10,... | collective-permute-start | bytes 294920 | tf_op jit(solution)/shard_map/ppermute | solution.py:517
  190.9 2.8 %collective-permute-done.16 = f32[96,256]{1,0:T(8,128)S(1)} collective-permute-done((f32[96,256]{1,0:T(8,128)S(1)}, f32[96,256]{1,0:T(8,128)S(1)}, u32[]{:S(2)}, u32[]{:S(2)}) %collective-permute-start.16) | collective-permute-done | bytes 98336 | tf_op jit(solution)/shard_map/ppermute | solution.py:517
  193.8 4.6 %collective-permute-done.17 = f32[96,256]{1,0:T(8,128)S(1)} collective-permute-done((f32[96,256]{1,0:T(8,128)S(1)}, f32[96,256]{1,0:T(8,128)S(1)}, u32[]{:S(2)}, u32[]{:S(2)}) %collective-permute-start.17) | collective-permute-done | bytes 98336 | tf_op jit(solution)/shard_map/ppermute | solution.py:520
  198.8 5.4 %collective-permute-done.18 = f32[192,256]{1,0:T(8,128)S(1)} collective-permute-done((f32[192,256]{1,0:T(8,128)S(1)}, f32[192,256]{1,0:T(8,128)S(1)}, u32[]{:S(2)}, u32[]{:S(2)}) %collective-permute-start.18) | collective-permute-done | bytes 196640 | tf_op jit(solution)/shard_map/ppermute | solution.py:520
  204.3 1.7 collective-permute-done.19
  206.0 0.8 broadcast_select_fusion
  206.8 0.6 fusion
  207.4 0.7 slice.61
  208.1 0.6 slice_bitcast_fusion
  208.7 0.5 slice_bitcast_fusion.9
  (52 shorter events, 1.9 us)
Async XLA Ops:
  0.6 23.1 %copy-start.2 = (bf16[64,4,8,256]{3,2,1,0:T(8,128)(2,1)S(1)}, bf16[64,4,8,256]{3,2,1,0:T(8,128)(2,1)}, u32[]{:S(2)}) copy-start(bf16[64,4,8,256]{3,2,1,0:T(8,128)(2,1)} %param.15) | copy-start | bytes 3145732
  14.3 20.1 %collective-permute-start = (f32[6,264,256]{2,1,0:T(8,128)}, f32[6,264,256]{2,1,0:T(8,128)}, u32[]{:S(2)}, u32[]{:S(2)}) collective-permute-start(f32[6,264,256]{2,1,0:T(8,128)} %get-tuple-element.41), channel_id=1, source_target_pairs={{0,4},{4,8},{8,12},{12,16},{16,20},{20,24},{24,28},{1,5},{5,9},{9,... | collective-permute-start | bytes 4866056 | tf_op jit(solution)/shard_map/ppermute | solution.py:535
  17.9 16.6 %collective-permute-start.1 = (f32[6,264,256]{2,1,0:T(8,128)}, f32[6,264,256]{2,1,0:T(8,128)}, u32[]{:S(2)}, u32[]{:S(2)}) collective-permute-start(f32[6,264,256]{2,1,0:T(8,128)} %get-tuple-element.42), channel_id=1, source_target_pairs={{4,0},{8,4},{12,8},{16,12},{20,16},{24,20},{28,24},{5,1},{9,5},{13... | collective-permute-start | bytes 4866056 | tf_op jit(solution)/shard_map/ppermute | solution.py:536
  19.2 7.3 %collective-permute-start.3 = (f32[8,2,8,128]{3,2,1,0:T(8,128)}, f32[8,2,8,128]{3,2,1,0:T(8,128)S(1)}, u32[]{:S(2)}, u32[]{:S(2)}) collective-permute-start(f32[8,2,8,128]{3,2,1,0:T(8,128)} %get-tuple-element.44), channel_id=1, source_target_pairs={{0,1},{1,2},{2,3},{3,0},{4,5},{5,6},{6,7},{7,4},{8,9},{9,10},{10,1... | collective-permute-start | bytes 196616 | tf_op jit(solution)/shard_map/ppermute | solution.py:534
  21.6 6.6 %collective-permute-start.2 = (f32[8,2,8,128]{3,2,1,0:T(8,128)}, f32[8,2,8,128]{3,2,1,0:T(8,128)S(1)}, u32[]{:S(2)}, u32[]{:S(2)}) collective-permute-start(f32[8,2,8,128]{3,2,1,0:T(8,128)} %get-tuple-element.43), channel_id=1, source_target_pairs={{1,0},{2,1},{3,2},{0,3},{5,4},{6,5},{7,6},{4,7},{9,8},{10,9},{11,1... | collective-permute-start | bytes 196616 | tf_op jit(solution)/shard_map/ppermute | solution.py:533
  26.4 8.7 %copy-start.5 = (f32[8,2,8,128]{3,2,1,0:T(8,128)}, f32[8,2,8,128]{3,2,1,0:T(8,128)S(1)}, u32[]{:S(2)}) copy-start(f32[8,2,8,128]{3,2,1,0:T(8,128)S(1)} %collective-permute-done.3.last) | copy-start | bytes 196612
  28.2 6.9 %copy-start.6 = (f32[8,2,8,128]{3,2,1,0:T(8,128)}, f32[8,2,8,128]{3,2,1,0:T(8,128)S(1)}, u32[]{:S(2)}) copy-start(f32[8,2,8,128]{3,2,1,0:T(8,128)S(1)} %collective-permute-done.2.first) | copy-start | bytes 196612
  28.2 3.4 %collective-permute-start.4 = (f32[2,6,2,8,128]{4,3,2,1,0:T(8,128)S(1)}, f32[2,6,2,8,128]{4,3,2,1,0:T(8,128)S(1)}, u32[]{:S(2)}, u32[]{:S(2)}) collective-permute-start(f32[2,6,2,8,128]{4,3,2,1,0:T(8,128)S(1)} %pad_maximum_fusion.2), channel_id=1, source_target_pairs={{0,4},{4,8},{8,12},{12,16},{16,20},{20,24},{24,28},{1,5},{5,9},{9,... | collective-permute-start | bytes 294920 | tf_op jit(solution)/shard_map/ppermute | solution.py:537
  30.2 4.2 %collective-permute-start.5 = (f32[2,6,2,8,128]{4,3,2,1,0:T(8,128)S(1)}, f32[2,6,2,8,128]{4,3,2,1,0:T(8,128)S(1)}, u32[]{:S(2)}, u32[]{:S(2)}) collective-permute-start(f32[2,6,2,8,128]{4,3,2,1,0:T(8,128)S(1)} %pad_maximum_fusion.3), channel_id=1, source_target_pairs={{4,0},{8,4},{12,8},{16,12},{20,16},{24,20},{28,24},{5,1},{9,5},{13... | collective-permute-start | bytes 294920 | tf_op jit(solution)/shard_map/ppermute | solution.py:538
  31.6 3.5 %copy-start.10 = (f32[2,6,2,8,128]{4,3,2,1,0:T(8,128)}, f32[2,6,2,8,128]{4,3,2,1,0:T(8,128)S(1)}, u32[]{:S(2)}) copy-start(f32[2,6,2,8,128]{4,3,2,1,0:T(8,128)S(1)} %collective-permute-done.4.s_edge) | copy-start | bytes 294916
  34.4 0.7 copy-start.11
  35.1 71.2 %copy-start.7 = (bf16[256,64]{0,1:T(8,128)(2,1)S(1)}, bf16[256,64]{0,1:T(8,128)(2,1)}, u32[]{:S(2)}) copy-start(bf16[256,64]{0,1:T(8,128)(2,1)} %param.26) | copy-start | bytes 98308
  66.2 54.7 %collective-permute-start.6 = (f32[6,256,256]{2,1,0:T(8,128)}, f32[6,256,256]{2,1,0:T(8,128)S(1)}, u32[]{:S(2)}, u32[]{:S(2)}) collective-permute-start(f32[6,256,256]{2,1,0:T(8,128)} %get-tuple-element.49), channel_id=1, source_target_pairs={{0,4},{4,8},{8,12},{12,16},{16,20},{20,24},{24,28},{1,5},{5,9},{9,... | collective-permute-start | bytes 4718600 | tf_op jit(solution)/shard_map/ppermute | solution.py:535
  92.2 28.7 %collective-permute-start.7 = (f32[6,256,256]{2,1,0:T(8,128)}, f32[6,256,256]{2,1,0:T(8,128)S(1)}, u32[]{:S(2)}, u32[]{:S(2)}) collective-permute-start(f32[6,256,256]{2,1,0:T(8,128)} %get-tuple-element.50), channel_id=1, source_target_pairs={{4,0},{8,4},{12,8},{16,12},{20,16},{24,20},{28,24},{5,1},{9,5},{13... | collective-permute-start | bytes 4718600 | tf_op jit(solution)/shard_map/ppermute | solution.py:536
  93.5 6.9 %collective-permute-start.9 = (f32[8,2,8,128]{3,2,1,0:T(8,128)}, f32[8,2,8,128]{3,2,1,0:T(8,128)S(1)}, u32[]{:S(2)}, u32[]{:S(2)}) collective-permute-start(f32[8,2,8,128]{3,2,1,0:T(8,128)} %get-tuple-element.52), channel_id=1, source_target_pairs={{0,1},{1,2},{2,3},{3,0},{4,5},{5,6},{6,7},{7,4},{8,9},{9,10},{10,1... | collective-permute-start | bytes 196616 | tf_op jit(solution)/shard_map/ppermute | solution.py:534
  95.2 6.5 %collective-permute-start.8 = (f32[8,2,8,128]{3,2,1,0:T(8,128)}, f32[8,2,8,128]{3,2,1,0:T(8,128)S(1)}, u32[]{:S(2)}, u32[]{:S(2)}) collective-permute-start(f32[8,2,8,128]{3,2,1,0:T(8,128)} %get-tuple-element.51), channel_id=1, source_target_pairs={{1,0},{2,1},{3,2},{0,3},{5,4},{6,5},{7,6},{4,7},{9,8},{10,9},{11,1... | collective-permute-start | bytes 196616 | tf_op jit(solution)/shard_map/ppermute | solution.py:533
  100.5 20.4 %copy-start.3 = (f32[8,2,8,128]{3,2,1,0:T(8,128)}, f32[8,2,8,128]{3,2,1,0:T(8,128)S(1)}, u32[]{:S(2)}) copy-start(f32[8,2,8,128]{3,2,1,0:T(8,128)S(1)} %collective-permute-done.9.last) | copy-start | bytes 196612
  101.6 19.2 %copy-start.4 = (f32[8,2,8,128]{3,2,1,0:T(8,128)}, f32[8,2,8,128]{3,2,1,0:T(8,128)S(1)}, u32[]{:S(2)}) copy-start(f32[8,2,8,128]{3,2,1,0:T(8,128)S(1)} %collective-permute-done.8.first) | copy-start | bytes 196612
  102.3 18.6 %collective-permute-start.10 = (f32[2,6,2,8,128]{4,3,2,1,0:T(8,128)}, f32[2,6,2,8,128]{4,3,2,1,0:T(8,128)S(1)}, u32[]{:S(2)}, u32[]{:S(2)}) collective-permute-start(f32[2,6,2,8,128]{4,3,2,1,0:T(8,128)} %pad_maximum_fusion.4), channel_id=1, source_target_pairs={{0,4},{4,8},{8,12},{12,16},{16,20},{20,24},{24,28},{1,5},{5,9},{9,... | collective-permute-start | bytes 294920 | tf_op jit(solution)/shard_map/ppermute | solution.py:537
  104.8 16.0 %collective-permute-start.11 = (f32[2,6,2,8,128]{4,3,2,1,0:T(8,128)}, f32[2,6,2,8,128]{4,3,2,1,0:T(8,128)S(1)}, u32[]{:S(2)}, u32[]{:S(2)}) collective-permute-start(f32[2,6,2,8,128]{4,3,2,1,0:T(8,128)} %pad_maximum_fusion.5), channel_id=1, source_target_pairs={{4,0},{8,4},{12,8},{16,12},{20,16},{24,20},{28,24},{5,1},{9,5},{13... | collective-permute-start | bytes 294920 | tf_op jit(solution)/shard_map/ppermute | solution.py:538
  120.9 0.6 copy-start.8
  120.9 0.7 copy-start.9
  120.9 1.2 copy-start
  120.9 1.7 copy-start.1
  159.5 10.8 %collective-permute-start.12 = (f32[384,256]{1,0:T(8,128)S(1)}, f32[384,256]{1,0:T(8,128)S(1)}, u32[]{:S(2)}, u32[]{:S(2)}) collective-permute-start(f32[384,256]{1,0:T(8,128)S(1)} %dynamic-slice_bitcast_fusion), channel_id=1, source_target_pairs={{0,4},{4,0},{8,12},{12,8},{16,20},{20,16},{24,28},{28,24},{1,5},{5... | collective-permute-start | bytes 1179656 | tf_op jit(solution)/shard_map/ppermute | solution.py:511
  171.4 7.2 %collective-permute-start.13 = (f32[192,256]{1,0:T(8,128)S(1)}, f32[192,256]{1,0:T(8,128)S(1)}, u32[]{:S(2)}, u32[]{:S(2)}) collective-permute-start(f32[192,256]{1,0:T(8,128)S(1)} %dynamic-slice_bitcast_fusion.1), channel_id=1, source_target_pairs={{0,8},{4,12},{8,0},{12,4},{16,24},{20,28},{24,16},{28,20},{1,9},{5... | collective-permute-start | bytes 589832 | tf_op jit(solution)/shard_map/ppermute | solution.py:511
  178.7 4.7 %collective-permute-start.14 = (f32[96,256]{1,0:T(8,128)S(1)}, f32[96,256]{1,0:T(8,128)S(1)}, u32[]{:S(2)}, u32[]{:S(2)}) collective-permute-start(f32[96,256]{1,0:T(8,128)S(1)} %dynamic-slice_bitcast_fusion.2), channel_id=1, source_target_pairs={{0,16},{4,20},{8,24},{12,28},{16,0},{20,4},{24,8},{28,12},{1,17},{... | collective-permute-start | bytes 294920 | tf_op jit(solution)/shard_map/ppermute | solution.py:511
  183.4 4.7 %collective-permute-start.15 = (f32[96,256]{1,0:T(8,128)S(1)}, f32[96,256]{1,0:T(8,128)S(1)}, u32[]{:S(2)}, u32[]{:S(2)}) collective-permute-start(f32[96,256]{1,0:T(8,128)S(1)} %bitcast_add_fusion.2), channel_id=1, source_target_pairs={{0,1},{1,0},{2,3},{3,2},{4,5},{5,4},{6,7},{7,6},{8,9},{9,8},{10,11... | collective-permute-start | bytes 294920 | tf_op jit(solution)/shard_map/ppermute | solution.py:517
  188.1 5.6 %collective-permute-start.16 = (f32[96,256]{1,0:T(8,128)S(1)}, f32[96,256]{1,0:T(8,128)S(1)}, u32[]{:S(2)}, u32[]{:S(2)}) collective-permute-start(f32[96,256]{1,0:T(8,128)S(1)} %add.84), channel_id=1, source_target_pairs={{0,2},{1,3},{2,0},{3,1},{4,6},{5,7},{6,4},{7,5},{8,10},{9,11},{10,... | collective-permute-start | bytes 294920 | tf_op jit(solution)/shard_map/ppermute | solution.py:517
  193.7 4.7 %collective-permute-start.17 = (f32[96,256]{1,0:T(8,128)S(1)}, f32[96,256]{1,0:T(8,128)S(1)}, u32[]{:S(2)}, u32[]{:S(2)}) collective-permute-start(f32[96,256]{1,0:T(8,128)S(1)} %add.85), channel_id=1, source_target_pairs={{0,16},{4,20},{8,24},{12,28},{16,0},{20,4},{24,8},{28,12},{1,17},{... | collective-permute-start | bytes 294920 | tf_op jit(solution)/shard_map/ppermute | solution.py:520
  198.4 5.7 %collective-permute-start.18 = (f32[192,256]{1,0:T(8,128)S(1)}, f32[192,256]{1,0:T(8,128)S(1)}, u32[]{:S(2)}, u32[]{:S(2)}) collective-permute-start(f32[192,256]{1,0:T(8,128)S(1)} %pad_maximum_fusion.1), channel_id=1, source_target_pairs={{0,8},{4,12},{8,0},{12,4},{16,24},{20,28},{24,16},{28,20},{1,9},{5... | collective-permute-start | bytes 589832 | tf_op jit(solution)/shard_map/ppermute | solution.py:520
  204.2 1.8 collective-permute-start.19
where the time goes:
time: 210 us; the launch traced here: 209 us
  Pallas kernels  92.7 us (44%)
  starting transfers between devices  62 us (30%)
  waiting for transfers between devices  39.4 us (19%)
  local copies, waits for them, and re-layouts  10.8 us (5%)
  other arithmetic  3.36 us (2%)
    pallas_call x1, Pallas kernels, per_device(): pl.pallas_call(transport_kernel, out_shape=(shape((planes * rows, width),...  31 us
    ppermute x2, starting transfers between devices, exchange(): s = lax.ppermute(north, 'band', up)  29.6 us
    pallas_call x1, Pallas kernels, per_device(): pl.pallas_call(adjoint_kernel, out_shape=flat, in_specs=specs(8), out_spe...  25.2 us
    pallas_call x1, Pallas kernels, per_device(): pl.pallas_call(recompute_kernel, out_shape=(flat, flat, shape((rows, fin,...  13.8 us
    ppermute x3, waiting for transfers between devices, sum_over_devices(): x = mine + lax.ppermute(theirs, 'band', perm)  12.9 us
    pallas_call x1, Pallas kernels, per_device(): pl.pallas_call(forward_kernel, out_shape=(flat, halo, halo, side, side, s...  12.1 us
    ppermute x3, waiting for transfers between devices, sum_over_devices(): other = lax.ppermute(x, 'band', perm)  11.7 us
    pallas_call x1, Pallas kernels, per_device(): pl.pallas_call(gradient_kernel, out_shape=shape((padded, hid), F32), in_s...  10.6 us
  transfers between devices with their start and end apart: 20, of which 13 were waited for; matrix products, arithmetic and copies ran while one was open for 2% of the time, Pallas kernels for 7%

commit v1 on v0

v1 whole, which is shorter than its diff:
```python
import functools

import jax
import jax.numpy as jnp
from jax import lax
from jax.experimental import pallas as pl
from jax.experimental.pallas import tpu as pltpu
from jax.sharding import PartitionSpec as P

STEPS = 6
DIFFUSIVITY = 0.1
LATITUDE_EDGE = 1.25
LAND_SHARE = 0.7
SETTLING_SPEEDS = (0.5, 1.0, 1.5, 2.0)

F32 = jnp.float32
BF16 = jnp.bfloat16
LANES = 128
SIDE = 8
WIDE = 16
VMEM_LIMIT = 56 * 1024 * 1024


def params():
    return pltpu.CompilerParams(vmem_limit_bytes=VMEM_LIMIT)


def cost(microseconds):
    return pl.CostEstimate(
        flops=int(microseconds * 1e6), bytes_accessed=int(microseconds * 3e6), transcendentals=0
    )


def specs(count):
    return [pl.BlockSpec(memory_space=pltpu.VMEM)] * count


def dot(a, b, dims):
    return lax.dot_general(a, b, (dims, ((), ())), preferred_element_type=F32)


def sigmoid(x):
    return 0.5 + 0.5 * jnp.tanh(0.5 * x)


def bias_column(bias_ref):
    row = bias_ref[...]
    return jnp.broadcast_to(row, (LANES, row.shape[1])).T


def add_column(values, column):
    width = values.shape[1] // LANES
    return values + jnp.concatenate([column] * width, axis=1)


def spread(ref, start, count):
    return jnp.concatenate(
        [ref[t, pl.ds(start, count, stride=8), :] for t in range(ref.shape[0])], axis=1
    )


def put_spread(ref, start, values):
    for t in range(ref.shape[0]):
        ref[t, pl.ds(start, values.shape[0], stride=8), :] = values[:, t * LANES : (t + 1) * LANES]


def fetch_tiles(source, dest, sem):
    copies = [
        pltpu.make_async_copy(source.at[:, pl.ds(t * LANES, LANES)], dest.at[t], sem.at[t])
        for t in range(dest.shape[0])
    ]
    for copy in copies:
        copy.start()
    for copy in copies:
        copy.wait()


def tiles_at(ref, at):
    return [ref[t, at, :] for t in range(ref.shape[0])]


def split_tiles(values):
    return [values[:, t * LANES : (t + 1) * LANES] for t in range(values.shape[1] // LANES)]


def closure_row(r, conc, cls, embed_t, w1, c1, w2, c2, w3, c3):
    planes = conc.shape[1] // 8
    features = spread(conc, r, planes).astype(BF16)
    classes = cls[pl.ds(r, 1), :]
    n_class = embed_t.shape[1]
    ids = lax.broadcasted_iota(jnp.int32, (n_class, classes.shape[1]), 0)
    onehot = (ids == classes).astype(F32).astype(BF16)
    surface = dot(embed_t, onehot, ((1,), (0,))).astype(BF16)
    inputs = jnp.concatenate([features, surface], axis=0)
    pre1 = add_column(dot(w1[...], inputs, ((0,), (0,))), c1)
    sig1 = sigmoid(pre1)
    act1 = (pre1 * sig1).astype(BF16)
    pre2 = add_column(dot(w2[...], act1, ((0,), (0,))), c2)
    sig2 = sigmoid(pre2)
    act2 = (pre2 * sig2).astype(BF16)
    raw = add_column(dot(w3[...], act2, ((0,), (0,))), c3)
    return inputs, pre1, sig1, act1, pre2, sig2, act2, raw


def factor_level(z, carry, conc, eddy, removal, levels):
    rests, halves, lower = carry
    level = pl.ds(pl.multiple_of(z * 8, 8), 8)
    upper = split_tiles(jnp.where(z < levels - 1, eddy[level, :], 0.0))
    rem = tiles_at(removal, level)
    bins = len(SETTLING_SPEEDS)
    tiles = len(upper)
    new_rests, new_halves, invs, ratios = [], [], [], []
    for b in range(bins):
        at = pl.ds(pl.multiple_of((z * bins + b) * 8, 8), 8)
        for t in range(tiles):
            n = b * tiles + t
            excess = 1.0 + SETTLING_SPEEDS[b] * rem[t] + rests[n]
            inv = 1.0 / (excess + upper[t])
            ratio = upper[t] * inv
            half = (conc[t, at, :] + lower[t] * halves[n]) * inv
            new_rests.append(ratio * excess)
            new_halves.append(half)
            invs.append(inv)
            ratios.append(ratio)
    return (tuple(new_rests), tuple(new_halves), tuple(upper)), invs, ratios, new_halves


def zero_tiles(count):
    return tuple(jnp.zeros((8, LANES), F32) for _ in range(count))


def store_bins(ref, z, bins, values):
    tiles = ref.shape[0]
    for b in range(bins):
        at = pl.ds(pl.multiple_of((z * bins + b) * 8, 8), 8)
        for t in range(tiles):
            ref[t, at, :] = values[b * tiles + t]


def load_bins(ref, z, bins):
    out = []
    for b in range(bins):
        out += tiles_at(ref, pl.ds(pl.multiple_of((z * bins + b) * 8, 8), 8))
    return out


def turned(source, r, p, q):
    return source[q, pl.ds(p * LANES * 8 + r, LANES, stride=8), :].T


def removal_rate(raw, landing):
    soft = jnp.maximum(raw, 0.0) + jnp.log1p(jnp.exp(-jnp.abs(raw)))
    return soft * landing


def landing_row(land, r):
    return 1.0 - LAND_SHARE * land[r : r + 1, :].astype(F32)


def back_substitute(settled, ratio, levels, bins):
    tiles = settled.shape[0]

    def up(i, following):
        z = levels - 1 - i
        halves, ratios = load_bins(settled, z, bins), load_bins(ratio, z, bins)
        new = tuple(h + r * q for h, r, q in zip(halves, ratios, following))
        store_bins(settled, z, bins, new)
        return new

    lax.fori_loop(0, levels, up, zero_tiles(bins * tiles), unroll=4)


def forward_kernel(
    conc_hbm, eddy, land, cls, embed, w1, b1, w2, b2, w3, b3, wind_u, wind_v,
    near, far0, far1, first, last,
    settled_h, inverse_h, ratio_h, rate_h, inputs_h, act1_h, slope1_h, act2_h, slope2_h,
    conc, removal, own, settled, inverse, ratio, rate, inputs, act1, slope1, act2, slope2,
    sem, row_sem, kept_sem, halo_sem,
):
    fetch_tiles(conc_hbm, conc, sem)
    levels = eddy.shape[0] // 8
    bins = conc_hbm.shape[0] // eddy.shape[0]
    planes = levels * bins
    width = conc_hbm.shape[1]
    tiles = width // LANES
    lon_total = wind_u.shape[1]
    c1, c2, c3 = bias_column(b1), bias_column(b2), bias_column(b3)
    embed_t = embed[...].T.astype(BF16)
    copies = []

    def send(source, dest, sem):
        copies.append(pltpu.make_async_copy(source, dest, sem))
        copies[-1].start()

    for r in range(8):
        given, pre1, sig1, first_act, pre2, sig2, second_act, raw = closure_row(
            r, conc, cls, embed_t, w1, c1, w2, c2, w3, c3
        )
        inputs[r] = given
        act1[r] = first_act
        act2[r] = second_act
        slope1[r] = sig1 * (1.0 + pre1 * (1.0 - sig1))
        slope2[r] = sig2 * (1.0 + pre2 * (1.0 - sig2))
        landing = landing_row(land, r)
        put_spread(removal, r, removal_rate(raw, landing))
        put_spread(rate, r, sigmoid(raw) * landing)
        rows = (inputs, inputs_h), (act1, act1_h), (slope1, slope1_h), (act2, act2_h), (slope2, slope2_h)
        for n, (source, dest) in enumerate(rows):
            send(source.at[r], dest.at[r], row_sem.at[r, n])
    send(rate, rate_h, kept_sem.at[0])

    def down(z, carry):
        carry, invs, ratios, halves = factor_level(z, carry, conc, eddy, removal, levels)
        store_bins(ratio, z, bins, ratios)
        store_bins(inverse, z, bins, invs)
        store_bins(settled, z, bins, halves)
        return carry

    many = bins * tiles
    start = (zero_tiles(many), zero_tiles(many), zero_tiles(tiles))
    lax.fori_loop(0, levels, down, start, unroll=2)
    send(ratio, ratio_h, kept_sem.at[1])
    send(inverse, inverse_h, kept_sem.at[2])
    back_substitute(settled, ratio, levels, bins)
    send(settled, settled_h, kept_sem.at[3])

    lon0 = lax.axis_index("lev") * width
    shift = lax.rem(lon_total + WIDE - lon0, lon_total)
    span = width + LANES
    winds = [pltpu.roll(wind[...], shift, 1)[:, :span] for wind in (wind_u, wind_v)]
    empty = jnp.zeros((8 - 2 * span // LANES, LANES), F32)

    for r in range(8):
        rows = []
        for wind in winds:
            rows += split_tiles(wind[r : r + 1, :])
        own[r, 0, width:, :] = jnp.concatenate(rows + [empty], axis=0)
    near_row, far_row = first_rows()
    for p, far in enumerate((far0, far1)):
        for r in range(8):
            for q in range(tiles):
                block = turned(settled, r, p, q)
                own[r, p, q * LANES : (q + 1) * LANES, :] = block
                if q == 0:
                    first[r, p] = block[:WIDE]
                if q == tiles - 1:
                    last[r, p] = block[LANES - WIDE :]
        send(own.at[pl.ds(far_row, STEPS), p, pl.ds(0, far.shape[1]), :], far, halo_sem.at[p])
    send(own.at[pl.ds(near_row, STEPS)], near, halo_sem.at[2])
    wait_copies(copies)


def even_band():
    return lax.rem(lax.axis_index("band"), 2) == 0


def first_rows():
    rest = 8 - STEPS
    return jnp.where(even_band(), rest, 0), jnp.where(even_band(), 0, rest)


def start_copies(pairs, sem):
    copies = [pltpu.make_async_copy(a, b, sem.at[i]) for i, (a, b) in enumerate(pairs)]
    for copy in copies:
        copy.start()
    return copies


def wait_copies(copies):
    for copy in copies:
        copy.wait()


def row_pairs(ext, near, far, own_near, own_far, at, data):
    rest = 8 - STEPS
    even = even_band()
    near_row, _ = first_rows()
    other = jnp.where(even, 0, STEPS - rest)
    other_at = STEPS + jnp.where(even, 0, STEPS)
    near_at, far_at = halo_rows()
    return [
        (near.at[:, data, :], ext.at[pl.ds(near_at, STEPS), at, :]),
        (far.at[:, data, :], ext.at[pl.ds(far_at, STEPS), at, :]),
        (own_near.at[:, data, :], ext.at[pl.ds(STEPS + near_row, STEPS), at, :]),
        (own_far.at[pl.ds(other, rest), data, :], ext.at[pl.ds(other_at, rest), at, :]),
    ]


def halo_rows():
    north = STEPS + 8
    return jnp.where(even_band(), north, 0), jnp.where(even_band(), 0, north)


def fill_coefficients(wind, turned_wind, along, across, centre, offset):
    rows, seg = across.shape[:2]
    span = turned_wind.shape[0] // LANES
    for q in range(span):
        lines = [wind[i, q : q + 1, :] for i in range(rows)]
        lines += [wind[i, span + q : span + q + 1, :] for i in range(rows)]
        lines = jnp.concatenate(lines, axis=0) + DIFFUSIVITY
        high = lines.astype(BF16).astype(F32)
        middle = (lines - high).astype(BF16).astype(F32)
        low = (lines - high - middle).astype(BF16).astype(F32)
        empty = jnp.zeros((LANES - 6 * rows, LANES), F32)
        turned_wind[pl.ds(q * LANES, LANES), :] = jnp.concatenate([high, middle, low, empty], axis=0).T
    terms = jnp.concatenate(
        [turned_wind[pl.ds(offset + l, 8, stride=seg), :] for l in range(seg)], axis=0
    ).astype(BF16)
    term = lax.broadcasted_iota(jnp.int32, (LANES, 2 * LANES), 0)
    second = jnp.where(lax.broadcasted_iota(jnp.int32, (LANES, 2 * LANES), 1) < LANES, 0, rows)
    place = jnp.where(term < 6 * rows, lax.rem(term, 2 * rows), -1) - second

    def fill(i, carry):
        pick = jnp.where(place == i, 1.0, 0.0).astype(BF16)
        values = dot(terms, pick, ((1,), (0,)))
        for l in range(seg):
            u = values[8 * l : 8 * l + 8, :LANES]
            v = values[8 * l : 8 * l + 8, LANES:]
            along[i, l + 1] = u
            across[i, l] = v
            centre[i, l] = (1.0 - 2.0 * DIFFUSIVITY) - u - v
            if l == seg - 1:
                along[i, 0] = pltpu.roll(u, 1, 0)
        return carry

    lax.fori_loop(0, rows, fill, 0, unroll=2)


def run_steps(ext, a, b, along, across, centre, transposed):
    rows, seg = a.shape[:2]
    south_end = lax.axis_index("band") == 0
    north_end = lax.axis_index("band") == lax.axis_size("band") - 1

    def load(i, carry):
        for l in range(seg):
            a[i, l] = ext[i, pl.ds(l, 8, stride=seg), :]
        return carry

    lax.fori_loop(0, rows, load, 0)
    for edge in (STEPS - 1, rows - STEPS):
        b[edge] = jnp.zeros(b.shape[1:], F32)

    source, target = a, b
    for step in range(1, STEPS + 1):
        low = jnp.where(south_end, STEPS, step)
        high = jnp.where(north_end, rows - STEPS, rows - step)

        def row(i, carry, source=source, target=target, final=step == STEPS):
            before = pltpu.roll(source[i, seg - 1], 1, 0)
            here = source[i, 0]
            wrapped = pltpu.roll(here, 7, 0)
            for l in range(seg):
                if transposed:
                    ka, kb = along[i, l + 1], across[i, l]
                else:
                    ka, kb = along[i, l], across[i - 1, l]
                kc = centre[i, l]
                east = source[i, l + 1] if l + 1 < seg else wrapped
                west = before
                s, n = source[i - 1, l], source[i + 1, l]
                if transposed:
                    plain, x, y = west + s, east, n
                else:
                    plain, x, y = east + n, west, s
                new = (kc * here + ka * x) + (kb * y + DIFFUSIVITY * plain)
                if final:
                    ext[i, pl.ds(l, 8, stride=seg), :] = new
                else:
                    target[i, l] = new
                before, here = here, east
            return carry

        lax.fori_loop(low, high, row, 0)
        source, target = target, source


def transport_kernel(part, *refs):
    (
        near, far, own_near, own_far, east, west, near_edge, far_edge,
        observed_h, observed_e, observed_w, area,
    ) = refs[:12]
    near, own_near = near.at[:, part], own_near.at[:, part]
    refs = list(refs[12:])
    given_wind = None if part == 0 else refs.pop(0)
    final_h, m_near, m_far = refs[:3]
    refs = refs[3:]
    wind = refs.pop(0) if part == 0 else given_wind
    ext, a, b, along, across, centre, turned_wind, observed, misfit, sem, wind_sem, seen_sem, out_sem = refs
    width = observed_h.shape[2]
    if part == 0:
        line = pl.ds(width, 8)
        winds = start_copies(
            row_pairs(wind, near, far, own_near, own_far, slice(None), line), wind_sem
        )
    mid = pl.ds(WIDE, width)
    low, high = pl.ds(0, WIDE), pl.ds(WIDE + width, WIDE)
    own = pl.ds(STEPS, 8)
    near_at, far_at = (pl.ds(i, STEPS) for i in halo_rows())
    copies = start_copies(
        row_pairs(ext, near, far, own_near, own_far, mid, pl.ds(0, width))
        + [
            (east.at[:, part], ext.at[own, high, :]),
            (west.at[:, part], ext.at[own, low, :]),
            (near_edge.at[0, :, part], ext.at[near_at, high, :]),
            (near_edge.at[1, :, part], ext.at[near_at, low, :]),
            (far_edge.at[0, :, part], ext.at[far_at, high, :]),
            (far_edge.at[1, :, part], ext.at[far_at, low, :]),
        ],
        sem,
    )
    seen = start_copies(
        [
            (observed_h.at[:, part], observed.at[:, pl.ds(SIDE, width), :]),
            (observed_w.at[:, part], observed.at[:, pl.ds(0, SIDE), :]),
            (observed_e.at[:, part], observed.at[:, pl.ds(SIDE + width, SIDE), :]),
        ],
        seen_sem,
    )
    if part == 0:
        wait_copies(winds)
    fill_coefficients(wind, turned_wind, along, across, centre, 0)
    wait_copies(copies)
    run_steps(ext, a, b, along, across, centre, False)
    results = start_copies([(ext.at[own, mid, :], final_h)], out_sem)
    wait_copies(seen)
    span = width + 2 * SIDE
    for r in range(8):
        value = ext[STEPS + r, WIDE - SIDE : WIDE - SIDE + span, :]
        misfit[r] = area[r : r + 1, :] * (value - observed[r])
    near_row, far_row = first_rows()
    results += start_copies(
        [
            (misfit.at[pl.ds(far_row, STEPS)], m_far),
            (misfit.at[pl.ds(near_row, STEPS)], m_near),
        ],
        out_sem.at[pl.ds(1, 2)],
    )
    wait_copies(results)


def adjoint_steps(part, near, far, own_near, own_far, wind, ext, a, b, along, across, centre, turned_wind, adjoint, sem):
    every = slice(None)
    copies = start_copies(row_pairs(ext, near, far, own_near, own_far, every, every), sem)
    fill_coefficients(wind, turned_wind, along, across, centre, WIDE - SIDE)
    wait_copies(copies)
    run_steps(ext, a, b, along, across, centre, True)
    turn_back(ext, STEPS, SIDE, adjoint, part * LANES * 8)


def adjoint_kernel(near, far, own_near, own_far, wind, adjoint, ext, a, b, along, across, centre, turned_wind, sem):
    adjoint_steps(
        0, near, far, own_near, own_far, wind, ext, a, b, along, across, centre, turned_wind, adjoint, sem
    )


def turn_kernel(source_hbm, out, first, last, source, sem):
    fetch_tiles(source_hbm, source, sem)
    tiles = source.shape[0]
    for r in range(8):
        for p in range(out.shape[1]):
            for q in range(tiles):
                block = turned(source, r, p, q)
                out[r, p, q * LANES : (q + 1) * LANES, :] = block
                if q == 0:
                    first[r, p] = block[:SIDE]
                if q == tiles - 1:
                    last[r, p] = block[LANES - SIDE :]


def turn_back(source, first_row, offset, dest, base):
    for r in range(8):
        for q in range(dest.shape[0]):
            at = offset + q * LANES
            block = source[first_row + r, at : at + LANES, :].T
            dest[q, pl.ds(base + r, LANES, stride=8), :] = block


def native_kernel(*refs):
    sources, (out_h, tiles, sem) = refs[:-3], refs[-3:]
    for part, source in enumerate(sources):
        turn_back(source, 0, 0, tiles, part * LANES * 8)
    wait_copies(
        start_copies(
            [(tiles.at[t], out_h.at[:, pl.ds(t * LANES, LANES)]) for t in range(tiles.shape[0])], sem
        )
    )


def gradient_kernel(
    near, far, own_near, own_far, wind, eddy, w2, w3, lower_h,
    settled_h, inverse_h, ratio_h, rate_h, inputs_h, act1_h, slope1_h, act2_h, slope2_h,
    out,
    ext, a, b, along, across, centre, turned_wind, adjoint, half, raw_grad,
    settled, inverse, ratio, rate, inputs, act1, slope1, act2, slope2, sem, kept_sem,
):
    done = lower_h.shape[1]
    kept = start_copies(
        [
            (lower_h, adjoint.at[:, pl.ds(0, done), :]),
            (settled_h, settled), (inverse_h, inverse), (ratio_h, ratio), (rate_h, rate),
            (inputs_h, inputs), (act1_h, act1), (slope1_h, slope1), (act2_h, act2), (slope2_h, slope2),
        ],
        kept_sem,
    )
    adjoint_steps(
        1, near, far, own_near, own_far, wind, ext, a, b, along, across, centre, turned_wind, adjoint, sem
    )
    wait_copies(kept)
    levels = eddy.shape[0] // 8
    bins = adjoint.shape[1] // eddy.shape[0]
    width = eddy.shape[1]
    tiles = width // LANES
    many = bins * tiles

    def down(z, carry):
        before, lower = carry
        upper = tuple(split_tiles(eddy[pl.ds(pl.multiple_of(z * 8, 8), 8), :]))
        rights, invs = load_bins(adjoint, z, bins), load_bins(inverse, z, bins)
        new = tuple(
            (rights[n] + lower[n % tiles] * before[n]) * invs[n] for n in range(many)
        )
        store_bins(half, z, bins, new)
        return new, upper

    lax.fori_loop(0, levels, down, (zero_tiles(many), zero_tiles(tiles)), unroll=4)

    def up(i, following):
        z = levels - 1 - i
        halves, ratios = load_bins(half, z, bins), load_bins(ratio, z, bins)
        own = load_bins(settled, z, bins)
        new = tuple(h + r * q for h, r, q in zip(halves, ratios, following))
        at = pl.ds(pl.multiple_of(z * 8, 8), 8)
        for t in range(tiles):
            total = sum(
                SETTLING_SPEEDS[b] * (new[b * tiles + t] * own[b * tiles + t])
                for b in range(bins)
            )
            raw_grad[t, at, :] = -total * rate[t, at, :]
        return new

    lax.fori_loop(0, levels, up, zero_tiles(many), unroll=4)

    fin, hid = inputs.shape[1], act1.shape[1]
    g1 = jnp.zeros((fin, hid), F32)
    g2 = jnp.zeros((hid, hid), F32)
    g3 = jnp.zeros((levels, hid), F32)
    s1 = jnp.zeros((hid, width), F32)
    s2 = jnp.zeros((hid, width), F32)
    s3 = jnp.zeros((levels, width), F32)
    for r in range(8):
        grad3 = spread(raw_grad, r, levels)
        half3 = grad3.astype(BF16)
        s3 = s3 + grad3
        g3 = g3 + dot(half3, act2[r], ((1,), (1,)))
        grad2 = dot(w3[...], half3, ((1,), (0,))) * slope2[r]
        half2 = grad2.astype(BF16)
        s2 = s2 + grad2
        g2 = g2 + dot(act1[r], half2, ((1,), (1,)))
        grad1 = dot(w2[...], half2, ((1,), (0,))) * slope1[r]
        half1 = grad1.astype(BF16)
        s1 = s1 + grad1
        g1 = g1 + dot(inputs[r], half1, ((1,), (1,)))
    out[:fin, :] = g1
    out[fin : fin + hid, :] = g2
    at = fin + hid
    out[at : at + levels, :] = g3
    at += levels
    rows1 = jnp.sum(s1.T, axis=0, keepdims=True)
    rows2 = jnp.sum(s2.T, axis=0, keepdims=True)
    rows3 = jnp.sum(s3.T, axis=0, keepdims=True)
    rows3 = jnp.concatenate([rows3, jnp.zeros((1, hid - levels), F32)], axis=1)
    out[at:, :] = jnp.zeros((out.shape[0] - at, hid), F32)
    out[at : at + 1, :] = rows1
    out[at + 1 : at + 2, :] = rows2
    out[at + 2 : at + 3, :] = rows3


def piece(parts, index):
    return lax.dynamic_index_in_dim(parts, index, 0, False)


def sum_over_devices(x):
    size = lax.axis_size("band")
    index = lax.axis_index("band")
    columns = x.shape[1]
    rounds = []
    step = 1
    while step < size:
        radix = 2 if step == 1 or size // step % 4 else 4
        at = (index // step) % radix
        parts = x.reshape(radix, -1, columns)
        total = piece(parts, at)
        for m in range(radix - 1, 0, -1):
            perm = [(i, i ^ (m * step)) for i in range(size)]
            total = total + lax.ppermute(piece(parts, at ^ m), "band", perm)
        x = total
        rounds.append((step, radix, at))
        step *= radix
    lev = lax.axis_size("lev")
    step = 1
    while step < lev:
        x = x + lax.ppermute(x, "lev", [(i, i ^ step) for i in range(lev)])
        step *= 2
    for step, radix, at in reversed(rounds):
        got = [x] + [
            lax.ppermute(x, "band", [(i, i ^ (m * step)) for i in range(size)])
            for m in range(1, radix)
        ]
        pieces = []
        for k in range(radix):
            chosen = got[0]
            for m in range(1, radix):
                chosen = jnp.where((at ^ k) == m, got[m], chosen)
            pieces.append(chosen)
        x = jnp.concatenate(pieces, 0)
    return x


def from_lon_neighbours(first, last):
    levs = lax.axis_size("lev")
    east = lax.ppermute(first, "lev", [((i + 1) % levs, i) for i in range(levs)])
    west = lax.ppermute(last, "lev", [(i, (i + 1) % levs) for i in range(levs)])
    return east, west


def from_near(x):
    return lax.ppermute(x, "band", [(i, i ^ 1) for i in range(lax.axis_size("band"))])


def from_far(x):
    bands = lax.axis_size("band")
    pairs = [(i, i + 1) for i in range(1, bands - 1, 2)]
    return lax.ppermute(x, "band", pairs + [(j, i) for i, j in pairs])


def per_device(
    concentration,
    observed,
    wind_zonal,
    wind_meridional,
    eddy_diffusion,
    land_mask,
    surface_class,
    class_embed,
    weight_first,
    bias_first,
    weight_second,
    bias_second,
    weight_third,
    bias_third,
):
    levels, bins, rows, width = concentration.shape
    lon_total = wind_zonal.shape[1]
    planes = levels * bins
    groups = planes // 8
    fin, hid = weight_first.shape
    shape = jax.ShapeDtypeStruct
    conc = concentration.reshape(planes * rows, width)
    eddy = eddy_diffusion.reshape(levels * rows, width)
    closure = (
        land_mask, surface_class, class_embed, weight_first, bias_first.reshape(1, -1),
        weight_second, bias_second.reshape(1, -1), weight_third, bias_third.reshape(1, -1),
    )
    tiles = width // LANES
    flat = shape((tiles, planes * rows, LANES), F32)
    level_flat = shape((tiles, levels * rows, LANES), F32)
    any_space = pl.BlockSpec(memory_space=pl.ANY)
    tiled = pltpu.VMEM((tiles, planes * rows, LANES), F32)
    tiled_levels = pltpu.VMEM((tiles, levels * rows, LANES), F32)
    parts = planes // LANES
    halos = (
        shape((STEPS, parts, width + 8, LANES), F32),
        shape((STEPS, width + 8, LANES), F32),
        shape((STEPS, width, LANES), F32),
    )
    m_halo = shape((STEPS, width + 2 * SIDE, LANES), F32)
    wide = shape((rows, parts, WIDE, LANES), F32)
    side = shape((rows, parts, SIDE, LANES), F32)
    across_lanes = shape((rows, parts, width, LANES), F32)
    n_rows = rows + 2 * STEPS

    def stepping(extended):
        seg = extended // 8
        return [
            pltpu.VMEM((n_rows, extended, LANES), F32),
            pltpu.VMEM((n_rows, seg, 8, LANES), F32),
            pltpu.VMEM((n_rows, seg, 8, LANES), F32),
            pltpu.VMEM((n_rows, seg + 1, 8, LANES), F32),
            pltpu.VMEM((n_rows, seg, 8, LANES), F32),
            pltpu.VMEM((n_rows, seg, 8, LANES), F32),
            pltpu.VMEM((width + LANES, LANES), F32),
        ]

    kept_shapes = (
        flat, flat, flat, level_flat,
        shape((rows, fin, width), BF16),
        shape((rows, hid, width), BF16),
        shape((rows, hid, width), F32),
        shape((rows, hid, width), BF16),
        shape((rows, hid, width), F32),
    )
    kept_scratch = [pltpu.VMEM(x.shape, x.dtype) for x in kept_shapes]
    near, far0, far1, first, last, *kept = pl.pallas_call(
        forward_kernel,
        out_shape=(*halos, wide, wide, *kept_shapes),
        in_specs=[any_space] + specs(12),
        out_specs=tuple([any_space] * 3 + specs(2) + [any_space] * 9),
        scratch_shapes=[
            tiled, tiled_levels, pltpu.VMEM((rows, *halos[0].shape[1:]), F32), *kept_scratch,
            pltpu.SemaphoreType.DMA((tiles,)),
            pltpu.SemaphoreType.DMA((rows, 5)),
            pltpu.SemaphoreType.DMA((4,)),
            pltpu.SemaphoreType.DMA((3,)),
        ],
        compiler_params=params(),
        cost_estimate=cost(14),
        name="forward",
    )(conc, eddy, *closure, wind_zonal, wind_meridional)

    got_far0 = from_far(far0)
    e, w = from_lon_neighbours(first, last)
    got_near = from_near(near)

    observed_b, _ = lax.optimization_barrier((observed, first))
    observed_flat = observed_b.astype(F32).reshape(planes * rows, width)
    observed_turned, observed_first, observed_last = pl.pallas_call(
        turn_kernel,
        out_shape=(across_lanes, side, side),
        in_specs=[any_space],
        out_specs=tuple(specs(3)),
        scratch_shapes=[tiled, pltpu.SemaphoreType.DMA((tiles,))],
        compiler_params=params(),
        cost_estimate=cost(4),
        name="turn",
    )(observed_flat)
    e, w, observed_first, observed_last = lax.optimization_barrier(
        (e, w, observed_first, observed_last)
    )
    near_row, far_row = first_rows()
    sides = jnp.stack([e, w])
    near_side = lax.dynamic_slice_in_dim(sides, near_row, STEPS, 1)
    far_side = lax.dynamic_slice_in_dim(sides, far_row, STEPS, 1)
    near_edge = from_near(near_side)
    far_edge = from_far(far_side)
    observed_e, observed_w = from_lon_neighbours(observed_first, observed_last)
    far1, *came = lax.optimization_barrier(
        (far1, got_far0, far_edge, near_edge, observed_e, observed_w)
    )
    got_far0, far_edge, near_edge, observed_e, observed_w = came
    got_far1 = from_far(far1)
    total_rows = rows * lax.axis_size("band")
    row_ids = lax.axis_index("band") * rows + jnp.arange(rows, dtype=jnp.int32)
    latitude = LATITUDE_EDGE * (row_ids.astype(F32) + 0.5) / total_rows
    area = jnp.cos(latitude) / (bins * total_rows * lon_total)
    area = jnp.broadcast_to(area[:, None], (rows, LANES))

    wind_shape = shape((n_rows, 8, LANES), F32)
    final_shape = shape((rows, width, LANES), F32)

    def transport(part, got_far, own_far, *winds):
        return pl.pallas_call(
            functools.partial(transport_kernel, part),
            out_shape=(final_shape, m_halo, m_halo) + ((wind_shape,) if part == 0 else ()),
            in_specs=[any_space] * 11 + specs(1 + len(winds)),
            out_specs=tuple([any_space] * 3 + specs(0 if winds else 1)),
            scratch_shapes=stepping(width + 2 * WIDE) + [
                pltpu.VMEM((rows, width + 2 * SIDE, LANES), F32),
                pltpu.VMEM((rows, width + 2 * SIDE, LANES), F32),
                pltpu.SemaphoreType.DMA((10,)),
                pltpu.SemaphoreType.DMA((4,)),
                pltpu.SemaphoreType.DMA((3,)),
                pltpu.SemaphoreType.DMA((3,)),
            ],
            compiler_params=params(),
            cost_estimate=cost(13),
            name=f"transport{part}",
        )(
            got_near, got_far, near, own_far, e, w, near_edge, far_edge,
            observed_turned, observed_e, observed_w, area, *winds,
        )

    final0, m_near0, m_far0, wind = transport(0, got_far0, far0)
    m_near0, m_far0, got_far1 = lax.optimization_barrier((m_near0, m_far0, got_far1))
    gm_far0, gm_near0 = from_far(m_far0), from_near(m_near0)
    final1, m_near1, m_far1 = transport(1, got_far1, far1, wind)
    m_near1, m_far1, gm_far0 = lax.optimization_barrier((m_near1, m_far1, gm_far0))
    gm_far1, gm_near1 = from_far(m_far1), from_near(m_near1)

    final = pl.pallas_call(
        native_kernel,
        out_shape=shape((planes * rows, width), F32),
        in_specs=specs(2),
        out_specs=any_space,
        scratch_shapes=[tiled, pltpu.SemaphoreType.DMA((tiles,))],
        compiler_params=params(),
        cost_estimate=cost(4),
        name="native",
    )(final0, final1)

    adjoint0 = pl.pallas_call(
        adjoint_kernel,
        out_shape=shape((tiles, LANES * rows, LANES), F32),
        in_specs=[any_space] * 4 + specs(1),
        out_specs=specs(1)[0],
        scratch_shapes=stepping(width + 2 * SIDE) + [pltpu.SemaphoreType.DMA((4,))],
        compiler_params=params(),
        cost_estimate=cost(12),
        name="adjoint0",
    )(gm_near0, gm_far0, m_near0, m_far0, wind)

    gm_far1, final = lax.optimization_barrier((gm_far1, final))
    bands = lax.axis_size("band")
    used = fin + hid + levels + 3
    padded = -(-used // (8 * bands)) * (8 * bands)
    grads = pl.pallas_call(
        gradient_kernel,
        out_shape=shape((padded, hid), F32),
        in_specs=[any_space] * 4 + specs(4) + [any_space] * 10,
        out_specs=specs(1)[0],
        scratch_shapes=stepping(width + 2 * SIDE) + [tiled, tiled, tiled_levels, *kept_scratch]
        + [pltpu.SemaphoreType.DMA((4,)), pltpu.SemaphoreType.DMA((10,))],
        compiler_params=params(),
        cost_estimate=cost(17),
        name="gradient",
    )(
        gm_near1, gm_far1, m_near1, m_far1, wind, eddy, weight_second, weight_third, adjoint0,
        *kept,
    )
    grads = sum_over_devices(grads)
    at = fin + hid + levels
    return (
        final.reshape(levels, bins, rows, width),
        grads[:fin],
        grads[at],
        grads[fin : fin + hid],
        grads[at + 1],
        grads[fin + hid : at].T,
        grads[at + 2, :levels],
    )


def solution(mesh):
    return jax.shard_map(
        per_device,
        mesh=mesh,
        in_specs=(
            P(None, None, "band", "lev"),
            P(None, None, "band", "lev"),
            P("band", None),
            P("band", None),
            P(None, "band", "lev"),
            P("band", "lev"),
            P("band", "lev"),
            P(),
            P(),
            P(),
            P(),
            P(),
            P(),
            P(),
        ),
        out_specs=(P(None, None, "band", "lev"), P(), P(), P(), P(), P(), P()),
        check_vma=False,
    )
```

time: 210 us -> 168 us (0.80)
  Pallas kernels: 92.7 us -> 66.2 us
  waiting for transfers between devices: 39.4 us -> 27.5 us
    pallas_call x4 -> x6, Pallas kernels: 82.1 us -> 49.6 us  [the longest x2 19.8 us: transport(): pl.pallas_call(functools.partial(transport_kernel, part), out_shape=(fina...]
    ppermute x18 -> x21, waiting for transfers between devices: 33.6 us -> 20.1 us  [the longest x2 6.51 us: from_lon_neighbours(): west = lax.ppermute(last, 'lev', [(i, (i + 1) % levs) for i in range(levs)])]
    pallas_call x1, Pallas kernels: 10.6 us -> 16.6 us  [per_device(): pl.pallas_call(gradient_kernel, out_shape=shape((padded, hid), F32), in_s...]
    transpose x2 -> x0, local copies, waits for them, and re-layouts: 2.55 us -> none  [per_device(): observed_flat = observed_flat.transpose(1, 0, 2)]
    unnamed x25 -> x29, local copies, waits for them, and re-layouts: 3.3 us -> 4.8 us
    ppermute x18 -> x21, starting transfers between devices: 57.6 us -> 57.7 us  [the longest x4 24.3 us: from_near(): lax.ppermute(x, 'band', [(i, i ^ 1) for i in range(lax.axis_size('band'))])]
  transfers between devices with their start and end apart: 20 -> 23, of which waited for: 13 -> 11; matrix products, arithmetic and copies ran while one was open for 2% -> 1% of each run, Pallas kernels for 7% -> 21%
where the time goes in v1:
time: 168 us
  Pallas kernels  66.2 us (39%)
  starting transfers between devices  60.5 us (36%)
  waiting for transfers between devices  27.5 us (16%)
  local copies, waits for them, and re-layouts  9.05 us (5%)
  other arithmetic  3.6 us (2%)
    ppermute x4, starting transfers between devices, from_near(): lax.ppermute(x, 'band', [(i, i ^ 1) for i in range(lax.axis_size('band'))])  24.3 us
    pallas_call x2, Pallas kernels, transport(): pl.pallas_call(functools.partial(transport_kernel, part), out_shape=(fina...  19.8 us
    pallas_call x1, Pallas kernels, per_device(): pl.pallas_call(gradient_kernel, out_shape=shape((padded, hid), F32), in_s...  16.6 us
    ppermute x4, starting transfers between devices, sum_over_devices(): total = total + lax.ppermute(piece(parts, at ^ m), 'band', perm)  15.8 us
    pallas_call x1, Pallas kernels, per_device(): pl.pallas_call(forward_kernel, out_shape=(*halos, wide, wide, *kept_shape...  13.9 us
    ppermute x2, starting transfers between devices, from_lon_neighbours(): lax.ppermute(first, 'lev', [((i + 1) % levs, i) for i in range(levs)])  8.93 us
    pallas_call x1, Pallas kernels, per_device(): pl.pallas_call(adjoint_kernel, out_shape=shape((tiles, LANES * rows, LANE...  8.67 us
    ppermute x2, waiting for transfers between devices, sum_over_devices(): x = x + lax.ppermute(x, 'lev', [(i, i ^ step) for i in range(lev)])  7.44 us
  transfers between devices with their start and end apart: 23, of which 11 were waited for; matrix products, arithmetic and copies ran while one was open for 1% of the time, Pallas kernels for 21%

profile of v1, /device:TPU:0, one launch (start us, length us, event | category | flops | bytes accessed | tf_op | source)
XLA Modules:
  0.0 167.9 jit_solution(17862900274319565229)
XLA Ops:
  0.6 1.6 copy.21.w3
  2.2 13.9 %forward.1 = (f32[6,2,264,128]{3,2,1,0:T(8,128)}, f32[6,264,128]{2,1,0:T(8,128)}, f32[6,256,128]{2,1,0:T(8,128)}, f32[8,2,16,128]{3,2,1,0:T(8,128)}, f32[8,2,16,...) custom-call(f32[2048,256]{1,0:T(8,128)} %bitcast.37, ...), custom_call_target="tpu_custom_call" | custom-call | flops 14000000 | bytes 42000000 | tf_op jit(solution)/shard_map/forward/pallas_call | solution.py:703
  16.1 5.1 %collective-permute-start.2 = (f32[8,2,16,128]{3,2,1,0:T(8,128)}, f32[8,2,16,128]{3,2,1,0:T(8,128)S(1)}, u32[]{:S(2)}, u32[]{:S(2)}) collective-permute-start(f32[8,2,16,128]{3,2,1,0:T(8,128)} %get-tuple-element.53), channel_id=1, source_target_pairs={{1,0},{2,1},{3,2},{0,3},{5,4},{6,5},{7,6},{4,7},{9,8},{10,9},{11,1... | collective-permute-start | bytes 393224 | tf_op jit(solution)/shard_map/ppermute | solution.py:621
  21.3 1.5 collective-permute-start.1
  22.8 2.0 %collective-permute-start = (f32[6,2,264,128]{3,2,1,0:T(8,128)}, f32[6,2,264,128]{3,2,1,0:T(8,128)S(1)}, u32[]{:S(2)}, u32[]{:S(2)}) collective-permute-start(f32[6,2,264,128]{3,2,1,0:T(8,128)} %get-tuple-element.50.refs_2_), channel_id=1, source_target_pairs={{0,4},{4,0},{8,12},{12,8},{16,20},{20,16},{24,28},{28,24},{1,5},{5... | collective-permute-start | bytes 4866056 | tf_op jit(solution)/shard_map/ppermute | solution.py:627
  24.8 1.5 bitcast_convert_fusion.source_hbm
  26.4 3.6 %turn.1 = (f32[8,2,256,128]{3,2,1,0:T(8,128)}, f32[8,2,8,128]{3,2,1,0:T(8,128)}, f32[8,2,8,128]{3,2,1,0:T(8,128)}) custom-call(f32[2048,256]{1,0:T(8,128)} %bitcast_convert_fusion.source_hbm), custom_call_target="tpu_custom_call" | custom-call | flops 4000000 | bytes 12000000 | tf_op jit(solution)/shard_map/turn/pallas_call | solution.py:726
  30.1 0.7 collective-permute-start.4
  30.8 2.9 %collective-permute-start.5 = (f32[2,6,2,16,128]{4,3,2,1,0:T(8,128)S(1)}, f32[2,6,2,16,128]{4,3,2,1,0:T(8,128)S(1)}, u32[]{:S(2)}, u32[]{:S(2)}) collective-permute-start(f32[2,6,2,16,128]{4,3,2,1,0:T(8,128)S(1)} %get-tuple-element.104), channel_id=1, source_target_pairs={{0,4},{4,0},{8,12},{12,8},{16,20},{20,16},{24,28},{28,24},{1,5},{5... | collective-permute-start | bytes 589832 | tf_op jit(solution)/shard_map/ppermute | solution.py:627
  33.7 3.8 %collective-permute-start.6 = (f32[8,2,8,128]{3,2,1,0:T(8,128)}, f32[8,2,8,128]{3,2,1,0:T(8,128)S(1)}, u32[]{:S(2)}, u32[]{:S(2)}) collective-permute-start(f32[8,2,8,128]{3,2,1,0:T(8,128)} %get-tuple-element.60), channel_id=1, source_target_pairs={{1,0},{2,1},{3,2},{0,3},{5,4},{6,5},{7,6},{4,7},{9,8},{10,9},{11,1... | collective-permute-start | bytes 196616 | tf_op jit(solution)/shard_map/ppermute | solution.py:621
  37.5 2.2 %collective-permute-done.6.refs_9_ = f32[8,2,8,128]{3,2,1,0:T(8,128)S(1)} collective-permute-done((f32[8,2,8,128]{3,2,1,0:T(8,128)}, f32[8,2,8,128]{3,2,1,0:T(8,128)S(1)}, u32[]{:S(2)}, u32[]{:S(2)}) %collective-permute-start.6) | collective-permute-done | bytes 65568 | tf_op jit(solution)/shard_map/ppermute | solution.py:621
  39.8 6.5 %collective-permute-done.7.refs_10_ = f32[8,2,8,128]{3,2,1,0:T(8,128)S(1)} collective-permute-done((f32[8,2,8,128]{3,2,1,0:T(8,128)}, f32[8,2,8,128]{3,2,1,0:T(8,128)S(1)}, u32[]{:S(2)}, u32[]{:S(2)}) %collective-permute-start.7) | collective-permute-done | bytes 65568 | tf_op jit(solution)/shard_map/ppermute | solution.py:622
  46.3 0.6 copy-done.13
  47.0 0.7 collective-permute-start.8
  47.8 0.8 broadcast_in_dim.2.refs_11_
  49.0 11.1 %transport0.1 = (f32[8,256,128]{2,1,0:T(8,128)}, f32[6,272,128]{2,1,0:T(8,128)}, f32[6,272,128]{2,1,0:T(8,128)}, f32[20,8,128]{2,1,0:T(8,128)}) custom-call(f32[6,2,264,128]{3,2,1,0:T(8,128)} %copy-done, f32[6,264,128]{2,1,0:T(8,128)} %collective-permute-done.1.refs_1_, f32[6,2,264,128]{3,2,1,0:T(8,128)} %get-tuple-element.50.refs_2_, ...), custom_call_target="tpu_custom_call" | custom-call | flops 13000000 | bytes 39000000 | tf_op jit(solution)/shard_map/transport0/pallas_call | solution.py:761
  60.1 0.7 collective-permute-start.9
  60.8 8.7 %collective-permute-start.12 = (f32[6,272,128]{2,1,0:T(8,128)}, f32[6,272,128]{2,1,0:T(8,128)S(1)}, u32[]{:S(2)}, u32[]{:S(2)}) collective-permute-start(f32[6,272,128]{2,1,0:T(8,128)} %get-tuple-element.82.own_near), channel_id=1, source_target_pairs={{0,4},{4,0},{8,12},{12,8},{16,20},{20,16},{24,28},{28,24},{1,5},{5... | collective-permute-start | bytes 2506760 | tf_op jit(solution)/shard_map/ppermute | solution.py:627
  69.5 8.7 %transport1.1 = (f32[8,256,128]{2,1,0:T(8,128)}, f32[6,272,128]{2,1,0:T(8,128)}, f32[6,272,128]{2,1,0:T(8,128)}) custom-call(f32[6,2,264,128]{3,2,1,0:T(8,128)} %copy-done, f32[6,256,128]{2,1,0:T(8,128)} %copy-done.9, f32[6,2,264,128]{3,2,1,0:T(8,128)} %get-tuple-element.50.refs_2_, f32[6,256,128]{2,1,0:T(8,128)} %get-tuple-element.70.refs_3_, ...), custom_call_target="tpu_custom_call" | custom-call | flops 13000000 | bytes 39000000 | tf_op jit(solution)/shard_map/transport1/pallas_call | solution.py:761
  78.2 0.9 collective-permute-start.10
  79.1 10.7 %collective-permute-start.11 = (f32[6,272,128]{2,1,0:T(8,128)}, f32[6,272,128]{2,1,0:T(8,128)S(1)}, u32[]{:S(2)}, u32[]{:S(2)}) collective-permute-start(f32[6,272,128]{2,1,0:T(8,128)} %get-tuple-element.80.own_near), channel_id=1, source_target_pairs={{0,4},{4,0},{8,12},{12,8},{16,20},{20,16},{24,28},{28,24},{1,5},{5... | collective-permute-start | bytes 2506760 | tf_op jit(solution)/shard_map/ppermute | solution.py:627
  89.8 3.6 %native.1 = f32[2048,256]{1,0:T(8,128)} custom-call(f32[8,256,128]{2,1,0:T(8,128)} %get-tuple-element.77.refs_0_, f32[8,256,128]{2,1,0:T(8,128)} %get-tuple-element.78.refs_1_), custom_call_target="tpu_custom_call" | custom-call | flops 4000000 | bytes 12000000 | tf_op jit(solution)/shard_map/native/pallas_call | solution.py:789
  93.4 0.9 copy-done.5
  94.4 8.7 %adjoint0.1.lower_h = f32[2,1024,128]{2,1,0:T(8,128)} custom-call(f32[6,272,128]{2,1,0:T(8,128)} %copy-done.5, f32[6,272,128]{2,1,0:T(8,128)} %copy-done.4, f32[6,272,128]{2,1,0:T(8,128)} %get-tuple-element.82.own_near, f32[6,272,128]{2,1,0:T(8,128)} %get-tuple-element.75.own_far, f32[20,8,128]{2,1,0:T(8,128)} %get-tuple-element.72.refs_12_.wind), custom_call_target="tpu_custom_call" | custom-call | flops 12000000 | bytes 36000000 | tf_op jit(solution)/shard_map/adjoint0/pallas_call | solution.py:800
  103.1 0.9 copy-done.6
  104.2 16.6 %gradient.1 = f32[768,256]{1,0:T(8,128)} custom-call(f32[6,272,128]{2,1,0:T(8,128)} %copy-done.7, f32[6,272,128]{2,1,0:T(8,128)} %copy-done.6, f32[6,272,128]{2,1,0:T(8,128)} %get-tuple-element.80.own_near, f32[6,272,128]{2,1,0:T(8,128)} %get-tuple-element.76.own_far, f32[20,8,128]{2,1,0:T(8,128)} %get-tuple-element.72.refs_12_.wind, f32[512,256]{1,0:T(8,128)} %bitcast.40, ...), custom_call_target="tpu_custom_call" | custom-call | flops 17000000 | bytes 51000000 | tf_op jit(solution)/shard_map/gradient/pallas_call | solution.py:815
  120.8 1.0 dynamic-slice_bitcast_fusion
  121.9 3.7 %collective-permute-start.13 = (f32[384,256]{1,0:T(8,128)S(1)}, f32[384,256]{1,0:T(8,128)S(1)}, u32[]{:S(2)}, u32[]{:S(2)}) collective-permute-start(f32[384,256]{1,0:T(8,128)S(1)} %dynamic-slice_bitcast_fusion), channel_id=1, source_target_pairs={{0,4},{4,0},{8,12},{12,8},{16,20},{20,16},{24,28},{28,24},{1,5},{5... | collective-permute-start | bytes 1179656 | tf_op jit(solution)/shard_map/ppermute | solution.py:595
  125.6 1.3 collective-permute-done.13
  126.9 1.0 bitcast_add_fusion
  128.0 8.7 %collective-permute-start.14 = (f32[96,256]{1,0:T(8,128)S(1)}, f32[96,256]{1,0:T(8,128)S(1)}, u32[]{:S(2)}, u32[]{:S(2)}) collective-permute-start(f32[96,256]{1,0:T(8,128)S(1)} %get-tuple-element.101), channel_id=1, source_target_pairs={{0,24},{4,28},{8,16},{12,20},{16,8},{20,12},{24,0},{28,4},{1,25},{... | collective-permute-start | bytes 294920 | tf_op jit(solution)/shard_map/ppermute | solution.py:595
  136.7 3.4 %collective-permute-start.15 = (f32[96,256]{1,0:T(8,128)S(1)}, f32[96,256]{1,0:T(8,128)S(1)}, u32[]{:S(2)}, u32[]{:S(2)}) collective-permute-start(f32[96,256]{1,0:T(8,128)S(1)} %get-tuple-element.103), channel_id=1, source_target_pairs={{0,16},{4,20},{8,24},{12,28},{16,0},{20,4},{24,8},{28,12},{1,17},{... | collective-permute-start | bytes 294920 | tf_op jit(solution)/shard_map/ppermute | solution.py:595
  140.1 3.0 %collective-permute-done.15 = f32[96,256]{1,0:T(8,128)S(1)} collective-permute-done((f32[96,256]{1,0:T(8,128)S(1)}, f32[96,256]{1,0:T(8,128)S(1)}, u32[]{:S(2)}, u32[]{:S(2)}) %collective-permute-start.15) | collective-permute-done | bytes 98336 | tf_op jit(solution)/shard_map/ppermute | solution.py:595
  143.1 1.6 collective-permute-done.16
  144.9 4.5 %collective-permute-done.17 = f32[96,256]{1,0:T(8,128)S(1)} collective-permute-done((f32[96,256]{1,0:T(8,128)S(1)}, f32[96,256]{1,0:T(8,128)S(1)}, u32[]{:S(2)}, u32[]{:S(2)}) %collective-permute-start.17) | collective-permute-done | bytes 98336 | tf_op jit(solution)/shard_map/ppermute | solution.py:602
  149.4 2.7 %collective-permute-start.18 = (f32[96,256]{1,0:T(8,128)S(1)}, f32[96,256]{1,0:T(8,128)S(1)}, u32[]{:S(2)}, u32[]{:S(2)}) collective-permute-start(f32[96,256]{1,0:T(8,128)S(1)} %add.81), channel_id=1, source_target_pairs={{0,2},{1,3},{2,0},{3,1},{4,6},{5,7},{6,4},{7,5},{8,10},{9,11},{10,... | collective-permute-start | bytes 294920 | tf_op jit(solution)/shard_map/ppermute | solution.py:602
  152.1 2.9 %collective-permute-done.18 = f32[96,256]{1,0:T(8,128)S(1)} collective-permute-done((f32[96,256]{1,0:T(8,128)S(1)}, f32[96,256]{1,0:T(8,128)S(1)}, u32[]{:S(2)}, u32[]{:S(2)}) %collective-permute-start.18) | collective-permute-done | bytes 98336 | tf_op jit(solution)/shard_map/ppermute | solution.py:602
  155.0 2.1 %collective-permute-start.19 = (f32[96,256]{1,0:T(8,128)S(1)}, f32[96,256]{1,0:T(8,128)S(1)}, u32[]{:S(2)}, u32[]{:S(2)}) collective-permute-start(f32[96,256]{1,0:T(8,128)S(1)} %add.82), channel_id=1, source_target_pairs={{0,24},{4,28},{8,16},{12,20},{16,8},{20,12},{24,0},{28,4},{1,25},{... | collective-permute-start | bytes 294920 | tf_op jit(solution)/shard_map/ppermute | solution.py:606
  157.1 0.6 collective-permute-start.20
  157.7 1.4 collective-permute-start.21
  159.1 2.2 %collective-permute-done.19 = f32[96,256]{1,0:T(8,128)S(1)} collective-permute-done((f32[96,256]{1,0:T(8,128)S(1)}, f32[96,256]{1,0:T(8,128)S(1)}, u32[]{:S(2)}, u32[]{:S(2)}) %collective-permute-start.19) | collective-permute-done | bytes 98336 | tf_op jit(solution)/shard_map/ppermute | solution.py:606
  161.4 0.9 collective-permute-done.20
  162.2 0.6 collective-permute-done.21
  163.0 1.7 %collective-permute-done.22 = f32[384,256]{1,0:T(8,128)S(1)} collective-permute-done((f32[384,256]{1,0:T(8,128)S(1)}, f32[384,256]{1,0:T(8,128)S(1)}, u32[]{:S(2)}, u32[]{:S(2)}) %collective-permute-start.22) | collective-permute-done | bytes 393248 | tf_op jit(solution)/shard_map/ppermute | solution.py:606
  164.7 0.8 broadcast_select_fusion
  165.5 0.7 slice.21
  166.2 0.6 slice_bitcast_fusion
  166.8 0.6 fusion.4
  (51 shorter events, 1.8 us)
Async XLA Ops:
  0.6 24.2 %copy-start.3 = (bf16[64,4,8,256]{3,2,1,0:T(8,128)(2,1)S(1)}, bf16[64,4,8,256]{3,2,1,0:T(8,128)(2,1)}, u32[]{:S(2)}) copy-start(bf16[64,4,8,256]{3,2,1,0:T(8,128)(2,1)} %param.15) | copy-start | bytes 3145732
  16.1 13.9 %collective-permute-start.2 = (f32[8,2,16,128]{3,2,1,0:T(8,128)}, f32[8,2,16,128]{3,2,1,0:T(8,128)S(1)}, u32[]{:S(2)}, u32[]{:S(2)}) collective-permute-start(f32[8,2,16,128]{3,2,1,0:T(8,128)} %get-tuple-element.53), channel_id=1, source_target_pairs={{1,0},{2,1},{3,2},{0,3},{5,4},{6,5},{7,6},{4,7},{9,8},{10,9},{11,1... | collective-permute-start | bytes 393224 | tf_op jit(solution)/shard_map/ppermute | solution.py:621
  21.2 8.8 %collective-permute-start.3 = (f32[8,2,16,128]{3,2,1,0:T(8,128)}, f32[8,2,16,128]{3,2,1,0:T(8,128)S(1)}, u32[]{:S(2)}, u32[]{:S(2)}) collective-permute-start(f32[8,2,16,128]{3,2,1,0:T(8,128)} %get-tuple-element.54), channel_id=1, source_target_pairs={{0,1},{1,2},{2,3},{3,0},{4,5},{5,6},{6,7},{7,4},{8,9},{9,10},{10,1... | collective-permute-start | bytes 393224 | tf_op jit(solution)/shard_map/ppermute | solution.py:622
  21.3 25.0 %collective-permute-start.1 = (f32[6,264,128]{2,1,0:T(8,128)}, f32[6,264,128]{2,1,0:T(8,128)}, u32[]{:S(2)}, u32[]{:S(2)}) collective-permute-start(f32[6,264,128]{2,1,0:T(8,128)} %get-tuple-element.52.refs_3_), channel_id=1, source_target_pairs={{4,8},{12,16},{20,24},{8,4},{16,12},{24,20},{5,9},{13,17},{21,25},... | collective-permute-start | bytes 2433032 | tf_op jit(solution)/shard_map/ppermute | solution.py:633
  22.8 25.0 %collective-permute-start = (f32[6,2,264,128]{3,2,1,0:T(8,128)}, f32[6,2,264,128]{3,2,1,0:T(8,128)S(1)}, u32[]{:S(2)}, u32[]{:S(2)}) collective-permute-start(f32[6,2,264,128]{3,2,1,0:T(8,128)} %get-tuple-element.50.refs_2_), channel_id=1, source_target_pairs={{0,4},{4,0},{8,12},{12,8},{16,20},{20,16},{24,28},{28,24},{1,5},{5... | collective-permute-start | bytes 4866056 | tf_op jit(solution)/shard_map/ppermute | solution.py:627
  26.4 20.7 %copy-start.8 = (f32[6,256,128]{2,1,0:T(8,128)S(1)}, f32[6,256,128]{2,1,0:T(8,128)}, u32[]{:S(2)}) copy-start(f32[6,256,128]{2,1,0:T(8,128)} %get-tuple-element.70.refs_3_) | copy-start | bytes 2359300
  30.0 18.5 %copy-start.1 = (f32[8,2,16,128]{3,2,1,0:T(8,128)}, f32[8,2,16,128]{3,2,1,0:T(8,128)S(1)}, u32[]{:S(2)}) copy-start(f32[8,2,16,128]{3,2,1,0:T(8,128)S(1)} %collective-permute-done.2.refs_4_) | copy-start | bytes 393220
  30.1 18.5 %copy-start.2 = (f32[8,2,16,128]{3,2,1,0:T(8,128)}, f32[8,2,16,128]{3,2,1,0:T(8,128)S(1)}, u32[]{:S(2)}) copy-start(f32[8,2,16,128]{3,2,1,0:T(8,128)S(1)} %collective-permute-done.3.refs_5_) | copy-start | bytes 393220
  30.1 16.1 %collective-permute-start.4 = (f32[2,6,2,16,128]{4,3,2,1,0:T(8,128)S(1)}, f32[2,6,2,16,128]{4,3,2,1,0:T(8,128)S(1)}, u32[]{:S(2)}, u32[]{:S(2)}) collective-permute-start(f32[2,6,2,16,128]{4,3,2,1,0:T(8,128)S(1)} %get-tuple-element.105), channel_id=1, source_target_pairs={{4,8},{12,16},{20,24},{8,4},{16,12},{24,20},{5,9},{13,17},{21,25},... | collective-permute-start | bytes 589832 | tf_op jit(solution)/shard_map/ppermute | solution.py:633
  30.8 15.5 %collective-permute-start.5 = (f32[2,6,2,16,128]{4,3,2,1,0:T(8,128)S(1)}, f32[2,6,2,16,128]{4,3,2,1,0:T(8,128)S(1)}, u32[]{:S(2)}, u32[]{:S(2)}) collective-permute-start(f32[2,6,2,16,128]{4,3,2,1,0:T(8,128)S(1)} %get-tuple-element.104), channel_id=1, source_target_pairs={{0,4},{4,0},{8,12},{12,8},{16,20},{20,16},{24,28},{28,24},{1,5},{5... | collective-permute-start | bytes 589832 | tf_op jit(solution)/shard_map/ppermute | solution.py:627
  33.7 6.0 %collective-permute-start.6 = (f32[8,2,8,128]{3,2,1,0:T(8,128)}, f32[8,2,8,128]{3,2,1,0:T(8,128)S(1)}, u32[]{:S(2)}, u32[]{:S(2)}) collective-permute-start(f32[8,2,8,128]{3,2,1,0:T(8,128)} %get-tuple-element.60), channel_id=1, source_target_pairs={{1,0},{2,1},{3,2},{0,3},{5,4},{6,5},{7,6},{4,7},{9,8},{10,9},{11,1... | collective-permute-start | bytes 196616 | tf_op jit(solution)/shard_map/ppermute | solution.py:621
  39.8 8.8 %copy-start.12 = (f32[8,2,8,128]{3,2,1,0:T(8,128)}, f32[8,2,8,128]{3,2,1,0:T(8,128)S(1)}, u32[]{:S(2)}) copy-start(f32[8,2,8,128]{3,2,1,0:T(8,128)S(1)} %collective-permute-done.6.refs_9_) | copy-start | bytes 196612
  39.8 6.5 %collective-permute-start.7 = (f32[8,2,8,128]{3,2,1,0:T(8,128)}, f32[8,2,8,128]{3,2,1,0:T(8,128)S(1)}, u32[]{:S(2)}, u32[]{:S(2)}) collective-permute-start(f32[8,2,8,128]{3,2,1,0:T(8,128)} %get-tuple-element.61), channel_id=1, source_target_pairs={{0,1},{1,2},{2,3},{3,0},{4,5},{5,6},{6,7},{7,4},{8,9},{9,10},{10,1... | collective-permute-start | bytes 196616 | tf_op jit(solution)/shard_map/ppermute | solution.py:622
  46.3 0.6 copy-start.13
  46.3 0.7 copy-start.10
  46.3 0.7 copy-start.11
  47.0 13.0 %collective-permute-start.8 = (f32[6,256,128]{2,1,0:T(8,128)S(1)}, f32[6,256,128]{2,1,0:T(8,128)S(1)}, u32[]{:S(2)}, u32[]{:S(2)}) collective-permute-start(f32[6,256,128]{2,1,0:T(8,128)S(1)} %copy-done.8), channel_id=1, source_target_pairs={{4,8},{12,16},{20,24},{8,4},{16,12},{24,20},{5,9},{13,17},{21,25},... | collective-permute-start | bytes 2359304 | tf_op jit(solution)/shard_map/ppermute | solution.py:633
  47.8 1.2 copy-start
  60.1 9.4 %copy-start.9 = (f32[6,256,128]{2,1,0:T(8,128)}, f32[6,256,128]{2,1,0:T(8,128)S(1)}, u32[]{:S(2)}) copy-start(f32[6,256,128]{2,1,0:T(8,128)S(1)} %collective-permute-done.8.refs_1_) | copy-start | bytes 2359300
  60.1 18.1 %collective-permute-start.9 = (f32[6,272,128]{2,1,0:T(8,128)}, f32[6,272,128]{2,1,0:T(8,128)S(1)}, u32[]{:S(2)}, u32[]{:S(2)}) collective-permute-start(f32[6,272,128]{2,1,0:T(8,128)} %get-tuple-element.75.own_far), channel_id=1, source_target_pairs={{4,8},{12,16},{20,24},{8,4},{16,12},{24,20},{5,9},{13,17},{21,25},... | collective-permute-start | bytes 2506760 | tf_op jit(solution)/shard_map/ppermute | solution.py:633
  60.8 32.6 %collective-permute-start.12 = (f32[6,272,128]{2,1,0:T(8,128)}, f32[6,272,128]{2,1,0:T(8,128)S(1)}, u32[]{:S(2)}, u32[]{:S(2)}) collective-permute-start(f32[6,272,128]{2,1,0:T(8,128)} %get-tuple-element.82.own_near), channel_id=1, source_target_pairs={{0,4},{4,0},{8,12},{12,8},{16,20},{20,16},{24,28},{28,24},{1,5},{5... | collective-permute-start | bytes 2506760 | tf_op jit(solution)/shard_map/ppermute | solution.py:627
  78.2 15.2 %copy-start.4 = (f32[6,272,128]{2,1,0:T(8,128)}, f32[6,272,128]{2,1,0:T(8,128)S(1)}, u32[]{:S(2)}) copy-start(f32[6,272,128]{2,1,0:T(8,128)S(1)} %collective-permute-done.9.far) | copy-start | bytes 2506756
  78.2 24.8 %collective-permute-start.10 = (f32[6,272,128]{2,1,0:T(8,128)}, f32[6,272,128]{2,1,0:T(8,128)S(1)}, u32[]{:S(2)}, u32[]{:S(2)}) collective-permute-start(f32[6,272,128]{2,1,0:T(8,128)} %get-tuple-element.76.own_far), channel_id=1, source_target_pairs={{4,8},{12,16},{20,24},{8,4},{16,12},{24,20},{5,9},{13,17},{21,25},... | collective-permute-start | bytes 2506760 | tf_op jit(solution)/shard_map/ppermute | solution.py:633
  79.1 23.9 %collective-permute-start.11 = (f32[6,272,128]{2,1,0:T(8,128)}, f32[6,272,128]{2,1,0:T(8,128)S(1)}, u32[]{:S(2)}, u32[]{:S(2)}) collective-permute-start(f32[6,272,128]{2,1,0:T(8,128)} %get-tuple-element.80.own_near), channel_id=1, source_target_pairs={{0,4},{4,0},{8,12},{12,8},{16,20},{20,16},{24,28},{28,24},{1,5},{5... | collective-permute-start | bytes 2506760 | tf_op jit(solution)/shard_map/ppermute | solution.py:627
  93.4 0.9 copy-start.5
  103.1 0.9 copy-start.6
  103.1 1.2 copy-start.7
  121.9 5.0 %collective-permute-start.13 = (f32[384,256]{1,0:T(8,128)S(1)}, f32[384,256]{1,0:T(8,128)S(1)}, u32[]{:S(2)}, u32[]{:S(2)}) collective-permute-start(f32[384,256]{1,0:T(8,128)S(1)} %dynamic-slice_bitcast_fusion), channel_id=1, source_target_pairs={{0,4},{4,0},{8,12},{12,8},{16,20},{20,16},{24,28},{28,24},{1,5},{5... | collective-permute-start | bytes 1179656 | tf_op jit(solution)/shard_map/ppermute | solution.py:595
  128.0 12.1 %collective-permute-start.14 = (f32[96,256]{1,0:T(8,128)S(1)}, f32[96,256]{1,0:T(8,128)S(1)}, u32[]{:S(2)}, u32[]{:S(2)}) collective-permute-start(f32[96,256]{1,0:T(8,128)S(1)} %get-tuple-element.101), channel_id=1, source_target_pairs={{0,24},{4,28},{8,16},{12,20},{16,8},{20,12},{24,0},{28,4},{1,25},{... | collective-permute-start | bytes 294920 | tf_op jit(solution)/shard_map/ppermute | solution.py:595
  136.7 6.4 %collective-permute-start.15 = (f32[96,256]{1,0:T(8,128)S(1)}, f32[96,256]{1,0:T(8,128)S(1)}, u32[]{:S(2)}, u32[]{:S(2)}) collective-permute-start(f32[96,256]{1,0:T(8,128)S(1)} %get-tuple-element.103), channel_id=1, source_target_pairs={{0,16},{4,20},{8,24},{12,28},{16,0},{20,4},{24,8},{28,12},{1,17},{... | collective-permute-start | bytes 294920 | tf_op jit(solution)/shard_map/ppermute | solution.py:595
  140.1 4.6 %collective-permute-start.16 = (f32[96,256]{1,0:T(8,128)S(1)}, f32[96,256]{1,0:T(8,128)S(1)}, u32[]{:S(2)}, u32[]{:S(2)}) collective-permute-start(f32[96,256]{1,0:T(8,128)S(1)} %get-tuple-element.102), channel_id=1, source_target_pairs={{0,8},{4,12},{8,0},{12,4},{16,24},{20,28},{24,16},{28,20},{1,9},{5... | collective-permute-start | bytes 294920 | tf_op jit(solution)/shard_map/ppermute | solution.py:595
  144.8 4.7 %collective-permute-start.17 = (f32[96,256]{1,0:T(8,128)S(1)}, f32[96,256]{1,0:T(8,128)S(1)}, u32[]{:S(2)}, u32[]{:S(2)}) collective-permute-start(f32[96,256]{1,0:T(8,128)S(1)} %fusion.3), channel_id=1, source_target_pairs={{0,1},{1,0},{2,3},{3,2},{4,5},{5,4},{6,7},{7,6},{8,9},{9,8},{10,11... | collective-permute-start | bytes 294920 | tf_op jit(solution)/shard_map/ppermute | solution.py:602
  149.4 5.6 %collective-permute-start.18 = (f32[96,256]{1,0:T(8,128)S(1)}, f32[96,256]{1,0:T(8,128)S(1)}, u32[]{:S(2)}, u32[]{:S(2)}) collective-permute-start(f32[96,256]{1,0:T(8,128)S(1)} %add.81), channel_id=1, source_target_pairs={{0,2},{1,3},{2,0},{3,1},{4,6},{5,7},{6,4},{7,5},{8,10},{9,11},{10,... | collective-permute-start | bytes 294920 | tf_op jit(solution)/shard_map/ppermute | solution.py:602
  155.0 6.3 %collective-permute-start.19 = (f32[96,256]{1,0:T(8,128)S(1)}, f32[96,256]{1,0:T(8,128)S(1)}, u32[]{:S(2)}, u32[]{:S(2)}) collective-permute-start(f32[96,256]{1,0:T(8,128)S(1)} %add.82), channel_id=1, source_target_pairs={{0,24},{4,28},{8,16},{12,20},{16,8},{20,12},{24,0},{28,4},{1,25},{... | collective-permute-start | bytes 294920 | tf_op jit(solution)/shard_map/ppermute | solution.py:606
  157.1 5.1 %collective-permute-start.20 = (f32[96,256]{1,0:T(8,128)S(1)}, f32[96,256]{1,0:T(8,128)S(1)}, u32[]{:S(2)}, u32[]{:S(2)}) collective-permute-start(f32[96,256]{1,0:T(8,128)S(1)} %add.82), channel_id=1, source_target_pairs={{0,16},{4,20},{8,24},{12,28},{16,0},{20,4},{24,8},{28,12},{1,17},{... | collective-permute-start | bytes 294920 | tf_op jit(solution)/shard_map/ppermute | solution.py:606
  157.7 5.1 %collective-permute-start.21 = (f32[96,256]{1,0:T(8,128)S(1)}, f32[96,256]{1,0:T(8,128)S(1)}, u32[]{:S(2)}, u32[]{:S(2)}) collective-permute-start(f32[96,256]{1,0:T(8,128)S(1)} %add.82), channel_id=1, source_target_pairs={{0,8},{4,12},{8,0},{12,4},{16,24},{20,28},{24,16},{28,20},{1,9},{5... | collective-permute-start | bytes 294920 | tf_op jit(solution)/shard_map/ppermute | solution.py:606
  162.9 1.8 %collective-permute-start.22 = (f32[384,256]{1,0:T(8,128)S(1)}, f32[384,256]{1,0:T(8,128)S(1)}, u32[]{:S(2)}, u32[]{:S(2)}) collective-permute-start(f32[384,256]{1,0:T(8,128)S(1)} %pad_maximum_fusion), channel_id=1, source_target_pairs={{0,4},{4,0},{8,12},{12,8},{16,20},{20,16},{24,28},{28,24},{1,5},{5... | collective-permute-start | bytes 1179656 | tf_op jit(solution)/shard_map/ppermute | solution.py:606

commit v2 on v1

--- a/solution.py
+++ b/solution.py
@@ -18,11 +18,10 @@
 LANES = 128
 SIDE = 8
 WIDE = 16
-VMEM_LIMIT = 56 * 1024 * 1024
-
-
-def params():
-    return pltpu.CompilerParams(vmem_limit_bytes=VMEM_LIMIT)
+
+
+def params(mebibytes):
+    return pltpu.CompilerParams(vmem_limit_bytes=mebibytes << 20)
 
 
 def cost(microseconds):
@@ -98,7 +97,7 @@
     pre2 = add_column(dot(w2[...], act1, ((0,), (0,))), c2)
     sig2 = sigmoid(pre2)
     act2 = (pre2 * sig2).astype(BF16)
-    raw = add_column(dot(w3[...], act2, ((0,), (0,))), c3)
+    raw = add_column(dot(w3[...], act2, ((1,), (0,))), c3)
     return inputs, pre1, sig1, act1, pre2, sig2, act2, raw
 
 
@@ -118,7 +117,7 @@
             inv = 1.0 / (excess + upper[t])
             ratio = upper[t] * inv
             half = (conc[t, at, :] + lower[t] * halves[n]) * inv
-            new_rests.append(ratio * excess)
+            new_rests.append((upper[t] * excess) * inv)
             new_halves.append(half)
             invs.append(inv)
             ratios.append(ratio)
@@ -438,13 +437,15 @@
     wait_copies(results)
 
 
-def adjoint_steps(part, near, far, own_near, own_far, wind, ext, a, b, along, across, centre, turned_wind, adjoint, sem):
+def adjoint_steps(part, near, far, own_near, own_far, wind, ext, a, b, along, across, centre, turned_wind, adjoint, sem, others=(), other_sem=None):
     every = slice(None)
     copies = start_copies(row_pairs(ext, near, far, own_near, own_far, every, every), sem)
+    others = start_copies(others, other_sem)
     fill_coefficients(wind, turned_wind, along, across, centre, WIDE - SIDE)
     wait_copies(copies)
     run_steps(ext, a, b, along, across, centre, True)
     turn_back(ext, STEPS, SIDE, adjoint, part * LANES * 8)
+    wait_copies(others)
 
 
 def adjoint_kernel(near, far, own_near, own_far, wind, adjoint, ext, a, b, along, across, centre, turned_wind, sem):
@@ -489,23 +490,20 @@
 def gradient_kernel(
     near, far, own_near, own_far, wind, eddy, w2, w3, lower_h,
     settled_h, inverse_h, ratio_h, rate_h, inputs_h, act1_h, slope1_h, act2_h, slope2_h,
-    out,
+    mine, theirs,
     ext, a, b, along, across, centre, turned_wind, adjoint, half, raw_grad,
-    settled, inverse, ratio, rate, inputs, act1, slope1, act2, slope2, sem, kept_sem,
+    settled, inverse, ratio, rate, inputs, act1, slope1, act2, slope2, total, sem, kept_sem,
 ):
     done = lower_h.shape[1]
-    kept = start_copies(
-        [
-            (lower_h, adjoint.at[:, pl.ds(0, done), :]),
-            (settled_h, settled), (inverse_h, inverse), (ratio_h, ratio), (rate_h, rate),
-            (inputs_h, inputs), (act1_h, act1), (slope1_h, slope1), (act2_h, act2), (slope2_h, slope2),
-        ],
-        kept_sem,
-    )
+    kept = [
+        (lower_h, adjoint.at[:, pl.ds(0, done), :]),
+        (settled_h, settled), (inverse_h, inverse), (ratio_h, ratio), (rate_h, rate),
+        (inputs_h, inputs), (act1_h, act1), (slope1_h, slope1), (act2_h, act2), (slope2_h, slope2),
+    ]
     adjoint_steps(
-        1, near, far, own_near, own_far, wind, ext, a, b, along, across, centre, turned_wind, adjoint, sem
-    )
-    wait_copies(kept)
+        1, near, far, own_near, own_far, wind, ext, a, b, along, across, centre, turned_wind, adjoint, sem,
+        kept, kept_sem,
+    )
     levels = eddy.shape[0] // 8
     bins = adjoint.shape[1] // eddy.shape[0]
     width = eddy.shape[1]
@@ -552,7 +550,7 @@
         half3 = grad3.astype(BF16)
         s3 = s3 + grad3
         g3 = g3 + dot(half3, act2[r], ((1,), (1,)))
-        grad2 = dot(w3[...], half3, ((1,), (0,))) * slope2[r]
+        grad2 = dot(w3[...], half3, ((0,), (0,))) * slope2[r]
         half2 = grad2.astype(BF16)
         s2 = s2 + grad2
         g2 = g2 + dot(act1[r], half2, ((1,), (1,)))
@@ -560,33 +558,36 @@
         half1 = grad1.astype(BF16)
         s1 = s1 + grad1
         g1 = g1 + dot(inputs[r], half1, ((1,), (1,)))
-    out[:fin, :] = g1
-    out[fin : fin + hid, :] = g2
+    total[:fin, :] = g1
+    total[fin : fin + hid, :] = g2
     at = fin + hid
-    out[at : at + levels, :] = g3
+    total[at : at + levels, :] = g3
     at += levels
-    rows1 = jnp.sum(s1.T, axis=0, keepdims=True)
-    rows2 = jnp.sum(s2.T, axis=0, keepdims=True)
     rows3 = jnp.sum(s3.T, axis=0, keepdims=True)
     rows3 = jnp.concatenate([rows3, jnp.zeros((1, hid - levels), F32)], axis=1)
-    out[at:, :] = jnp.zeros((out.shape[0] - at, hid), F32)
-    out[at : at + 1, :] = rows1
-    out[at + 1 : at + 2, :] = rows2
-    out[at + 2 : at + 3, :] = rows3
+    total[at:, :] = jnp.zeros((total.shape[0] - at, hid), F32)
+    total[at : at + 1, :] = jnp.sum(s1.T, axis=0, keepdims=True)
+    total[at + 1 : at + 2, :] = jnp.sum(s2.T, axis=0, keepdims=True)
+    total[at + 2 : at + 3, :] = rows3
+    many = mine.shape[0]
+    own = pl.ds(jnp.where(even_band(), 0, many), many)
+    other = pl.ds(jnp.where(even_band(), many, 0), many)
+    wait_copies(start_copies([(total.at[own, :], mine), (total.at[other, :], theirs)], sem))
 
 
 def piece(parts, index):
     return lax.dynamic_index_in_dim(parts, index, 0, False)
 
 
-def sum_over_devices(x):
+def sum_over_devices(x, theirs):
     size = lax.axis_size("band")
     index = lax.axis_index("band")
     columns = x.shape[1]
-    rounds = []
-    step = 1
+    x = x + from_near(theirs)
+    rounds = [(1, 2, index % 2)]
+    step = 2
     while step < size:
-        radix = 2 if step == 1 or size // step % 4 else 4
+        radix = 2 if size // step % 4 else 4
         at = (index // step) % radix
         parts = x.reshape(radix, -1, columns)
         total = piece(parts, at)
@@ -659,7 +660,7 @@
     eddy = eddy_diffusion.reshape(levels * rows, width)
     closure = (
         land_mask, surface_class, class_embed, weight_first, bias_first.reshape(1, -1),
-        weight_second, bias_second.reshape(1, -1), weight_third, bias_third.reshape(1, -1),
+        weight_second, bias_second.reshape(1, -1), weight_third.T, bias_third.reshape(1, -1),
     )
     tiles = width // LANES
     flat = shape((tiles, planes * rows, LANES), F32)
@@ -704,7 +705,7 @@
         forward_kernel,
         out_shape=(*halos, wide, wide, *kept_shapes),
         in_specs=[any_space] + specs(12),
-        out_specs=tuple([any_space] * 3 + specs(2) + [any_space] * 9),
+        out_specs=tuple(specs(5) + [any_space] * 9),
         scratch_shapes=[
             tiled, tiled_levels, pltpu.VMEM((rows, *halos[0].shape[1:]), F32), *kept_scratch,
             pltpu.SemaphoreType.DMA((tiles,)),
@@ -712,7 +713,7 @@
             pltpu.SemaphoreType.DMA((4,)),
             pltpu.SemaphoreType.DMA((3,)),
         ],
-        compiler_params=params(),
+        compiler_params=params(58),
         cost_estimate=cost(14),
         name="forward",
     )(conc, eddy, *closure, wind_zonal, wind_meridional)
@@ -729,12 +730,17 @@
         in_specs=[any_space],
         out_specs=tuple(specs(3)),
         scratch_shapes=[tiled, pltpu.SemaphoreType.DMA((tiles,))],
-        compiler_params=params(),
+        compiler_params=params(12),
         cost_estimate=cost(4),
         name="turn",
     )(observed_flat)
-    e, w, observed_first, observed_last = lax.optimization_barrier(
-        (e, w, observed_first, observed_last)
+    total_rows = rows * lax.axis_size("band")
+    row_ids = lax.axis_index("band") * rows + jnp.arange(rows, dtype=jnp.int32)
+    latitude = LATITUDE_EDGE * (row_ids.astype(F32) + 0.5) / total_rows
+    area = jnp.cos(latitude) / (bins * total_rows * lon_total)
+    area = jnp.broadcast_to(area[:, None], (rows, LANES))
+    e, w, observed_first, observed_last, area = lax.optimization_barrier(
+        (e, w, observed_first, observed_last, area)
     )
     near_row, far_row = first_rows()
     sides = jnp.stack([e, w])
@@ -748,12 +754,6 @@
     )
     got_far0, far_edge, near_edge, observed_e, observed_w = came
     got_far1 = from_far(far1)
-    total_rows = rows * lax.axis_size("band")
-    row_ids = lax.axis_index("band") * rows + jnp.arange(rows, dtype=jnp.int32)
-    latitude = LATITUDE_EDGE * (row_ids.astype(F32) + 0.5) / total_rows
-    area = jnp.cos(latitude) / (bins * total_rows * lon_total)
-    area = jnp.broadcast_to(area[:, None], (rows, LANES))
-
     wind_shape = shape((n_rows, 8, LANES), F32)
     final_shape = shape((rows, width, LANES), F32)
 
@@ -761,8 +761,8 @@
         return pl.pallas_call(
             functools.partial(transport_kernel, part),
             out_shape=(final_shape, m_halo, m_halo) + ((wind_shape,) if part == 0 else ()),
-            in_specs=[any_space] * 11 + specs(1 + len(winds)),
-            out_specs=tuple([any_space] * 3 + specs(0 if winds else 1)),
+            in_specs=specs(8) + [any_space] + specs(3 + len(winds)),
+            out_specs=tuple([any_space] + specs(2 if winds else 3)),
             scratch_shapes=stepping(width + 2 * WIDE) + [
                 pltpu.VMEM((rows, width + 2 * SIDE, LANES), F32),
                 pltpu.VMEM((rows, width + 2 * SIDE, LANES), F32),
@@ -771,7 +771,7 @@
                 pltpu.SemaphoreType.DMA((3,)),
                 pltpu.SemaphoreType.DMA((3,)),
             ],
-            compiler_params=params(),
+            compiler_params=params(30),
             cost_estimate=cost(13),
             name=f"transport{part}",
         )(
@@ -792,7 +792,7 @@
         in_specs=specs(2),
         out_specs=any_space,
         scratch_shapes=[tiled, pltpu.SemaphoreType.DMA((tiles,))],
-        compiler_params=params(),
+        compiler_params=params(10),
         cost_estimate=cost(4),
         name="native",
     )(final0, final1)
@@ -800,10 +800,10 @@
     adjoint0 = pl.pallas_call(
         adjoint_kernel,
         out_shape=shape((tiles, LANES * rows, LANES), F32),
-        in_specs=[any_space] * 4 + specs(1),
+        in_specs=specs(5),
         out_specs=specs(1)[0],
         scratch_shapes=stepping(width + 2 * SIDE) + [pltpu.SemaphoreType.DMA((4,))],
-        compiler_params=params(),
+        compiler_params=params(30),
         cost_estimate=cost(12),
         name="adjoint0",
     )(gm_near0, gm_far0, m_near0, m_far0, wind)
@@ -812,21 +812,22 @@
     bands = lax.axis_size("band")
     used = fin + hid + levels + 3
     padded = -(-used // (8 * bands)) * (8 * bands)
-    grads = pl.pallas_call(
+    mine, theirs = pl.pallas_call(
         gradient_kernel,
-        out_shape=shape((padded, hid), F32),
-        in_specs=[any_space] * 4 + specs(4) + [any_space] * 10,
-        out_specs=specs(1)[0],
+        out_shape=(shape((padded // 2, hid), F32),) * 2,
+        in_specs=specs(8) + [any_space] * 10,
+        out_specs=(any_space, any_space),
         scratch_shapes=stepping(width + 2 * SIDE) + [tiled, tiled, tiled_levels, *kept_scratch]
+        + [pltpu.VMEM((padded, hid), F32)]
         + [pltpu.SemaphoreType.DMA((4,)), pltpu.SemaphoreType.DMA((10,))],
-        compiler_params=params(),
+        compiler_params=params(50),
         cost_estimate=cost(17),
         name="gradient",
     )(
-        gm_near1, gm_far1, m_near1, m_far1, wind, eddy, weight_second, weight_third, adjoint0,
+        gm_near1, gm_far1, m_near1, m_far1, wind, eddy, weight_second, weight_third.T, adjoint0,
         *kept,
     )
-    grads = sum_over_devices(grads)
+    grads = sum_over_devices(mine, theirs)
     at = fin + hid + levels
     return (
         final.reshape(levels, bins, rows, width),

time: 168 us -> 159 us (0.946)
  Pallas kernels: 66.2 us -> 54.5 us
  starting transfers between devices: 60.5 us -> 70 us
  local copies, waits for them, and re-layouts: 9.05 us -> 3.59 us
  other arithmetic: 3.6 us -> 1.27 us
    ppermute x4 -> x5, starting transfers between devices: 24.3 us -> 38.3 us  [from_near(): lax.ppermute(x, 'band', [(i, i ^ 1) for i in range(lax.axis_size('band'))])]
    unnamed x29 -> x22, local copies, waits for them, and re-layouts: 4.8 us -> 1.05 us
    ppermute x4 -> x3, starting transfers between devices: 15.8 us -> 12.1 us  [sum_over_devices(): total = total + lax.ppermute(piece(parts, at ^ m), 'band', perm)]
    pallas_call x1, Pallas kernels: 16.6 us -> 12.9 us  [per_device(): pl.pallas_call(gradient_kernel, out_shape=(shape((padded // 2, hid), F32)...]
    pallas_call x1, Pallas kernels: 3.65 us -> 0.78 us  [per_device(): pl.pallas_call(turn_kernel, out_shape=(across_lanes, side, side), in_spec...]
    pallas_call x2, Pallas kernels: 19.8 us -> 17.4 us  [transport(): pl.pallas_call(functools.partial(transport_kernel, part), out_shape=(fina...]
    ppermute x2, starting transfers between devices: 8.93 us -> 6.66 us  [from_lon_neighbours(): lax.ppermute(first, 'lev', [((i + 1) % levs, i) for i in range(levs)])]
    ppermute x4 -> x3, waiting for transfers between devices: 5.96 us -> 4.61 us  [sum_over_devices(): total = total + lax.ppermute(piece(parts, at ^ m), 'band', perm)]
  transfers between devices with their start and end apart: 23 -> 23, of which waited for: 11 -> 12; matrix products, arithmetic and copies ran while one was open for 1% -> 0% of each run, Pallas kernels for 21% -> 17%
where the time goes in v2:
time: 159 us
  starting transfers between devices  70 us (44%)
  Pallas kernels  54.5 us (34%)
  waiting for transfers between devices  28.4 us (18%)
  local copies, waits for them, and re-layouts  3.59 us (2%)
    ppermute x5, starting transfers between devices, from_near(): lax.ppermute(x, 'band', [(i, i ^ 1) for i in range(lax.axis_size('band'))])  38.3 us
    pallas_call x2, Pallas kernels, transport(): pl.pallas_call(functools.partial(transport_kernel, part), out_shape=(fina...  17.4 us
    pallas_call x1, Pallas kernels, per_device(): pl.pallas_call(forward_kernel, out_shape=(*halos, wide, wide, *kept_shape...  14.1 us
    pallas_call x1, Pallas kernels, per_device(): pl.pallas_call(gradient_kernel, out_shape=(shape((padded // 2, hid), F32)...  12.9 us
    ppermute x3, starting transfers between devices, sum_over_devices(): total = total + lax.ppermute(piece(parts, at ^ m), 'band', perm)  12.1 us
    ppermute x2, waiting for transfers between devices, sum_over_devices(): x = x + lax.ppermute(x, 'lev', [(i, i ^ step) for i in range(lev)])  7.26 us
    pallas_call x1, Pallas kernels, per_device(): pl.pallas_call(adjoint_kernel, out_shape=shape((tiles, LANES * rows, LANE...  7.23 us
    ppermute x2, waiting for transfers between devices, from_lon_neighbours(): west = lax.ppermute(last, 'lev', [(i, (i + 1) % levs) for i in range(levs)])  7.02 us
  transfers between devices with their start and end apart: 23, of which 12 were waited for; matrix products, arithmetic and copies ran while one was open for 0% of the time, Pallas kernels for 17%

profile of v2, /device:TPU:0, one launch (start us, length us, event | category | flops | bytes accessed | tf_op | source)
XLA Modules:
  0.0 158.7 jit_solution(4313238817902530398)
XLA Ops:
  0.6 14.1 %forward.1 = (f32[6,2,264,128]{3,2,1,0:T(8,128)}, f32[6,264,128]{2,1,0:T(8,128)}, f32[6,256,128]{2,1,0:T(8,128)}, f32[8,2,16,128]{3,2,1,0:T(8,128)}, f32[8,2,16,...) custom-call(f32[2048,256]{1,0:T(8,128)} %bitcast.37, ...), custom_call_target="tpu_custom_call" | custom-call | flops 14000000 | bytes 42000000 | tf_op jit(solution)/shard_map/forward/pallas_call | solution.py:704
  14.8 5.1 %collective-permute-start.2 = (f32[8,2,16,128]{3,2,1,0:T(8,128)}, f32[8,2,16,128]{3,2,1,0:T(8,128)S(1)}, u32[]{:S(2)}, u32[]{:S(2)}) collective-permute-start(f32[8,2,16,128]{3,2,1,0:T(8,128)} %get-tuple-element.56), channel_id=1, source_target_pairs={{1,0},{2,1},{3,2},{0,3},{5,4},{6,5},{7,6},{4,7},{9,8},{10,9},{11,1... | collective-permute-start | bytes 393224 | tf_op jit(solution)/shard_map/ppermute | solution.py:622
  19.9 1.6 collective-permute-start.1
  21.4 2.0 %collective-permute-start = (f32[6,2,264,128]{3,2,1,0:T(8,128)}, f32[6,2,264,128]{3,2,1,0:T(8,128)}, u32[]{:S(2)}, u32[]{:S(2)}) collective-permute-start(f32[6,2,264,128]{3,2,1,0:T(8,128)} %get-tuple-element.53.refs_2_), channel_id=1, source_target_pairs={{0,4},{4,0},{8,12},{12,8},{16,20},{20,16},{24,28},{28,24},{1,5},{5... | collective-permute-start | bytes 4866056 | tf_op jit(solution)/shard_map/ppermute | solution.py:628
  23.4 0.2 bitcast_convert_fusion.source_hbm
  23.7 0.8 turn.1
  24.6 2.3 %collective-permute-done.3.refs_5_ = f32[8,2,16,128]{3,2,1,0:T(8,128)S(1)} collective-permute-done((f32[8,2,16,128]{3,2,1,0:T(8,128)}, f32[8,2,16,128]{3,2,1,0:T(8,128)S(1)}, u32[]{:S(2)}, u32[]{:S(2)}) %collective-permute-start.3) | collective-permute-done | bytes 131104 | tf_op jit(solution)/shard_map/ppermute | solution.py:623
  26.8 0.1 broadcast_in_dim.2.refs_11_
  26.9 0.7 collective-permute-start.4
  27.6 2.9 %collective-permute-start.5 = (f32[2,6,2,16,128]{4,3,2,1,0:T(8,128)S(1)}, f32[2,6,2,16,128]{4,3,2,1,0:T(8,128)S(1)}, u32[]{:S(2)}, u32[]{:S(2)}) collective-permute-start(f32[2,6,2,16,128]{4,3,2,1,0:T(8,128)S(1)} %get-tuple-element.110), channel_id=1, source_target_pairs={{0,4},{4,0},{8,12},{12,8},{16,20},{20,16},{24,28},{28,24},{1,5},{5... | collective-permute-start | bytes 589832 | tf_op jit(solution)/shard_map/ppermute | solution.py:628
  30.5 1.6 collective-permute-start.6
  32.1 2.7 %collective-permute-done.6.refs_9_ = f32[8,2,8,128]{3,2,1,0:T(8,128)S(1)} collective-permute-done((f32[8,2,8,128]{3,2,1,0:T(8,128)S(1)}, f32[8,2,8,128]{3,2,1,0:T(8,128)S(1)}, u32[]{:S(2)}, u32[]{:S(2)}) %collective-permute-start.6) | collective-permute-done | bytes 65568 | tf_op jit(solution)/shard_map/ppermute | solution.py:622
  34.8 1.3 collective-permute-start.7
  36.1 4.7 %collective-permute-done.7.refs_10_ = f32[8,2,8,128]{3,2,1,0:T(8,128)S(1)} collective-permute-done((f32[8,2,8,128]{3,2,1,0:T(8,128)S(1)}, f32[8,2,8,128]{3,2,1,0:T(8,128)S(1)}, u32[]{:S(2)}, u32[]{:S(2)}) %collective-permute-start.7) | collective-permute-done | bytes 65568 | tf_op jit(solution)/shard_map/ppermute | solution.py:623
  40.9 0.7 collective-permute-start.8
  41.6 8.8 %transport0.1 = (f32[8,256,128]{2,1,0:T(8,128)S(1)}, f32[6,272,128]{2,1,0:T(8,128)S(1)}, f32[6,272,128]{2,1,0:T(8,128)S(1)}, f32[20,8,128]{2,1,0:T(8,128)S(1)}) custom-call(f32[6,2,264,128]{3,2,1,0:T(8,128)} %collective-permute-done.refs_0_, f32[6,264,128]{2,1,0:T(8,128)} %collective-permute-done.1.refs_1_, f32[6,2,264,128]{3,2,1,0:T(8,128)S(1)} %copy-done, ...), custom_call_target="tpu_custom_call" | custom-call | flops 13000000 | bytes 39000000 | tf_op jit(solution)/shard_map/transport0/pallas_call | solution.py:761
  50.5 0.7 collective-permute-start.9
  51.2 16.4 %collective-permute-start.12 = (f32[6,272,128]{2,1,0:T(8,128)S(1)}, f32[6,272,128]{2,1,0:T(8,128)S(1)}, u32[]{:S(2)}, u32[]{:S(2)}) collective-permute-start(f32[6,272,128]{2,1,0:T(8,128)S(1)} %get-tuple-element.86.own_near), channel_id=1, source_target_pairs={{0,4},{4,0},{8,12},{12,8},{16,20},{20,16},{24,28},{28,24},{1,5},{5... | collective-permute-start | bytes 2506760 | tf_op jit(solution)/shard_map/ppermute | solution.py:628
  67.6 8.5 %transport1.1 = (f32[8,256,128]{2,1,0:T(8,128)S(1)}, f32[6,272,128]{2,1,0:T(8,128)S(1)}, f32[6,272,128]{2,1,0:T(8,128)S(1)}) custom-call(f32[6,2,264,128]{3,2,1,0:T(8,128)} %collective-permute-done.refs_0_, f32[6,256,128]{2,1,0:T(8,128)S(1)} %collective-permute-done.8.refs_1_, f32[6,2,264,128]{3,2,1,0:T(8,128)S(1)} %copy-done, f32[6,256,128]{2,1,0:T(8,128)S(1)} %copy-done.6, ...), custom_call_target="tpu_custom_call" | custom-call | flops 13000000 | bytes 39000000 | tf_op jit(solution)/shard_map/transport1/pallas_call | solution.py:761
  76.2 0.9 collective-permute-start.10
  77.1 10.6 %collective-permute-start.11 = (f32[6,272,128]{2,1,0:T(8,128)S(1)}, f32[6,272,128]{2,1,0:T(8,128)S(1)}, u32[]{:S(2)}, u32[]{:S(2)}) collective-permute-start(f32[6,272,128]{2,1,0:T(8,128)S(1)} %get-tuple-element.84.own_near), channel_id=1, source_target_pairs={{0,4},{4,0},{8,12},{12,8},{16,20},{20,16},{24,28},{28,24},{1,5},{5... | collective-permute-start | bytes 2506760 | tf_op jit(solution)/shard_map/ppermute | solution.py:628
  87.7 2.0 %native.1 = f32[2048,256]{1,0:T(8,128)} custom-call(f32[8,256,128]{2,1,0:T(8,128)S(1)} %get-tuple-element.81.refs_0_, f32[8,256,128]{2,1,0:T(8,128)S(1)} %get-tuple-element.82.refs_1_), custom_call_target="tpu_custom_call" | custom-call | flops 4000000 | bytes 12000000 | tf_op jit(solution)/shard_map/native/pallas_call | solution.py:789
  89.8 7.2 %adjoint0.1.lower_h = f32[2,1024,128]{2,1,0:T(8,128)S(1)} custom-call(f32[6,272,128]{2,1,0:T(8,128)S(1)} %collective-permute-done.12.near, f32[6,272,128]{2,1,0:T(8,128)S(1)} %collective-permute-done.9.far, f32[6,272,128]{2,1,0:T(8,128)S(1)} %get-tuple-element.86.own_near, f32[6,272,128]{2,1,0:T(8,128)S(1)} %get-tuple-element.79.own_far, ...), custom_call_target="tpu_custom_call" | custom-call | flops 12000000 | bytes 36000000 | tf_op jit(solution)/shard_map/adjoint0/pallas_call | solution.py:800
  97.1 1.0 copy-done.1
  98.1 12.9 %gradient.1 = (f32[384,256]{1,0:T(8,128)S(1)}, f32[384,256]{1,0:T(8,128)S(1)}) custom-call(f32[6,272,128]{2,1,0:T(8,128)S(1)} %collective-permute-done.11.near, f32[6,272,128]{2,1,0:T(8,128)S(1)} %collective-permute-done.10.far, f32[6,272,128]{2,1,0:T(8,128)} %copy-done.3, f32[6,272,128]{2,1,0:T(8,128)} %copy-done.4, ...), custom_call_target="tpu_custom_call" | custom-call | flops 17000000 | bytes 51000000 | tf_op jit(solution)/shard_map/gradient/pallas_call | solution.py:815
  111.0 6.3 %collective-permute-start.13 = (f32[384,256]{1,0:T(8,128)S(1)}, f32[384,256]{1,0:T(8,128)S(1)}, u32[]{:S(2)}, u32[]{:S(2)}) collective-permute-start(f32[384,256]{1,0:T(8,128)S(1)} %get-tuple-element.98), channel_id=1, source_target_pairs={{0,4},{4,0},{8,12},{12,8},{16,20},{20,16},{24,28},{28,24},{1,5},{5... | collective-permute-start | bytes 1179656 | tf_op jit(solution)/shard_map/ppermute | solution.py:628
  117.4 1.3 collective-permute-done.13
  118.8 8.7 %collective-permute-start.14 = (f32[96,256]{1,0:T(8,128)S(1)}, f32[96,256]{1,0:T(8,128)S(1)}, u32[]{:S(2)}, u32[]{:S(2)}) collective-permute-start(f32[96,256]{1,0:T(8,128)S(1)} %get-tuple-element.107), channel_id=1, source_target_pairs={{0,24},{4,28},{8,16},{12,20},{16,8},{20,12},{24,0},{28,4},{1,25},{... | collective-permute-start | bytes 294920 | tf_op jit(solution)/shard_map/ppermute | solution.py:596
  127.6 3.4 %collective-permute-start.15 = (f32[96,256]{1,0:T(8,128)S(1)}, f32[96,256]{1,0:T(8,128)S(1)}, u32[]{:S(2)}, u32[]{:S(2)}) collective-permute-start(f32[96,256]{1,0:T(8,128)S(1)} %get-tuple-element.109), channel_id=1, source_target_pairs={{0,16},{4,20},{8,24},{12,28},{16,0},{20,4},{24,8},{28,12},{1,17},{... | collective-permute-start | bytes 294920 | tf_op jit(solution)/shard_map/ppermute | solution.py:596
  130.9 3.0 %collective-permute-done.15 = f32[96,256]{1,0:T(8,128)S(1)} collective-permute-done((f32[96,256]{1,0:T(8,128)S(1)}, f32[96,256]{1,0:T(8,128)S(1)}, u32[]{:S(2)}, u32[]{:S(2)}) %collective-permute-start.15) | collective-permute-done | bytes 98336 | tf_op jit(solution)/shard_map/ppermute | solution.py:596
  134.0 1.6 collective-permute-done.16
  135.6 0.3 collective-permute-start.17
  135.9 4.4 %collective-permute-done.17 = f32[96,256]{1,0:T(8,128)S(1)} collective-permute-done((f32[96,256]{1,0:T(8,128)S(1)}, f32[96,256]{1,0:T(8,128)S(1)}, u32[]{:S(2)}, u32[]{:S(2)}) %collective-permute-start.17) | collective-permute-done | bytes 98336 | tf_op jit(solution)/shard_map/ppermute | solution.py:603
  140.3 2.7 %collective-permute-start.18 = (f32[96,256]{1,0:T(8,128)S(1)}, f32[96,256]{1,0:T(8,128)S(1)}, u32[]{:S(2)}, u32[]{:S(2)}) collective-permute-start(f32[96,256]{1,0:T(8,128)S(1)} %add.71), channel_id=1, source_target_pairs={{0,2},{1,3},{2,0},{3,1},{4,6},{5,7},{6,4},{7,5},{8,10},{9,11},{10,... | collective-permute-start | bytes 294920 | tf_op jit(solution)/shard_map/ppermute | solution.py:603
  143.0 2.9 %collective-permute-done.18 = f32[96,256]{1,0:T(8,128)S(1)} collective-permute-done((f32[96,256]{1,0:T(8,128)S(1)}, f32[96,256]{1,0:T(8,128)S(1)}, u32[]{:S(2)}, u32[]{:S(2)}) %collective-permute-start.18) | collective-permute-done | bytes 98336 | tf_op jit(solution)/shard_map/ppermute | solution.py:603
  145.9 2.1 %collective-permute-start.19 = (f32[96,256]{1,0:T(8,128)S(1)}, f32[96,256]{1,0:T(8,128)S(1)}, u32[]{:S(2)}, u32[]{:S(2)}) collective-permute-start(f32[96,256]{1,0:T(8,128)S(1)} %add.72), channel_id=1, source_target_pairs={{0,24},{4,28},{8,16},{12,20},{16,8},{20,12},{24,0},{28,4},{1,25},{... | collective-permute-start | bytes 294920 | tf_op jit(solution)/shard_map/ppermute | solution.py:607
  148.0 0.6 collective-permute-start.20
  148.6 1.4 collective-permute-start.21
  149.9 2.2 %collective-permute-done.19 = f32[96,256]{1,0:T(8,128)S(1)} collective-permute-done((f32[96,256]{1,0:T(8,128)S(1)}, f32[96,256]{1,0:T(8,128)S(1)}, u32[]{:S(2)}, u32[]{:S(2)}) %collective-permute-start.19) | collective-permute-done | bytes 98336 | tf_op jit(solution)/shard_map/ppermute | solution.py:607
  152.2 0.9 collective-permute-done.20
  153.0 0.6 collective-permute-done.21
  153.7 0.1 collective-permute-start.22
  153.8 1.7 %collective-permute-done.22 = f32[384,256]{1,0:T(8,128)S(1)} collective-permute-done((f32[384,256]{1,0:T(8,128)S(1)}, f32[384,256]{1,0:T(8,128)S(1)}, u32[]{:S(2)}, u32[]{:S(2)}) %collective-permute-start.22) | collective-permute-done | bytes 393248 | tf_op jit(solution)/shard_map/ppermute | solution.py:607
  155.5 0.8 broadcast_select_fusion
  156.3 0.7 slice.21
  157.0 0.6 slice_bitcast_fusion
  157.6 0.6 fusion.4
  158.2 0.5 slice_bitcast_fusion.1
  (43 shorter events, 0.4 us)
Async XLA Ops:
  0.6 22.8 %copy-start.10 = (bf16[64,4,8,256]{3,2,1,0:T(8,128)(2,1)S(1)}, bf16[64,4,8,256]{3,2,1,0:T(8,128)(2,1)}, u32[]{:S(2)}) copy-start(bf16[64,4,8,256]{3,2,1,0:T(8,128)(2,1)} %param.15) | copy-start | bytes 3145732
  14.8 9.8 %collective-permute-start.2 = (f32[8,2,16,128]{3,2,1,0:T(8,128)}, f32[8,2,16,128]{3,2,1,0:T(8,128)S(1)}, u32[]{:S(2)}, u32[]{:S(2)}) collective-permute-start(f32[8,2,16,128]{3,2,1,0:T(8,128)} %get-tuple-element.56), channel_id=1, source_target_pairs={{1,0},{2,1},{3,2},{0,3},{5,4},{6,5},{7,6},{4,7},{9,8},{10,9},{11,1... | collective-permute-start | bytes 393224 | tf_op jit(solution)/shard_map/ppermute | solution.py:622
  19.9 7.0 %collective-permute-start.3 = (f32[8,2,16,128]{3,2,1,0:T(8,128)}, f32[8,2,16,128]{3,2,1,0:T(8,128)S(1)}, u32[]{:S(2)}, u32[]{:S(2)}) collective-permute-start(f32[8,2,16,128]{3,2,1,0:T(8,128)} %get-tuple-element.57), channel_id=1, source_target_pairs={{0,1},{1,2},{2,3},{3,0},{4,5},{5,6},{6,7},{7,4},{8,9},{9,10},{10,1... | collective-permute-start | bytes 393224 | tf_op jit(solution)/shard_map/ppermute | solution.py:623
  19.9 21.0 %collective-permute-start.1 = (f32[6,264,128]{2,1,0:T(8,128)}, f32[6,264,128]{2,1,0:T(8,128)}, u32[]{:S(2)}, u32[]{:S(2)}) collective-permute-start(f32[6,264,128]{2,1,0:T(8,128)} %get-tuple-element.55.refs_3_), channel_id=1, source_target_pairs={{4,8},{12,16},{20,24},{8,4},{16,12},{24,20},{5,9},{13,17},{21,25},... | collective-permute-start | bytes 2433032 | tf_op jit(solution)/shard_map/ppermute | solution.py:634
  21.4 20.2 %collective-permute-start = (f32[6,2,264,128]{3,2,1,0:T(8,128)}, f32[6,2,264,128]{3,2,1,0:T(8,128)}, u32[]{:S(2)}, u32[]{:S(2)}) collective-permute-start(f32[6,2,264,128]{3,2,1,0:T(8,128)} %get-tuple-element.53.refs_2_), channel_id=1, source_target_pairs={{0,4},{4,0},{8,12},{12,8},{16,20},{20,16},{24,28},{28,24},{1,5},{5... | collective-permute-start | bytes 4866056 | tf_op jit(solution)/shard_map/ppermute | solution.py:628
  23.7 17.9 %copy-start.5 = (f32[6,264,128]{2,1,0:T(8,128)S(1)}, f32[6,264,128]{2,1,0:T(8,128)}, u32[]{:S(2)}) copy-start(f32[6,264,128]{2,1,0:T(8,128)} %get-tuple-element.55.refs_3_) | copy-start | bytes 2433028
  23.7 17.9 %copy-start = (f32[6,2,264,128]{3,2,1,0:T(8,128)S(1)}, f32[6,2,264,128]{3,2,1,0:T(8,128)}, u32[]{:S(2)}) copy-start(f32[6,2,264,128]{3,2,1,0:T(8,128)} %get-tuple-element.53.refs_2_) | copy-start | bytes 4866052
  26.9 13.9 %collective-permute-start.4 = (f32[2,6,2,16,128]{4,3,2,1,0:T(8,128)S(1)}, f32[2,6,2,16,128]{4,3,2,1,0:T(8,128)S(1)}, u32[]{:S(2)}, u32[]{:S(2)}) collective-permute-start(f32[2,6,2,16,128]{4,3,2,1,0:T(8,128)S(1)} %get-tuple-element.111), channel_id=1, source_target_pairs={{4,8},{12,16},{20,24},{8,4},{16,12},{24,20},{5,9},{13,17},{21,25},... | collective-permute-start | bytes 589832 | tf_op jit(solution)/shard_map/ppermute | solution.py:634
  27.6 13.2 %collective-permute-start.5 = (f32[2,6,2,16,128]{4,3,2,1,0:T(8,128)S(1)}, f32[2,6,2,16,128]{4,3,2,1,0:T(8,128)S(1)}, u32[]{:S(2)}, u32[]{:S(2)}) collective-permute-start(f32[2,6,2,16,128]{4,3,2,1,0:T(8,128)S(1)} %get-tuple-element.110), channel_id=1, source_target_pairs={{0,4},{4,0},{8,12},{12,8},{16,20},{20,16},{24,28},{28,24},{1,5},{5... | collective-permute-start | bytes 589832 | tf_op jit(solution)/shard_map/ppermute | solution.py:628
  30.5 4.3 %collective-permute-start.6 = (f32[8,2,8,128]{3,2,1,0:T(8,128)S(1)}, f32[8,2,8,128]{3,2,1,0:T(8,128)S(1)}, u32[]{:S(2)}, u32[]{:S(2)}) collective-permute-start(f32[8,2,8,128]{3,2,1,0:T(8,128)S(1)} %get-tuple-element.63), channel_id=1, source_target_pairs={{1,0},{2,1},{3,2},{0,3},{5,4},{6,5},{7,6},{4,7},{9,8},{10,9},{11,1... | collective-permute-start | bytes 196616 | tf_op jit(solution)/shard_map/ppermute | solution.py:622
  34.8 6.1 %collective-permute-start.7 = (f32[8,2,8,128]{3,2,1,0:T(8,128)S(1)}, f32[8,2,8,128]{3,2,1,0:T(8,128)S(1)}, u32[]{:S(2)}, u32[]{:S(2)}) collective-permute-start(f32[8,2,8,128]{3,2,1,0:T(8,128)S(1)} %get-tuple-element.64), channel_id=1, source_target_pairs={{0,1},{1,2},{2,3},{3,0},{4,5},{5,6},{6,7},{7,4},{8,9},{9,10},{10,1... | collective-permute-start | bytes 196616 | tf_op jit(solution)/shard_map/ppermute | solution.py:623
  40.9 9.6 %collective-permute-start.8 = (f32[6,256,128]{2,1,0:T(8,128)}, f32[6,256,128]{2,1,0:T(8,128)S(1)}, u32[]{:S(2)}, u32[]{:S(2)}) collective-permute-start(f32[6,256,128]{2,1,0:T(8,128)} %get-tuple-element.74.refs_3_), channel_id=1, source_target_pairs={{4,8},{12,16},{20,24},{8,4},{16,12},{24,20},{5,9},{13,17},{21,25},... | collective-permute-start | bytes 2359304 | tf_op jit(solution)/shard_map/ppermute | solution.py:634
  41.6 26.0 %copy-start.6 = (f32[6,256,128]{2,1,0:T(8,128)S(1)}, f32[6,256,128]{2,1,0:T(8,128)}, u32[]{:S(2)}) copy-start(f32[6,256,128]{2,1,0:T(8,128)} %get-tuple-element.74.refs_3_) | copy-start | bytes 2359300
  50.5 25.7 %collective-permute-start.9 = (f32[6,272,128]{2,1,0:T(8,128)S(1)}, f32[6,272,128]{2,1,0:T(8,128)S(1)}, u32[]{:S(2)}, u32[]{:S(2)}) collective-permute-start(f32[6,272,128]{2,1,0:T(8,128)S(1)} %get-tuple-element.79.own_far), channel_id=1, source_target_pairs={{4,8},{12,16},{20,24},{8,4},{16,12},{24,20},{5,9},{13,17},{21,25},... | collective-permute-start | bytes 2506760 | tf_op jit(solution)/shard_map/ppermute | solution.py:634
  51.2 38.6 %collective-permute-start.12 = (f32[6,272,128]{2,1,0:T(8,128)S(1)}, f32[6,272,128]{2,1,0:T(8,128)S(1)}, u32[]{:S(2)}, u32[]{:S(2)}) collective-permute-start(f32[6,272,128]{2,1,0:T(8,128)S(1)} %get-tuple-element.86.own_near), channel_id=1, source_target_pairs={{0,4},{4,0},{8,12},{12,8},{16,20},{20,16},{24,28},{28,24},{1,5},{5... | collective-permute-start | bytes 2506760 | tf_op jit(solution)/shard_map/ppermute | solution.py:628
  76.1 13.6 %copy-start.3 = (f32[6,272,128]{2,1,0:T(8,128)}, f32[6,272,128]{2,1,0:T(8,128)S(1)}, u32[]{:S(2)}) copy-start(f32[6,272,128]{2,1,0:T(8,128)S(1)} %get-tuple-element.84.own_near) | copy-start | bytes 2506756
  76.2 13.6 %copy-start.4 = (f32[6,272,128]{2,1,0:T(8,128)}, f32[6,272,128]{2,1,0:T(8,128)S(1)}, u32[]{:S(2)}) copy-start(f32[6,272,128]{2,1,0:T(8,128)S(1)} %get-tuple-element.80.own_far) | copy-start | bytes 2506756
  76.2 21.9 %collective-permute-start.10 = (f32[6,272,128]{2,1,0:T(8,128)S(1)}, f32[6,272,128]{2,1,0:T(8,128)S(1)}, u32[]{:S(2)}, u32[]{:S(2)}) collective-permute-start(f32[6,272,128]{2,1,0:T(8,128)S(1)} %get-tuple-element.80.own_far), channel_id=1, source_target_pairs={{4,8},{12,16},{20,24},{8,4},{16,12},{24,20},{5,9},{13,17},{21,25},... | collective-permute-start | bytes 2506760 | tf_op jit(solution)/shard_map/ppermute | solution.py:634
  77.1 21.0 %collective-permute-start.11 = (f32[6,272,128]{2,1,0:T(8,128)S(1)}, f32[6,272,128]{2,1,0:T(8,128)S(1)}, u32[]{:S(2)}, u32[]{:S(2)}) collective-permute-start(f32[6,272,128]{2,1,0:T(8,128)S(1)} %get-tuple-element.84.own_near), channel_id=1, source_target_pairs={{0,4},{4,0},{8,12},{12,8},{16,20},{20,16},{24,28},{28,24},{1,5},{5... | collective-permute-start | bytes 2506760 | tf_op jit(solution)/shard_map/ppermute | solution.py:628
  89.8 8.3 %copy-start.2 = (f32[64,8,256]{2,1,0:T(8,128)S(1)}, f32[64,8,256]{2,1,0:T(8,128)}, u32[]{:S(2)}) copy-start(f32[64,8,256]{2,1,0:T(8,128)} %param.18) | copy-start | bytes 1572868
  89.8 8.3 %copy-start.7 = (bf16[256,256]{1,0:T(8,128)(2,1)S(1)}, bf16[256,256]{1,0:T(8,128)(2,1)}, u32[]{:S(2)}) copy-start(bf16[256,256]{1,0:T(8,128)(2,1)} %w2.3) | copy-start | bytes 393220
  89.8 8.3 %copy-start.8 = (f32[2,512,128]{2,1,0:T(8,128)S(1)}, f32[2,512,128]{2,1,0:T(8,128)}, u32[]{:S(2)}) copy-start(f32[2,512,128]{2,1,0:T(8,128)} %get-tuple-element.91.rate_h) | copy-start | bytes 1572868
  89.8 8.3 %copy-start.9 = (bf16[256,64]{0,1:T(8,128)(2,1)S(1)}, bf16[256,64]{0,1:T(8,128)(2,1)}, u32[]{:S(2)}) copy-start(bf16[256,64]{0,1:T(8,128)(2,1)} %param.26) | copy-start | bytes 98308
  97.1 1.0 copy-start.1
  111.0 7.7 %collective-permute-start.13 = (f32[384,256]{1,0:T(8,128)S(1)}, f32[384,256]{1,0:T(8,128)S(1)}, u32[]{:S(2)}, u32[]{:S(2)}) collective-permute-start(f32[384,256]{1,0:T(8,128)S(1)} %get-tuple-element.98), channel_id=1, source_target_pairs={{0,4},{4,0},{8,12},{12,8},{16,20},{20,16},{24,28},{28,24},{1,5},{5... | collective-permute-start | bytes 1179656 | tf_op jit(solution)/shard_map/ppermute | solution.py:628
  118.8 12.1 %collective-permute-start.14 = (f32[96,256]{1,0:T(8,128)S(1)}, f32[96,256]{1,0:T(8,128)S(1)}, u32[]{:S(2)}, u32[]{:S(2)}) collective-permute-start(f32[96,256]{1,0:T(8,128)S(1)} %get-tuple-element.107), channel_id=1, source_target_pairs={{0,24},{4,28},{8,16},{12,20},{16,8},{20,12},{24,0},{28,4},{1,25},{... | collective-permute-start | bytes 294920 | tf_op jit(solution)/shard_map/ppermute | solution.py:596
  127.6 6.4 %collective-permute-start.15 = (f32[96,256]{1,0:T(8,128)S(1)}, f32[96,256]{1,0:T(8,128)S(1)}, u32[]{:S(2)}, u32[]{:S(2)}) collective-permute-start(f32[96,256]{1,0:T(8,128)S(1)} %get-tuple-element.109), channel_id=1, source_target_pairs={{0,16},{4,20},{8,24},{12,28},{16,0},{20,4},{24,8},{28,12},{1,17},{... | collective-permute-start | bytes 294920 | tf_op jit(solution)/shard_map/ppermute | solution.py:596
  130.9 4.6 %collective-permute-start.16 = (f32[96,256]{1,0:T(8,128)S(1)}, f32[96,256]{1,0:T(8,128)S(1)}, u32[]{:S(2)}, u32[]{:S(2)}) collective-permute-start(f32[96,256]{1,0:T(8,128)S(1)} %get-tuple-element.108), channel_id=1, source_target_pairs={{0,8},{4,12},{8,0},{12,4},{16,24},{20,28},{24,16},{28,20},{1,9},{5... | collective-permute-start | bytes 294920 | tf_op jit(solution)/shard_map/ppermute | solution.py:596
  135.6 4.7 %collective-permute-start.17 = (f32[96,256]{1,0:T(8,128)S(1)}, f32[96,256]{1,0:T(8,128)S(1)}, u32[]{:S(2)}, u32[]{:S(2)}) collective-permute-start(f32[96,256]{1,0:T(8,128)S(1)} %fusion.3), channel_id=1, source_target_pairs={{0,1},{1,0},{2,3},{3,2},{4,5},{5,4},{6,7},{7,6},{8,9},{9,8},{10,11... | collective-permute-start | bytes 294920 | tf_op jit(solution)/shard_map/ppermute | solution.py:603
  140.3 5.6 %collective-permute-start.18 = (f32[96,256]{1,0:T(8,128)S(1)}, f32[96,256]{1,0:T(8,128)S(1)}, u32[]{:S(2)}, u32[]{:S(2)}) collective-permute-start(f32[96,256]{1,0:T(8,128)S(1)} %add.71), channel_id=1, source_target_pairs={{0,2},{1,3},{2,0},{3,1},{4,6},{5,7},{6,4},{7,5},{8,10},{9,11},{10,... | collective-permute-start | bytes 294920 | tf_op jit(solution)/shard_map/ppermute | solution.py:603
  145.9 6.3 %collective-permute-start.19 = (f32[96,256]{1,0:T(8,128)S(1)}, f32[96,256]{1,0:T(8,128)S(1)}, u32[]{:S(2)}, u32[]{:S(2)}) collective-permute-start(f32[96,256]{1,0:T(8,128)S(1)} %add.72), channel_id=1, source_target_pairs={{0,24},{4,28},{8,16},{12,20},{16,8},{20,12},{24,0},{28,4},{1,25},{... | collective-permute-start | bytes 294920 | tf_op jit(solution)/shard_map/ppermute | solution.py:607
  148.0 5.1 %collective-permute-start.20 = (f32[96,256]{1,0:T(8,128)S(1)}, f32[96,256]{1,0:T(8,128)S(1)}, u32[]{:S(2)}, u32[]{:S(2)}) collective-permute-start(f32[96,256]{1,0:T(8,128)S(1)} %add.72), channel_id=1, source_target_pairs={{0,16},{4,20},{8,24},{12,28},{16,0},{20,4},{24,8},{28,12},{1,17},{... | collective-permute-start | bytes 294920 | tf_op jit(solution)/shard_map/ppermute | solution.py:607
  148.6 5.1 %collective-permute-start.21 = (f32[96,256]{1,0:T(8,128)S(1)}, f32[96,256]{1,0:T(8,128)S(1)}, u32[]{:S(2)}, u32[]{:S(2)}) collective-permute-start(f32[96,256]{1,0:T(8,128)S(1)} %add.72), channel_id=1, source_target_pairs={{0,8},{4,12},{8,0},{12,4},{16,24},{20,28},{24,16},{28,20},{1,9},{5... | collective-permute-start | bytes 294920 | tf_op jit(solution)/shard_map/ppermute | solution.py:607
  153.7 1.8 %collective-permute-start.22 = (f32[384,256]{1,0:T(8,128)S(1)}, f32[384,256]{1,0:T(8,128)S(1)}, u32[]{:S(2)}, u32[]{:S(2)}) collective-permute-start(f32[384,256]{1,0:T(8,128)S(1)} %pad_maximum_fusion), channel_id=1, source_target_pairs={{0,4},{4,0},{8,12},{12,8},{16,20},{20,16},{24,28},{28,24},{1,5},{5... | collective-permute-start | bytes 1179656 | tf_op jit(solution)/shard_map/ppermute | solution.py:607

commit v3 on v2

--- a/solution.py
+++ b/solution.py
@@ -613,8 +613,19 @@
             for m in range(1, radix):
                 chosen = jnp.where((at ^ k) == m, got[m], chosen)
             pieces.append(chosen)
-        x = jnp.concatenate(pieces, 0)
-    return x
+        if step > 1:
+            x = jnp.concatenate(pieces, 0)
+    return pieces
+
+
+def rows_of(pieces, start, stop):
+    out, at = [], 0
+    for x in pieces:
+        low, high = max(start - at, 0), min(stop - at, x.shape[0])
+        if low < high:
+            out.append(x[low:high])
+        at += x.shape[0]
+    return out[0] if len(out) == 1 else jnp.concatenate(out, 0)
 
 
 def from_lon_neighbours(first, last):
@@ -831,12 +842,12 @@
     at = fin + hid + levels
     return (
         final.reshape(levels, bins, rows, width),
-        grads[:fin],
-        grads[at],
-        grads[fin : fin + hid],
-        grads[at + 1],
-        grads[fin + hid : at].T,
-        grads[at + 2, :levels],
+        rows_of(grads, 0, fin),
+        rows_of(grads, at, at + 1)[0],
+        rows_of(grads, fin, fin + hid),
+        rows_of(grads, at + 1, at + 2)[0],
+        rows_of(grads, fin + hid, at).T,
+        rows_of(grads, at + 2, at + 3)[0, :levels],
     )
 
 

time: 159 us -> 159 us (level)
  no operation moved by 1% of the time
where the time goes in v3:
time: 159 us
  starting transfers between devices  70 us (44%)
  Pallas kernels  54.5 us (34%)
  waiting for transfers between devices  28.4 us (18%)
  local copies, waits for them, and re-layouts  3.59 us (2%)
    ppermute x5, starting transfers between devices, from_near(): lax.ppermute(x, 'band', [(i, i ^ 1) for i in range(lax.axis_size('band'))])  38.3 us
    pallas_call x2, Pallas kernels, transport(): pl.pallas_call(functools.partial(transport_kernel, part), out_shape=(fina...  17.4 us
    pallas_call x1, Pallas kernels, per_device(): pl.pallas_call(forward_kernel, out_shape=(*halos, wide, wide, *kept_shape...  14.1 us
    pallas_call x1, Pallas kernels, per_device(): pl.pallas_call(gradient_kernel, out_shape=(shape((padded // 2, hid), F32)...  12.9 us
    ppermute x3, starting transfers between devices, sum_over_devices(): total = total + lax.ppermute(piece(parts, at ^ m), 'band', perm)  12.1 us
    ppermute x2, waiting for transfers between devices, sum_over_devices(): x = x + lax.ppermute(x, 'lev', [(i, i ^ step) for i in range(lev)])  7.26 us
    pallas_call x1, Pallas kernels, per_device(): pl.pallas_call(adjoint_kernel, out_shape=shape((tiles, LANES * rows, LANE...  7.23 us
    ppermute x2, waiting for transfers between devices, from_lon_neighbours(): west = lax.ppermute(last, 'lev', [(i, (i + 1) % levs) for i in range(levs)])  7.02 us
  transfers between devices with their start and end apart: 23, of which 12 were waited for; matrix products, arithmetic and copies ran while one was open for 0% of the time, Pallas kernels for 17%

profile of v3, /device:TPU:0, one launch (start us, length us, event | category | flops | bytes accessed | tf_op | source)
XLA Modules:
  0.0 158.7 jit_solution(4313238817902530398)
XLA Ops:
  0.6 14.1 %forward.1 = (f32[6,2,264,128]{3,2,1,0:T(8,128)}, f32[6,264,128]{2,1,0:T(8,128)}, f32[6,256,128]{2,1,0:T(8,128)}, f32[8,2,16,128]{3,2,1,0:T(8,128)}, f32[8,2,16,...) custom-call(f32[2048,256]{1,0:T(8,128)} %bitcast.37, ...), custom_call_target="tpu_custom_call" | custom-call | flops 14000000 | bytes 42000000 | tf_op jit(solution)/shard_map/forward/pallas_call | solution.py:715
  14.8 5.1 %collective-permute-start.2 = (f32[8,2,16,128]{3,2,1,0:T(8,128)}, f32[8,2,16,128]{3,2,1,0:T(8,128)S(1)}, u32[]{:S(2)}, u32[]{:S(2)}) collective-permute-start(f32[8,2,16,128]{3,2,1,0:T(8,128)} %get-tuple-element.56), channel_id=1, source_target_pairs={{1,0},{2,1},{3,2},{0,3},{5,4},{6,5},{7,6},{4,7},{9,8},{10,9},{11,1... | collective-permute-start | bytes 393224 | tf_op jit(solution)/shard_map/ppermute | solution.py:633
  19.9 1.6 collective-permute-start.1
  21.4 2.0 %collective-permute-start = (f32[6,2,264,128]{3,2,1,0:T(8,128)}, f32[6,2,264,128]{3,2,1,0:T(8,128)}, u32[]{:S(2)}, u32[]{:S(2)}) collective-permute-start(f32[6,2,264,128]{3,2,1,0:T(8,128)} %get-tuple-element.53.refs_2_), channel_id=1, source_target_pairs={{0,4},{4,0},{8,12},{12,8},{16,20},{20,16},{24,28},{28,24},{1,5},{5... | collective-permute-start | bytes 4866056 | tf_op jit(solution)/shard_map/ppermute | solution.py:639
  23.4 0.2 bitcast_convert_fusion.source_hbm
  23.7 0.8 turn.1
  24.6 2.3 %collective-permute-done.3.refs_5_ = f32[8,2,16,128]{3,2,1,0:T(8,128)S(1)} collective-permute-done((f32[8,2,16,128]{3,2,1,0:T(8,128)}, f32[8,2,16,128]{3,2,1,0:T(8,128)S(1)}, u32[]{:S(2)}, u32[]{:S(2)}) %collective-permute-start.3) | collective-permute-done | bytes 131104 | tf_op jit(solution)/shard_map/ppermute | solution.py:634
  26.8 0.1 broadcast_in_dim.2.refs_11_
  26.9 0.7 collective-permute-start.4
  27.6 2.9 %collective-permute-start.5 = (f32[2,6,2,16,128]{4,3,2,1,0:T(8,128)S(1)}, f32[2,6,2,16,128]{4,3,2,1,0:T(8,128)S(1)}, u32[]{:S(2)}, u32[]{:S(2)}) collective-permute-start(f32[2,6,2,16,128]{4,3,2,1,0:T(8,128)S(1)} %get-tuple-element.110), channel_id=1, source_target_pairs={{0,4},{4,0},{8,12},{12,8},{16,20},{20,16},{24,28},{28,24},{1,5},{5... | collective-permute-start | bytes 589832 | tf_op jit(solution)/shard_map/ppermute | solution.py:639
  30.5 1.6 collective-permute-start.6
  32.1 2.7 %collective-permute-done.6.refs_9_ = f32[8,2,8,128]{3,2,1,0:T(8,128)S(1)} collective-permute-done((f32[8,2,8,128]{3,2,1,0:T(8,128)S(1)}, f32[8,2,8,128]{3,2,1,0:T(8,128)S(1)}, u32[]{:S(2)}, u32[]{:S(2)}) %collective-permute-start.6) | collective-permute-done | bytes 65568 | tf_op jit(solution)/shard_map/ppermute | solution.py:633
  34.8 1.3 collective-permute-start.7
  36.1 4.7 %collective-permute-done.7.refs_10_ = f32[8,2,8,128]{3,2,1,0:T(8,128)S(1)} collective-permute-done((f32[8,2,8,128]{3,2,1,0:T(8,128)S(1)}, f32[8,2,8,128]{3,2,1,0:T(8,128)S(1)}, u32[]{:S(2)}, u32[]{:S(2)}) %collective-permute-start.7) | collective-permute-done | bytes 65568 | tf_op jit(solution)/shard_map/ppermute | solution.py:634
  40.9 0.7 collective-permute-start.8
  41.6 8.8 %transport0.1 = (f32[8,256,128]{2,1,0:T(8,128)S(1)}, f32[6,272,128]{2,1,0:T(8,128)S(1)}, f32[6,272,128]{2,1,0:T(8,128)S(1)}, f32[20,8,128]{2,1,0:T(8,128)S(1)}) custom-call(f32[6,2,264,128]{3,2,1,0:T(8,128)} %collective-permute-done.refs_0_, f32[6,264,128]{2,1,0:T(8,128)} %collective-permute-done.1.refs_1_, f32[6,2,264,128]{3,2,1,0:T(8,128)S(1)} %copy-done, ...), custom_call_target="tpu_custom_call" | custom-call | flops 13000000 | bytes 39000000 | tf_op jit(solution)/shard_map/transport0/pallas_call | solution.py:772
  50.5 0.7 collective-permute-start.9
  51.2 16.4 %collective-permute-start.12 = (f32[6,272,128]{2,1,0:T(8,128)S(1)}, f32[6,272,128]{2,1,0:T(8,128)S(1)}, u32[]{:S(2)}, u32[]{:S(2)}) collective-permute-start(f32[6,272,128]{2,1,0:T(8,128)S(1)} %get-tuple-element.86.own_near), channel_id=1, source_target_pairs={{0,4},{4,0},{8,12},{12,8},{16,20},{20,16},{24,28},{28,24},{1,5},{5... | collective-permute-start | bytes 2506760 | tf_op jit(solution)/shard_map/ppermute | solution.py:639
  67.6 8.5 %transport1.1 = (f32[8,256,128]{2,1,0:T(8,128)S(1)}, f32[6,272,128]{2,1,0:T(8,128)S(1)}, f32[6,272,128]{2,1,0:T(8,128)S(1)}) custom-call(f32[6,2,264,128]{3,2,1,0:T(8,128)} %collective-permute-done.refs_0_, f32[6,256,128]{2,1,0:T(8,128)S(1)} %collective-permute-done.8.refs_1_, f32[6,2,264,128]{3,2,1,0:T(8,128)S(1)} %copy-done, f32[6,256,128]{2,1,0:T(8,128)S(1)} %copy-done.6, ...), custom_call_target="tpu_custom_call" | custom-call | flops 13000000 | bytes 39000000 | tf_op jit(solution)/shard_map/transport1/pallas_call | solution.py:772
  76.2 0.9 collective-permute-start.10
  77.1 10.6 %collective-permute-start.11 = (f32[6,272,128]{2,1,0:T(8,128)S(1)}, f32[6,272,128]{2,1,0:T(8,128)S(1)}, u32[]{:S(2)}, u32[]{:S(2)}) collective-permute-start(f32[6,272,128]{2,1,0:T(8,128)S(1)} %get-tuple-element.84.own_near), channel_id=1, source_target_pairs={{0,4},{4,0},{8,12},{12,8},{16,20},{20,16},{24,28},{28,24},{1,5},{5... | collective-permute-start | bytes 2506760 | tf_op jit(solution)/shard_map/ppermute | solution.py:639
  87.7 2.0 %native.1 = f32[2048,256]{1,0:T(8,128)} custom-call(f32[8,256,128]{2,1,0:T(8,128)S(1)} %get-tuple-element.81.refs_0_, f32[8,256,128]{2,1,0:T(8,128)S(1)} %get-tuple-element.82.refs_1_), custom_call_target="tpu_custom_call" | custom-call | flops 4000000 | bytes 12000000 | tf_op jit(solution)/shard_map/native/pallas_call | solution.py:800
  89.8 7.2 %adjoint0.1.lower_h = f32[2,1024,128]{2,1,0:T(8,128)S(1)} custom-call(f32[6,272,128]{2,1,0:T(8,128)S(1)} %collective-permute-done.12.near, f32[6,272,128]{2,1,0:T(8,128)S(1)} %collective-permute-done.9.far, f32[6,272,128]{2,1,0:T(8,128)S(1)} %get-tuple-element.86.own_near, f32[6,272,128]{2,1,0:T(8,128)S(1)} %get-tuple-element.79.own_far, ...), custom_call_target="tpu_custom_call" | custom-call | flops 12000000 | bytes 36000000 | tf_op jit(solution)/shard_map/adjoint0/pallas_call | solution.py:811
  97.1 1.0 copy-done.1
  98.1 12.9 %gradient.1 = (f32[384,256]{1,0:T(8,128)S(1)}, f32[384,256]{1,0:T(8,128)S(1)}) custom-call(f32[6,272,128]{2,1,0:T(8,128)S(1)} %collective-permute-done.11.near, f32[6,272,128]{2,1,0:T(8,128)S(1)} %collective-permute-done.10.far, f32[6,272,128]{2,1,0:T(8,128)} %copy-done.3, f32[6,272,128]{2,1,0:T(8,128)} %copy-done.4, ...), custom_call_target="tpu_custom_call" | custom-call | flops 17000000 | bytes 51000000 | tf_op jit(solution)/shard_map/gradient/pallas_call | solution.py:826
  111.0 6.3 %collective-permute-start.13 = (f32[384,256]{1,0:T(8,128)S(1)}, f32[384,256]{1,0:T(8,128)S(1)}, u32[]{:S(2)}, u32[]{:S(2)}) collective-permute-start(f32[384,256]{1,0:T(8,128)S(1)} %get-tuple-element.98), channel_id=1, source_target_pairs={{0,4},{4,0},{8,12},{12,8},{16,20},{20,16},{24,28},{28,24},{1,5},{5... | collective-permute-start | bytes 1179656 | tf_op jit(solution)/shard_map/ppermute | solution.py:639
  117.4 1.3 collective-permute-done.13
  118.8 8.7 %collective-permute-start.14 = (f32[96,256]{1,0:T(8,128)S(1)}, f32[96,256]{1,0:T(8,128)S(1)}, u32[]{:S(2)}, u32[]{:S(2)}) collective-permute-start(f32[96,256]{1,0:T(8,128)S(1)} %get-tuple-element.107), channel_id=1, source_target_pairs={{0,24},{4,28},{8,16},{12,20},{16,8},{20,12},{24,0},{28,4},{1,25},{... | collective-permute-start | bytes 294920 | tf_op jit(solution)/shard_map/ppermute | solution.py:596
  127.6 3.4 %collective-permute-start.15 = (f32[96,256]{1,0:T(8,128)S(1)}, f32[96,256]{1,0:T(8,128)S(1)}, u32[]{:S(2)}, u32[]{:S(2)}) collective-permute-start(f32[96,256]{1,0:T(8,128)S(1)} %get-tuple-element.109), channel_id=1, source_target_pairs={{0,16},{4,20},{8,24},{12,28},{16,0},{20,4},{24,8},{28,12},{1,17},{... | collective-permute-start | bytes 294920 | tf_op jit(solution)/shard_map/ppermute | solution.py:596
  130.9 3.0 %collective-permute-done.15 = f32[96,256]{1,0:T(8,128)S(1)} collective-permute-done((f32[96,256]{1,0:T(8,128)S(1)}, f32[96,256]{1,0:T(8,128)S(1)}, u32[]{:S(2)}, u32[]{:S(2)}) %collective-permute-start.15) | collective-permute-done | bytes 98336 | tf_op jit(solution)/shard_map/ppermute | solution.py:596
  134.0 1.6 collective-permute-done.16
  135.6 0.3 collective-permute-start.17
  135.9 4.4 %collective-permute-done.17 = f32[96,256]{1,0:T(8,128)S(1)} collective-permute-done((f32[96,256]{1,0:T(8,128)S(1)}, f32[96,256]{1,0:T(8,128)S(1)}, u32[]{:S(2)}, u32[]{:S(2)}) %collective-permute-start.17) | collective-permute-done | bytes 98336 | tf_op jit(solution)/shard_map/ppermute | solution.py:603
  140.3 2.7 %collective-permute-start.18 = (f32[96,256]{1,0:T(8,128)S(1)}, f32[96,256]{1,0:T(8,128)S(1)}, u32[]{:S(2)}, u32[]{:S(2)}) collective-permute-start(f32[96,256]{1,0:T(8,128)S(1)} %add.71), channel_id=1, source_target_pairs={{0,2},{1,3},{2,0},{3,1},{4,6},{5,7},{6,4},{7,5},{8,10},{9,11},{10,... | collective-permute-start | bytes 294920 | tf_op jit(solution)/shard_map/ppermute | solution.py:603
  143.0 2.9 %collective-permute-done.18 = f32[96,256]{1,0:T(8,128)S(1)} collective-permute-done((f32[96,256]{1,0:T(8,128)S(1)}, f32[96,256]{1,0:T(8,128)S(1)}, u32[]{:S(2)}, u32[]{:S(2)}) %collective-permute-start.18) | collective-permute-done | bytes 98336 | tf_op jit(solution)/shard_map/ppermute | solution.py:603
  145.9 2.1 %collective-permute-start.19 = (f32[96,256]{1,0:T(8,128)S(1)}, f32[96,256]{1,0:T(8,128)S(1)}, u32[]{:S(2)}, u32[]{:S(2)}) collective-permute-start(f32[96,256]{1,0:T(8,128)S(1)} %add.72), channel_id=1, source_target_pairs={{0,24},{4,28},{8,16},{12,20},{16,8},{20,12},{24,0},{28,4},{1,25},{... | collective-permute-start | bytes 294920 | tf_op jit(solution)/shard_map/ppermute | solution.py:607
  148.0 0.6 collective-permute-start.20
  148.6 1.4 collective-permute-start.21
  149.9 2.2 %collective-permute-done.19 = f32[96,256]{1,0:T(8,128)S(1)} collective-permute-done((f32[96,256]{1,0:T(8,128)S(1)}, f32[96,256]{1,0:T(8,128)S(1)}, u32[]{:S(2)}, u32[]{:S(2)}) %collective-permute-start.19) | collective-permute-done | bytes 98336 | tf_op jit(solution)/shard_map/ppermute | solution.py:607
  152.2 0.9 collective-permute-done.20
  153.0 0.6 collective-permute-done.21
  153.7 0.1 collective-permute-start.22
  153.8 1.7 %collective-permute-done.22 = f32[384,256]{1,0:T(8,128)S(1)} collective-permute-done((f32[384,256]{1,0:T(8,128)S(1)}, f32[384,256]{1,0:T(8,128)S(1)}, u32[]{:S(2)}, u32[]{:S(2)}) %collective-permute-start.22) | collective-permute-done | bytes 393248 | tf_op jit(solution)/shard_map/ppermute | solution.py:607
  155.5 0.8 broadcast_select_fusion
  156.3 0.7 slice.23
  157.0 0.6 slice_bitcast_fusion
  157.6 0.6 fusion.4
  158.2 0.5 slice_bitcast_fusion.1
  (43 shorter events, 0.4 us)
Async XLA Ops:
  0.6 22.8 %copy-start.10 = (bf16[64,4,8,256]{3,2,1,0:T(8,128)(2,1)S(1)}, bf16[64,4,8,256]{3,2,1,0:T(8,128)(2,1)}, u32[]{:S(2)}) copy-start(bf16[64,4,8,256]{3,2,1,0:T(8,128)(2,1)} %param.15) | copy-start | bytes 3145732
  14.8 9.8 %collective-permute-start.2 = (f32[8,2,16,128]{3,2,1,0:T(8,128)}, f32[8,2,16,128]{3,2,1,0:T(8,128)S(1)}, u32[]{:S(2)}, u32[]{:S(2)}) collective-permute-start(f32[8,2,16,128]{3,2,1,0:T(8,128)} %get-tuple-element.56), channel_id=1, source_target_pairs={{1,0},{2,1},{3,2},{0,3},{5,4},{6,5},{7,6},{4,7},{9,8},{10,9},{11,1... | collective-permute-start | bytes 393224 | tf_op jit(solution)/shard_map/ppermute | solution.py:633
  19.9 7.0 %collective-permute-start.3 = (f32[8,2,16,128]{3,2,1,0:T(8,128)}, f32[8,2,16,128]{3,2,1,0:T(8,128)S(1)}, u32[]{:S(2)}, u32[]{:S(2)}) collective-permute-start(f32[8,2,16,128]{3,2,1,0:T(8,128)} %get-tuple-element.57), channel_id=1, source_target_pairs={{0,1},{1,2},{2,3},{3,0},{4,5},{5,6},{6,7},{7,4},{8,9},{9,10},{10,1... | collective-permute-start | bytes 393224 | tf_op jit(solution)/shard_map/ppermute | solution.py:634
  19.9 21.0 %collective-permute-start.1 = (f32[6,264,128]{2,1,0:T(8,128)}, f32[6,264,128]{2,1,0:T(8,128)}, u32[]{:S(2)}, u32[]{:S(2)}) collective-permute-start(f32[6,264,128]{2,1,0:T(8,128)} %get-tuple-element.55.refs_3_), channel_id=1, source_target_pairs={{4,8},{12,16},{20,24},{8,4},{16,12},{24,20},{5,9},{13,17},{21,25},... | collective-permute-start | bytes 2433032 | tf_op jit(solution)/shard_map/ppermute | solution.py:645
  21.4 20.2 %collective-permute-start = (f32[6,2,264,128]{3,2,1,0:T(8,128)}, f32[6,2,264,128]{3,2,1,0:T(8,128)}, u32[]{:S(2)}, u32[]{:S(2)}) collective-permute-start(f32[6,2,264,128]{3,2,1,0:T(8,128)} %get-tuple-element.53.refs_2_), channel_id=1, source_target_pairs={{0,4},{4,0},{8,12},{12,8},{16,20},{20,16},{24,28},{28,24},{1,5},{5... | collective-permute-start | bytes 4866056 | tf_op jit(solution)/shard_map/ppermute | solution.py:639
  23.7 17.9 %copy-start.5 = (f32[6,264,128]{2,1,0:T(8,128)S(1)}, f32[6,264,128]{2,1,0:T(8,128)}, u32[]{:S(2)}) copy-start(f32[6,264,128]{2,1,0:T(8,128)} %get-tuple-element.55.refs_3_) | copy-start | bytes 2433028
  23.7 17.9 %copy-start = (f32[6,2,264,128]{3,2,1,0:T(8,128)S(1)}, f32[6,2,264,128]{3,2,1,0:T(8,128)}, u32[]{:S(2)}) copy-start(f32[6,2,264,128]{3,2,1,0:T(8,128)} %get-tuple-element.53.refs_2_) | copy-start | bytes 4866052
  26.9 13.9 %collective-permute-start.4 = (f32[2,6,2,16,128]{4,3,2,1,0:T(8,128)S(1)}, f32[2,6,2,16,128]{4,3,2,1,0:T(8,128)S(1)}, u32[]{:S(2)}, u32[]{:S(2)}) collective-permute-start(f32[2,6,2,16,128]{4,3,2,1,0:T(8,128)S(1)} %get-tuple-element.111), channel_id=1, source_target_pairs={{4,8},{12,16},{20,24},{8,4},{16,12},{24,20},{5,9},{13,17},{21,25},... | collective-permute-start | bytes 589832 | tf_op jit(solution)/shard_map/ppermute | solution.py:645
  27.6 13.2 %collective-permute-start.5 = (f32[2,6,2,16,128]{4,3,2,1,0:T(8,128)S(1)}, f32[2,6,2,16,128]{4,3,2,1,0:T(8,128)S(1)}, u32[]{:S(2)}, u32[]{:S(2)}) collective-permute-start(f32[2,6,2,16,128]{4,3,2,1,0:T(8,128)S(1)} %get-tuple-element.110), channel_id=1, source_target_pairs={{0,4},{4,0},{8,12},{12,8},{16,20},{20,16},{24,28},{28,24},{1,5},{5... | collective-permute-start | bytes 589832 | tf_op jit(solution)/shard_map/ppermute | solution.py:639
  30.5 4.3 %collective-permute-start.6 = (f32[8,2,8,128]{3,2,1,0:T(8,128)S(1)}, f32[8,2,8,128]{3,2,1,0:T(8,128)S(1)}, u32[]{:S(2)}, u32[]{:S(2)}) collective-permute-start(f32[8,2,8,128]{3,2,1,0:T(8,128)S(1)} %get-tuple-element.63), channel_id=1, source_target_pairs={{1,0},{2,1},{3,2},{0,3},{5,4},{6,5},{7,6},{4,7},{9,8},{10,9},{11,1... | collective-permute-start | bytes 196616 | tf_op jit(solution)/shard_map/ppermute | solution.py:633
  34.8 6.1 %collective-permute-start.7 = (f32[8,2,8,128]{3,2,1,0:T(8,128)S(1)}, f32[8,2,8,128]{3,2,1,0:T(8,128)S(1)}, u32[]{:S(2)}, u32[]{:S(2)}) collective-permute-start(f32[8,2,8,128]{3,2,1,0:T(8,128)S(1)} %get-tuple-element.64), channel_id=1, source_target_pairs={{0,1},{1,2},{2,3},{3,0},{4,5},{5,6},{6,7},{7,4},{8,9},{9,10},{10,1... | collective-permute-start | bytes 196616 | tf_op jit(solution)/shard_map/ppermute | solution.py:634
  40.9 9.6 %collective-permute-start.8 = (f32[6,256,128]{2,1,0:T(8,128)}, f32[6,256,128]{2,1,0:T(8,128)S(1)}, u32[]{:S(2)}, u32[]{:S(2)}) collective-permute-start(f32[6,256,128]{2,1,0:T(8,128)} %get-tuple-element.74.refs_3_), channel_id=1, source_target_pairs={{4,8},{12,16},{20,24},{8,4},{16,12},{24,20},{5,9},{13,17},{21,25},... | collective-permute-start | bytes 2359304 | tf_op jit(solution)/shard_map/ppermute | solution.py:645
  41.6 26.0 %copy-start.6 = (f32[6,256,128]{2,1,0:T(8,128)S(1)}, f32[6,256,128]{2,1,0:T(8,128)}, u32[]{:S(2)}) copy-start(f32[6,256,128]{2,1,0:T(8,128)} %get-tuple-element.74.refs_3_) | copy-start | bytes 2359300
  50.5 25.7 %collective-permute-start.9 = (f32[6,272,128]{2,1,0:T(8,128)S(1)}, f32[6,272,128]{2,1,0:T(8,128)S(1)}, u32[]{:S(2)}, u32[]{:S(2)}) collective-permute-start(f32[6,272,128]{2,1,0:T(8,128)S(1)} %get-tuple-element.79.own_far), channel_id=1, source_target_pairs={{4,8},{12,16},{20,24},{8,4},{16,12},{24,20},{5,9},{13,17},{21,25},... | collective-permute-start | bytes 2506760 | tf_op jit(solution)/shard_map/ppermute | solution.py:645
  51.2 38.6 %collective-permute-start.12 = (f32[6,272,128]{2,1,0:T(8,128)S(1)}, f32[6,272,128]{2,1,0:T(8,128)S(1)}, u32[]{:S(2)}, u32[]{:S(2)}) collective-permute-start(f32[6,272,128]{2,1,0:T(8,128)S(1)} %get-tuple-element.86.own_near), channel_id=1, source_target_pairs={{0,4},{4,0},{8,12},{12,8},{16,20},{20,16},{24,28},{28,24},{1,5},{5... | collective-permute-start | bytes 2506760 | tf_op jit(solution)/shard_map/ppermute | solution.py:639
  76.1 13.6 %copy-start.3 = (f32[6,272,128]{2,1,0:T(8,128)}, f32[6,272,128]{2,1,0:T(8,128)S(1)}, u32[]{:S(2)}) copy-start(f32[6,272,128]{2,1,0:T(8,128)S(1)} %get-tuple-element.84.own_near) | copy-start | bytes 2506756
  76.2 13.6 %copy-start.4 = (f32[6,272,128]{2,1,0:T(8,128)}, f32[6,272,128]{2,1,0:T(8,128)S(1)}, u32[]{:S(2)}) copy-start(f32[6,272,128]{2,1,0:T(8,128)S(1)} %get-tuple-element.80.own_far) | copy-start | bytes 2506756
  76.2 21.9 %collective-permute-start.10 = (f32[6,272,128]{2,1,0:T(8,128)S(1)}, f32[6,272,128]{2,1,0:T(8,128)S(1)}, u32[]{:S(2)}, u32[]{:S(2)}) collective-permute-start(f32[6,272,128]{2,1,0:T(8,128)S(1)} %get-tuple-element.80.own_far), channel_id=1, source_target_pairs={{4,8},{12,16},{20,24},{8,4},{16,12},{24,20},{5,9},{13,17},{21,25},... | collective-permute-start | bytes 2506760 | tf_op jit(solution)/shard_map/ppermute | solution.py:645
  77.1 21.0 %collective-permute-start.11 = (f32[6,272,128]{2,1,0:T(8,128)S(1)}, f32[6,272,128]{2,1,0:T(8,128)S(1)}, u32[]{:S(2)}, u32[]{:S(2)}) collective-permute-start(f32[6,272,128]{2,1,0:T(8,128)S(1)} %get-tuple-element.84.own_near), channel_id=1, source_target_pairs={{0,4},{4,0},{8,12},{12,8},{16,20},{20,16},{24,28},{28,24},{1,5},{5... | collective-permute-start | bytes 2506760 | tf_op jit(solution)/shard_map/ppermute | solution.py:639
  89.8 8.3 %copy-start.2 = (f32[64,8,256]{2,1,0:T(8,128)S(1)}, f32[64,8,256]{2,1,0:T(8,128)}, u32[]{:S(2)}) copy-start(f32[64,8,256]{2,1,0:T(8,128)} %param.18) | copy-start | bytes 1572868
  89.8 8.3 %copy-start.7 = (bf16[256,256]{1,0:T(8,128)(2,1)S(1)}, bf16[256,256]{1,0:T(8,128)(2,1)}, u32[]{:S(2)}) copy-start(bf16[256,256]{1,0:T(8,128)(2,1)} %w2.3) | copy-start | bytes 393220
  89.8 8.3 %copy-start.8 = (f32[2,512,128]{2,1,0:T(8,128)S(1)}, f32[2,512,128]{2,1,0:T(8,128)}, u32[]{:S(2)}) copy-start(f32[2,512,128]{2,1,0:T(8,128)} %get-tuple-element.91.rate_h) | copy-start | bytes 1572868
  89.8 8.3 %copy-start.9 = (bf16[256,64]{0,1:T(8,128)(2,1)S(1)}, bf16[256,64]{0,1:T(8,128)(2,1)}, u32[]{:S(2)}) copy-start(bf16[256,64]{0,1:T(8,128)(2,1)} %param.26) | copy-start | bytes 98308
  97.1 1.0 copy-start.1
  111.0 7.7 %collective-permute-start.13 = (f32[384,256]{1,0:T(8,128)S(1)}, f32[384,256]{1,0:T(8,128)S(1)}, u32[]{:S(2)}, u32[]{:S(2)}) collective-permute-start(f32[384,256]{1,0:T(8,128)S(1)} %get-tuple-element.98), channel_id=1, source_target_pairs={{0,4},{4,0},{8,12},{12,8},{16,20},{20,16},{24,28},{28,24},{1,5},{5... | collective-permute-start | bytes 1179656 | tf_op jit(solution)/shard_map/ppermute | solution.py:639
  118.8 12.1 %collective-permute-start.14 = (f32[96,256]{1,0:T(8,128)S(1)}, f32[96,256]{1,0:T(8,128)S(1)}, u32[]{:S(2)}, u32[]{:S(2)}) collective-permute-start(f32[96,256]{1,0:T(8,128)S(1)} %get-tuple-element.107), channel_id=1, source_target_pairs={{0,24},{4,28},{8,16},{12,20},{16,8},{20,12},{24,0},{28,4},{1,25},{... | collective-permute-start | bytes 294920 | tf_op jit(solution)/shard_map/ppermute | solution.py:596
  127.6 6.4 %collective-permute-start.15 = (f32[96,256]{1,0:T(8,128)S(1)}, f32[96,256]{1,0:T(8,128)S(1)}, u32[]{:S(2)}, u32[]{:S(2)}) collective-permute-start(f32[96,256]{1,0:T(8,128)S(1)} %get-tuple-element.109), channel_id=1, source_target_pairs={{0,16},{4,20},{8,24},{12,28},{16,0},{20,4},{24,8},{28,12},{1,17},{... | collective-permute-start | bytes 294920 | tf_op jit(solution)/shard_map/ppermute | solution.py:596
  130.9 4.6 %collective-permute-start.16 = (f32[96,256]{1,0:T(8,128)S(1)}, f32[96,256]{1,0:T(8,128)S(1)}, u32[]{:S(2)}, u32[]{:S(2)}) collective-permute-start(f32[96,256]{1,0:T(8,128)S(1)} %get-tuple-element.108), channel_id=1, source_target_pairs={{0,8},{4,12},{8,0},{12,4},{16,24},{20,28},{24,16},{28,20},{1,9},{5... | collective-permute-start | bytes 294920 | tf_op jit(solution)/shard_map/ppermute | solution.py:596
  135.6 4.7 %collective-permute-start.17 = (f32[96,256]{1,0:T(8,128)S(1)}, f32[96,256]{1,0:T(8,128)S(1)}, u32[]{:S(2)}, u32[]{:S(2)}) collective-permute-start(f32[96,256]{1,0:T(8,128)S(1)} %fusion.3), channel_id=1, source_target_pairs={{0,1},{1,0},{2,3},{3,2},{4,5},{5,4},{6,7},{7,6},{8,9},{9,8},{10,11... | collective-permute-start | bytes 294920 | tf_op jit(solution)/shard_map/ppermute | solution.py:603
  140.3 5.6 %collective-permute-start.18 = (f32[96,256]{1,0:T(8,128)S(1)}, f32[96,256]{1,0:T(8,128)S(1)}, u32[]{:S(2)}, u32[]{:S(2)}) collective-permute-start(f32[96,256]{1,0:T(8,128)S(1)} %add.71), channel_id=1, source_target_pairs={{0,2},{1,3},{2,0},{3,1},{4,6},{5,7},{6,4},{7,5},{8,10},{9,11},{10,... | collective-permute-start | bytes 294920 | tf_op jit(solution)/shard_map/ppermute | solution.py:603
  145.9 6.3 %collective-permute-start.19 = (f32[96,256]{1,0:T(8,128)S(1)}, f32[96,256]{1,0:T(8,128)S(1)}, u32[]{:S(2)}, u32[]{:S(2)}) collective-permute-start(f32[96,256]{1,0:T(8,128)S(1)} %add.72), channel_id=1, source_target_pairs={{0,24},{4,28},{8,16},{12,20},{16,8},{20,12},{24,0},{28,4},{1,25},{... | collective-permute-start | bytes 294920 | tf_op jit(solution)/shard_map/ppermute | solution.py:607
  148.0 5.1 %collective-permute-start.20 = (f32[96,256]{1,0:T(8,128)S(1)}, f32[96,256]{1,0:T(8,128)S(1)}, u32[]{:S(2)}, u32[]{:S(2)}) collective-permute-start(f32[96,256]{1,0:T(8,128)S(1)} %add.72), channel_id=1, source_target_pairs={{0,16},{4,20},{8,24},{12,28},{16,0},{20,4},{24,8},{28,12},{1,17},{... | collective-permute-start | bytes 294920 | tf_op jit(solution)/shard_map/ppermute | solution.py:607
  148.6 5.1 %collective-permute-start.21 = (f32[96,256]{1,0:T(8,128)S(1)}, f32[96,256]{1,0:T(8,128)S(1)}, u32[]{:S(2)}, u32[]{:S(2)}) collective-permute-start(f32[96,256]{1,0:T(8,128)S(1)} %add.72), channel_id=1, source_target_pairs={{0,8},{4,12},{8,0},{12,4},{16,24},{20,28},{24,16},{28,20},{1,9},{5... | collective-permute-start | bytes 294920 | tf_op jit(solution)/shard_map/ppermute | solution.py:607
  153.7 1.8 %collective-permute-start.22 = (f32[384,256]{1,0:T(8,128)S(1)}, f32[384,256]{1,0:T(8,128)S(1)}, u32[]{:S(2)}, u32[]{:S(2)}) collective-permute-start(f32[384,256]{1,0:T(8,128)S(1)} %pad_maximum_fusion), channel_id=1, source_target_pairs={{0,4},{4,0},{8,12},{12,8},{16,20},{20,16},{24,28},{28,24},{1,5},{5... | collective-permute-start | bytes 1179656 | tf_op jit(solution)/shard_map/ppermute | solution.py:607
